TPU v7x, 512 devices: a whole 4x8x8 slice. The times are simulated.
512 devices in a mesh: rep: 4 (over x), grp: 8 (over y), exp: 16 (over z, core).
Axes of the slice: x: 4, y: 8, z: 8, core: 2. Of those that a mesh axis runs over, the one named last changes fastest.
Arguments:
- tokens: bfloat16 [16384, 2048], P(('rep', 'grp', 'exp')), may hold values from -6 to 6
- out_grad: bfloat16 [16384, 2048], P(('rep', 'grp', 'exp')), may hold values from -6 to 6
- gate_prob: float32 [16384, 8], P(('rep', 'grp', 'exp')), may hold values from 0.05 to 0.5
- routes: int32 [16384, 8], P(('rep', 'grp', 'exp')), may hold values from 0 to 127, as said below
- limits: int32 [128], replicated, may hold values from 2 to 3, as said below
- w_gate: bfloat16 [128, 2048, 768], P(('grp', 'exp'), 'rep'), may hold values from -0.125 to 0.125
- w_up: bfloat16 [128, 2048, 768], P(('grp', 'exp'), 'rep'), may hold values from -0.125 to 0.125
- w_down: bfloat16 [128, 768, 2048], P(('grp', 'exp'), None, 'rep'), may hold values from -0.21875 to 0.21875
- up_in: bfloat16 [128, 32, 2048], P(('grp', 'exp')), may hold values from -0.125 to 0.125
- up_out: bfloat16 [128, 32, 768], P(('grp', 'exp')), may hold values from -0.25 to 0.25
- down_in: bfloat16 [128, 32, 768], P(('grp', 'exp')), may hold values from -0.21875 to 0.21875
- down_out: bfloat16 [128, 32, 2048], P(('grp', 'exp')), may hold values from -0.25 to 0.25
Outputs:
- token_grad: bfloat16 [16384, 2048], P(('rep', 'grp', 'exp'))
- up_in_grad: float32 [128, 32, 2048], P(('grp', 'exp'))
- up_out_grad: float32 [128, 32, 768], P(('grp', 'exp'))
- down_in_grad: float32 [128, 32, 768], P(('grp', 'exp'))
- down_out_grad: float32 [128, 32, 2048], P(('grp', 'exp'))
Inputs may be any that keep to these rules, and one draw needn't show every extreme that they name: `routes`: each row names 8 different experts, all in at most 4 groups of 16 consecutive experts. The first 3 tokens of every source block name one common expert, whose limit is 3. `limits`: at least one expert has the limit 3.
All inputs are finite; a program needn't handle non-finite values.
Results may differ from a plain program's by a relative error of at most 0.014.
Values may be sent and summed in bfloat16 or wider, within the bound.
No kernel may reach another device: no remote copies, remote signals or barrier semaphores. Data moves between devices by JAX's collectives and lax.ppermute only.
A program may use at most 64 MiB of HBM per device.

v0:
```python
import jax
import jax.numpy as jnp
from jax import lax
from jax.sharding import PartitionSpec as P

CAP = 3


ADAPTER_SCALE = 2.0


def gated_product(left_side, right_side, left_dim, right_dim):
    return lax.dot_general(
        left_side,
        right_side,
        (((left_dim,), (right_dim,)), ((), ())),
        preferred_element_type=jnp.float32,
    )


def expert_backward_pass(
    input_rows,
    row_gradient,
    gate_weight,
    up_weight,
    down_weight,
    adapter_up_input,
    adapter_up_output,
    adapter_down_input,
    adapter_down_output,
):
    low_rank_up = gated_product(input_rows, adapter_up_input, 1, 1).astype(jnp.bfloat16)
    gate_pre = gated_product(input_rows, gate_weight, 1, 0)
    up_total_sum = gated_product(input_rows, up_weight, 1, 0) + ADAPTER_SCALE * gated_product(
        low_rank_up, adapter_up_output, 1, 0
    )
    sigmoid_gate = jax.nn.sigmoid(gate_pre)
    active = gate_pre * sigmoid_gate
    hidden_state = (active * up_total_sum).astype(jnp.bfloat16)
    low_rank_down = gated_product(hidden_state, adapter_down_input, 1, 1).astype(jnp.bfloat16)
    down_output_gradient = ADAPTER_SCALE * gated_product(low_rank_down, row_gradient, 0, 0)
    backward_low_rank = gated_product(row_gradient, adapter_down_output, 1, 1).astype(jnp.bfloat16)
    down_input_gradient = ADAPTER_SCALE * gated_product(backward_low_rank, hidden_state, 0, 0)
    hidden_gradient = gated_product(
        row_gradient, down_weight, 1, 1
    ) + ADAPTER_SCALE * gated_product(backward_low_rank, adapter_down_input, 1, 0)
    gate_gradient = (
        hidden_gradient * up_total_sum * sigmoid_gate * (1.0 + gate_pre * (1.0 - sigmoid_gate))
    ).astype(jnp.bfloat16)
    up_gradient = (hidden_gradient * active).astype(jnp.bfloat16)
    up_output_gradient = ADAPTER_SCALE * gated_product(low_rank_up, up_gradient, 0, 0)
    up_low_rank = gated_product(up_gradient, adapter_up_output, 1, 1).astype(jnp.bfloat16)
    up_input_gradient = ADAPTER_SCALE * gated_product(up_low_rank, input_rows, 0, 0)
    slot_gradient = (
        gated_product(gate_gradient, gate_weight, 1, 1)
        + gated_product(up_gradient, up_weight, 1, 1)
        + ADAPTER_SCALE * gated_product(up_low_rank, adapter_up_input, 1, 0)
    ).astype(jnp.bfloat16)
    return (
        slot_gradient,
        up_input_gradient,
        up_output_gradient,
        down_input_gradient,
        down_output_gradient,
    )


def on_device(
    tokens,
    out_grad,
    gate_prob,
    routes,
    limits,
    w_gate,
    w_up,
    w_down,
    up_in,
    up_out,
    down_in,
    down_out,
):
    grp_count = lax.axis_size("grp")
    exp_count = lax.axis_size("exp")
    experts = grp_count * exp_count
    model_width = tokens.shape[1]
    top_count = routes.shape[1]
    pair_count = routes.shape[0] * top_count
    buffer_rows = experts * CAP
    flat_routes = routes.reshape(-1)
    onehot = (flat_routes[:, None] == jnp.arange(experts, dtype=jnp.int32)[None, :]).astype(
        jnp.int32
    )
    slot_rank = jnp.sum((jnp.cumsum(onehot, axis=0) - 1) * onehot, axis=1)
    limit_of = jnp.sum(onehot * limits[None, :], axis=1)
    kept_pair = slot_rank < limit_of
    where_to = jnp.where(kept_pair, flat_routes * CAP + slot_rank, buffer_rows)
    owner_slot = (
        jnp.full((buffer_rows,), -1, jnp.int32)
        .at[where_to]
        .set(jnp.arange(pair_count, dtype=jnp.int32), mode="drop")
    )
    valid_row = (owner_slot >= 0)[:, None]
    safe_owner = jnp.maximum(owner_slot, 0)
    token_idx = safe_owner // top_count
    input_rows = jnp.where(valid_row, tokens[token_idx], jnp.zeros((), jnp.bfloat16))
    scaled = (
        gate_prob.reshape(-1)[safe_owner][:, None] * out_grad[token_idx].astype(jnp.float32)
    ).astype(jnp.bfloat16)
    row_gradient = jnp.where(valid_row, scaled, jnp.zeros((), jnp.bfloat16))
    recv_in, recv_grad = (
        lax.all_to_all(
            input_rows.reshape(experts, CAP, model_width),
            ("grp", "exp"),
            split_axis=0,
            concat_axis=0,
            tiled=True,
        ),
        lax.all_to_all(
            row_gradient.reshape(experts, CAP, model_width),
            ("grp", "exp"),
            split_axis=0,
            concat_axis=0,
            tiled=True,
        ),
    )
    full_gate, full_up = (
        lax.all_gather(w_gate[0], "rep", axis=0, tiled=True),
        lax.all_gather(w_up[0], "rep", axis=0, tiled=True),
    )
    full_down = lax.all_gather(w_down[0], "rep", axis=1, tiled=True)
    (
        slot_gradient,
        up_input_gradient,
        up_output_gradient,
        down_input_gradient,
        down_output_gradient,
    ) = expert_backward_pass(
        recv_in.reshape(buffer_rows, model_width),
        recv_grad.reshape(buffer_rows, model_width),
        full_gate,
        full_up,
        full_down,
        up_in[0],
        up_out[0],
        down_in[0],
        down_out[0],
    )
    up_input_gradient, up_output_gradient, down_input_gradient, down_output_gradient = (
        lax.psum(up_input_gradient.astype(jnp.bfloat16), "rep").astype(jnp.float32),
        lax.psum(up_output_gradient.astype(jnp.bfloat16), "rep").astype(jnp.float32),
        lax.psum(down_input_gradient.astype(jnp.bfloat16), "rep").astype(jnp.float32),
        lax.psum(down_output_gradient.astype(jnp.bfloat16), "rep").astype(jnp.float32),
    )
    returned = lax.all_to_all(
        slot_gradient.reshape(experts, CAP, model_width),
        ("grp", "exp"),
        split_axis=0,
        concat_axis=0,
        tiled=True,
    )
    returned_rows = returned.reshape(buffer_rows, model_width)[jnp.where(kept_pair, where_to, 0)]
    returned_rows = jnp.where(
        kept_pair[:, None], returned_rows.astype(jnp.float32), jnp.zeros((), jnp.float32)
    )
    token_grad = jnp.sum(
        returned_rows.reshape(routes.shape[0], top_count, model_width), axis=1
    ).astype(jnp.bfloat16)
    return (
        token_grad,
        up_input_gradient[None],
        up_output_gradient[None],
        down_input_gradient[None],
        down_output_gradient[None],
    )


def solution(mesh):
    placed = (
        P(("rep", "grp", "exp"), None),
        P(("rep", "grp", "exp"), None),
        P(("rep", "grp", "exp"), None),
        P(("rep", "grp", "exp"), None),
        P(),
        P(("grp", "exp"), "rep", None),
        P(("grp", "exp"), "rep", None),
        P(("grp", "exp"), None, "rep"),
        P(("grp", "exp"), None, None),
        P(("grp", "exp"), None, None),
        P(("grp", "exp"), None, None),
        P(("grp", "exp"), None, None),
    )
    return jax.shard_map(
        on_device,
        mesh=mesh,
        in_specs=placed,
        out_specs=(
            P(("rep", "grp", "exp"), None),
            P(("grp", "exp"), None, None),
            P(("grp", "exp"), None, None),
            P(("grp", "exp"), None, None),
            P(("grp", "exp"), None, None),
        ),
        check_vma=False,
    )
```

profile of v0, /device:TPU:6, one launch (start us, length us, event | category | flops | bytes accessed | tf_op | source)
XLA Modules:
  0.0 328.6 jit_solution(2272713516282823981)
XLA Ops:
  11.3 2.5 gather_fusion.1
  13.8 3.2 reshape.152
  17.0 3.1 gather_fusion.2
  20.1 4.0 %gather.17 = bf16[128,3,2048]{2,1,0:T(4,128)(2,1)S(1)} reshape(bf16[384,2048]{1,0:T(8,128)(2,1)} %gather_fusion.2) | data formatting | bytes 3145728 | tf_op jit(solution)/shard_map/gather | solution.py:105
  24.3 2.8 gather_fusion
  27.6 4.7 %fusion.14 = (bf16[128,3,2048]{2,1,0:T(4,128)(2,1)S(1)}, bf16[128,3,2048]{2,1,0:T(4,128)(2,1)}) fusion(f32[128,3,2048]{2,1,0:T(4,128)} %reshape.152, f32[128,3]{1,0:T(8,128)S(1)} %mul.93, pred[128,3]{1,0:T(8,128)(4,1)S(1)} %broadcast_in_dim.79, bf16[128,3,2048]{2,1,0:T(4,128)(2,1)S(1)} %gather.17), kind=kLoop, calls=%fused_computation.23 | loop fusion | flops 3145728 | bytes 7866240 | tf_op jit(solution)/shard_map/jit(_where)/select_n | solution.py:109
  32.3 69.7 %all_to_all.15 = bf16[128,3,2048]{2,1,0:T(4,128)(2,1)} all-to-all(bf16[128,3,2048]{2,1,0:T(4,128)(2,1)S(1)} %get-tuple-element.13), channel_id=1, replica_groups=mesh['rep'=4,'grp'=8,'exp'=16] {'grp','exp'}, dimensions={0} | all-to-all | bytes 3145728 | tf_op jit(solution)/shard_map/all_to_all | solution.py:118
  102.0 8.6 %all-to-all-start.1 = ((bf16[128,3,2048]{2,1,0:T(4,128)(2,1)}), bf16[128,3,2048]{2,1,0:T(4,128)(2,1)}, u32[]{:S(2)}, u32[]{:S(2)}) async-start(bf16[128,3,2048]{2,1,0:T(4,128)(2,1)} %get-tuple-element.14), calls=%async_computation.1 | async-start | bytes 4194304 | tf_op jit(solution)/shard_map/all_to_all | solution.py:111
  111.3 3.9 %reshape.148 = bf16[384,2048]{1,0:T(8,128)(2,1)S(1)} reshape(bf16[128,3,2048]{2,1,0:T(4,128)(2,1)} %all_to_all.15) | data formatting | bytes 3145728 | tf_op jit(solution)/shard_map/reshape | solution.py:139
  115.2 46.8 %all-to-all-done.1 = bf16[128,3,2048]{2,1,0:T(4,128)(2,1)} async-done(((bf16[128,3,2048]{2,1,0:T(4,128)(2,1)}), bf16[128,3,2048]{2,1,0:T(4,128)(2,1)}, u32[]{:S(2)}, u32[]{:S(2)}) %all-to-all-start.1) | async-done | bytes 1572896 | tf_op jit(solution)/shard_map/all_to_all | solution.py:111
  162.0 3.9 %reshape.149 = bf16[384,2048]{1,0:T(8,128)(2,1)S(1)} reshape(bf16[128,3,2048]{2,1,0:T(4,128)(2,1)} %all-to-all-done.1) | data formatting | bytes 3145728 | tf_op jit(solution)/shard_map/reshape | solution.py:138
  167.1 3.3 %fusion.8 = f32[384,768]{1,0:T(8,128)S(1)} fusion(bf16[384,2048]{1,0:T(8,128)(2,1)S(1)} %reshape.148, bf16[1,768,2048]{2,1,0:T(8,128)(2,1)} %all-gather.7.cloned.1.call-done), kind=kOutput, calls=%fused_computation.14 | convolution fusion | flops 1207959552 | bytes 5898240 | tf_op jit(solution)/shard_map/dot_general | solution.py:13
  171.8 4.3 %fusion.6 = f32[384,768]{1,0:T(8,128)} fusion(bf16[384,2048]{1,0:T(8,128)(2,1)S(1)} %reshape.149, bf16[1,2048,768]{2,1,0:T(8,128)(2,1)} %all-gather.9.cloned.1.call-done), kind=kOutput, calls=%fused_computation.12 | convolution fusion | flops 1207959552 | bytes 5898240 | tf_op jit(solution)/shard_map/dot_general | solution.py:13
  176.2 3.4 %fusion.2 = f32[384,768]{1,0:T(8,128)S(1)} fusion(bf16[384,2048]{1,0:T(8,128)(2,1)S(1)} %reshape.149, bf16[1,2048,768]{2,1,0:T(8,128)(2,1)} %all-gather.11.cloned.1.call-done), kind=kOutput, calls=%fused_computation.8 | convolution fusion | flops 1207959552 | bytes 5898240 | tf_op jit(solution)/shard_map/dot_general | solution.py:13
  183.6 1.7 fusion
  185.3 1.7 add_convert_fusion
  187.1 5.1 %reshape.150 = bf16[128,3,2048]{2,1,0:T(4,128)(2,1)} reshape(bf16[384,2048]{1,0:T(8,128)(2,1)} %add_convert_fusion) | data formatting | bytes 3145728 | tf_op jit(solution)/shard_map/reshape | solution.py:155
  192.2 8.6 %all-to-all-start.2 = ((bf16[128,3,2048]{2,1,0:T(4,128)(2,1)}), bf16[128,3,2048]{2,1,0:T(4,128)(2,1)}, u32[]{:S(2)}, u32[]{:S(2)}) async-start(bf16[128,3,2048]{2,1,0:T(4,128)(2,1)} %reshape.150), calls=%async_computation.2 | async-start | bytes 4194304 | tf_op jit(solution)/shard_map/all_to_all | solution.py:154
  200.8 1.9 fusion.22
  202.7 1.9 fusion.21
  204.9 2.6 fusion.12
  208.7 47.3 %all-reduce.5.cloned.1.call-done = (bf16[1,32,768]{2,1,0:T(8,128)(2,1)}, bf16[1,32,768]{2,1,0:T(8,128)(2,1)}) async-done(((bf16[1,32,768]{2,1,0:T(8,128)(2,1)}, bf16[1,32,768]{2,1,0:T(8,128)(2,1)}), (bf16[1,32,768]{2,1,0:T(8,128)(2,1)}, bf16[1,32,768]{2,1,0:T(8,128)(2,1)})) %all-reduce.5.cloned.1.call-update) | async-done | bytes 98320 | tf_op jit(solution)/shard_map/psum | solution.py:150
  258.9 53.1 %all-reduce.7.cloned.1.call-done = (bf16[1,32,2048]{2,1,0:T(8,128)(2,1)}, bf16[1,32,2048]{2,1,0:T(8,128)(2,1)}) async-done(((bf16[1,32,2048]{2,1,0:T(8,128)(2,1)}, bf16[1,32,2048]{2,1,0:T(8,128)(2,1)}), (bf16[1,32,2048]{2,1,0:T(8,128)(2,1)}, bf16[1,32,2048]{2,1,0:T(8,128)(2,1)})) %all-reduce.7.cloned.1.call-update) | async-done | bytes 262160 | tf_op jit(solution)/shard_map/psum | solution.py:149
  315.2 3.9 %reshape.151 = bf16[384,2048]{1,0:T(8,128)(2,1)S(1)} reshape(bf16[128,3,2048]{2,1,0:T(4,128)(2,1)} %all-to-all-done.2) | data formatting | bytes 3145728 | tf_op jit(solution)/shard_map/reshape | solution.py:161
  (82 shorter events, 22.4 us)
Async XLA Ops:
  7.2 159.4 %copy-start = (bf16[1,32,2048]{2,1,0:T(8,128)(2,1)S(1)}, bf16[1,32,2048]{2,1,0:T(8,128)(2,1)}, u32[]{:S(2)}) copy-start(bf16[1,32,2048]{2,1,0:T(8,128)(2,1)} %param.20) | copy-start | bytes 393220
  7.2 1.5 copy-start.8
  7.2 2.4 copy-start.10
  7.2 4.1 %copy-start.1 = (bf16[32,2048]{1,0:T(8,128)(2,1)S(1)}, bf16[32,2048]{1,0:T(8,128)(2,1)}, u32[]{:S(2)}) copy-start(bf16[32,2048]{1,0:T(8,128)(2,1)} %param.13) | copy-start | bytes 393220
  7.2 159.9 %all-gather.7.cloned.1.call-start = ((), (), s32[]{:S(2)}) async-start(), calls=%async_computation.3 | async-start | bytes 3932160 | tf_op jit(solution)/shard_map/all_gather | solution.py:130
  7.9 163.9 %all-gather.9.cloned.1.call-start = ((), (), s32[]{:S(2)}) async-start(), calls=%async_computation.4 | async-start | bytes 3932160 | tf_op jit(solution)/shard_map/all_gather | solution.py:128
  13.8 3.2 copy-start.2
  20.1 4.0 %copy-start.9 = (f32[32,8]{0,1:T(8,128)S(1)}, f32[32,8]{0,1:T(8,128)}, u32[]{:S(2)}) copy-start(f32[32,8]{0,1:T(8,128)} %param.14) | copy-start | bytes 3076
  102.0 60.0 %all-to-all-start.1 = ((bf16[128,3,2048]{2,1,0:T(4,128)(2,1)}), bf16[128,3,2048]{2,1,0:T(4,128)(2,1)}, u32[]{:S(2)}, u32[]{:S(2)}) async-start(bf16[128,3,2048]{2,1,0:T(4,128)(2,1)} %get-tuple-element.14), calls=%async_computation.1 | async-start | bytes 4194304 | tf_op jit(solution)/shard_map/all_to_all | solution.py:111
  110.5 65.6 %all-gather.11.cloned.1.call-start = ((), (), s32[]{:S(2)}) async-start(), calls=%async_computation.5 | async-start | bytes 3932160 | tf_op jit(solution)/shard_map/all_gather | solution.py:127
  115.2 50.7 %copy-start.6 = (bf16[1,32,2048]{2,1,0:T(8,128)(2,1)S(1)}, bf16[1,32,2048]{2,1,0:T(8,128)(2,1)}, u32[]{:S(2)}) copy-start(bf16[1,32,2048]{2,1,0:T(8,128)(2,1)} %param.23) | copy-start | bytes 393220
  167.1 3.4 %copy-start.5 = (bf16[1,32,768]{2,1,0:T(8,128)(2,1)S(1)}, bf16[1,32,768]{2,1,0:T(8,128)(2,1)}, u32[]{:S(2)}) copy-start(bf16[1,32,768]{2,1,0:T(8,128)(2,1)} %param.22) | copy-start | bytes 147460
  176.2 3.4 %copy-start.7 = (bf16[1,32,768]{2,1,0:T(8,128)(2,1)S(1)}, bf16[1,32,768]{2,1,0:T(8,128)(2,1)}, u32[]{:S(2)}) copy-start(bf16[1,32,768]{2,1,0:T(8,128)(2,1)} %param.21) | copy-start | bytes 147460
  176.2 3.4 %copy-start.4 = (f32[384,768]{1,0:T(8,128)S(1)}, f32[384,768]{1,0:T(8,128)}, u32[]{:S(2)}) copy-start(f32[384,768]{1,0:T(8,128)} %fusion.16) | copy-start | bytes 3538948
  176.2 3.4 %copy-start.13 = (f32[384,768]{1,0:T(8,128)S(1)}, f32[384,768]{1,0:T(8,128)}, u32[]{:S(2)}) copy-start(f32[384,768]{1,0:T(8,128)} %fusion.6) | copy-start | bytes 3538948
  179.6 2.1 copy-start.11
  181.0 2.2 copy-start.3
  181.7 1.9 copy-start.12
  192.2 123.0 %all-to-all-start.2 = ((bf16[128,3,2048]{2,1,0:T(4,128)(2,1)}), bf16[128,3,2048]{2,1,0:T(4,128)(2,1)}, u32[]{:S(2)}, u32[]{:S(2)}) async-start(bf16[128,3,2048]{2,1,0:T(4,128)(2,1)} %reshape.150), calls=%async_computation.2 | async-start | bytes 4194304 | tf_op jit(solution)/shard_map/all_to_all | solution.py:154
  200.8 55.2 %all-reduce.5.cloned.1.call-start = ((), (), s32[]{:S(2)}) async-start(), calls=%async_computation.6 | async-start | bytes 196608 | tf_op jit(solution)/shard_map/psum | solution.py:150
  204.6 107.3 %all-reduce.7.cloned.1.call-start = ((), (), s32[]{:S(2)}) async-start(), calls=%async_computation.7 | async-start | bytes 524288 | tf_op jit(solution)/shard_map/psum | solution.py:149
Sparse Core Ops, SparseCore 0:
  10.1 47.6 all-gather.6
  59.9 45.1 all-gather.8
  113.5 43.4 all-gather.10
  204.7 51.1 all-reduce.4
  258.9 52.9 all-reduce.6
where the time goes:
time: 331 us; the launch traced here: 329 us
  waiting for transfers between devices  149 us (45%)
  blocking collectives  69.7 us (21%)
  local copies, waits for them, and re-layouts  37.5 us (11%)
  matrix products  27.4 us (8%)
  starting transfers between devices  17.7 us (5%)
  between operations  14.2 us (4%)
  other arithmetic  13 us (4%)
    all_to_all x1, blocking collectives, on_device(): lax.all_to_all(row_gradient.reshape(experts, CAP, model_width), ('grp', '...  69.7 us
    psum x1, waiting for transfers between devices, on_device(): lax.psum(up_input_gradient.astype(jnp.bfloat16), 'rep').astype(jnp.float32)  53.1 us
    psum x1, waiting for transfers between devices, on_device(): lax.psum(up_output_gradient.astype(jnp.bfloat16), 'rep').astype(jnp.float32)  47.3 us
    all_to_all x1, waiting for transfers between devices, on_device(): lax.all_to_all(input_rows.reshape(experts, CAP, model_width), ('grp', 'ex...  46.8 us
    dot_general x15, matrix products, gated_product(): lax.dot_general(left_side, right_side, (((left_dim,), (right_dim,)), ((),...  27.4 us
    all_to_all x1, starting transfers between devices, on_device(): lax.all_to_all(input_rows.reshape(experts, CAP, model_width), ('grp', 'ex...  8.56 us
    all_to_all x1, starting transfers between devices, on_device(): lax.all_to_all(slot_gradient.reshape(experts, CAP, model_width), ('grp',...  8.55 us
    gather x2, local copies, waits for them, and re-layouts, on_device(): tokens[token_idx]  7.13 us
  transfers between devices with their start and end apart: 7, of which 3 were waited for; matrix products, arithmetic and copies ran while one was open for 17% of the time, Pallas kernels for 0%

commit v1 on v0

v1 whole, which is shorter than its diff:
```python
import jax
import jax.numpy as jnp
from jax import lax
from jax.experimental import pallas as pl
from jax.experimental.pallas import tpu as pltpu
from jax.sharding import PartitionSpec as P

CAP = 3
LANES = 128
COLS = 256
SCALE = 2.0
F32 = jnp.float32
BF16 = jnp.bfloat16

VMEM = pl.BlockSpec(memory_space=pltpu.VMEM)
SMEM = pl.BlockSpec(memory_space=pltpu.SMEM)
ANY = pl.BlockSpec(memory_space=pl.ANY)


def params(mib):
    return pltpu.CompilerParams(vmem_limit_bytes=mib * 1024 * 1024)


def pack_kernel(gate, up, down, packed, sems):
    copies = []
    row = 0
    for ref in (gate, up, down):
        rows, cols = ref.shape[1:]
        for c in range(cols // COLS):
            copies.append(
                pltpu.make_async_copy(
                    ref.at[0, :, pl.ds(c * COLS, COLS)],
                    packed.at[pl.ds(row, rows), :],
                    sems.at[len(copies)],
                )
            )
            row += rows
    for copy in copies:
        copy.start()
    for copy in copies:
        copy.wait()


def pack_weights(w_gate, w_up, w_down):
    size = w_gate.size + w_up.size + w_down.size
    blocks = (w_gate.shape[2] + w_up.shape[2] + w_down.shape[2]) // COLS
    return pl.pallas_call(
        pack_kernel,
        out_shape=jax.ShapeDtypeStruct((size // COLS, COLS), BF16),
        in_specs=[ANY] * 3,
        out_specs=ANY,
        scratch_shapes=[pltpu.SemaphoreType.DMA((blocks,))],
        compiler_params=params(8),
        cost_estimate=pl.CostEstimate(flops=0, bytes_accessed=4 * size, transcendentals=0),
        name="pack_weights",
    )(w_gate, w_up, w_down)


def place_kernel(routes, prob, limits, tokens, grads, send, slots, count):
    experts = send.shape[0]
    send[...] = jnp.zeros_like(send)

    def clear(e, carry):
        count[e] = 0
        return carry

    lax.fori_loop(0, experts, clear, 0)

    def one_token(t, carry):
        row = tokens[t]
        grad = grads[t].astype(F32)
        for k in range(routes.shape[1]):
            e = routes[t, k]
            rank = count[e]
            count[e] = rank + 1
            kept = rank < limits[e]
            slots[t, k] = jnp.where(kept, e * CAP + rank, -1)

            @pl.when(kept)
            def _():
                send[e, rank] = row
                send[e, CAP + rank] = (prob[t, k] * grad).astype(BF16)

        return carry

    lax.fori_loop(0, routes.shape[0], one_token, 0)


def place_rows(routes, prob, limits, tokens, grads):
    count, width = tokens.shape
    subs = width // LANES
    experts = limits.shape[0]
    return pl.pallas_call(
        place_kernel,
        out_shape=(
            jax.ShapeDtypeStruct((experts, 2 * CAP, subs, LANES), BF16),
            jax.ShapeDtypeStruct(routes.shape, jnp.int32),
        ),
        in_specs=[SMEM, SMEM, SMEM, VMEM, VMEM],
        out_specs=(VMEM, SMEM),
        scratch_shapes=[pltpu.SMEM((experts,), jnp.int32)],
        compiler_params=params(16),
        name="place_rows",
    )(routes, prob, limits, tokens.reshape(count, subs, LANES), grads.reshape(count, subs, LANES))


def combine_kernel(slots, back, out):
    def one_token(t, carry):
        total = jnp.zeros(out.shape[1:], F32)
        for k in range(slots.shape[1]):
            slot = slots[t, k]
            row = back[jnp.maximum(slot, 0)].astype(F32)
            total += jnp.where(slot >= 0, row, 0.0)
        out[t] = total.astype(BF16)
        return carry

    lax.fori_loop(0, slots.shape[0], one_token, 0)


def combine_rows(slots, back):
    return pl.pallas_call(
        combine_kernel,
        out_shape=jax.ShapeDtypeStruct((slots.shape[0],) + back.shape[1:], BF16),
        in_specs=[SMEM, VMEM],
        out_specs=VMEM,
        compiler_params=params(16),
        name="combine_rows",
    )(slots, back)


def dot(left, right, left_dim, right_dim):
    return lax.dot_general(
        left, right, (((left_dim,), (right_dim,)), ((), ())), preferred_element_type=F32
    )


def expert_kernel(
    rows_in, rows_grad, packed, up_in, up_out, down_in, down_out,
    slot_grad, adapters,
    gate, up, down, hidden, grad_gate, grad_up, sems,
):
    width, inner = gate.shape
    shards = packed.shape[0]
    part = width // shards
    groups = []
    row = 0
    number = 0
    for ref, by_rows in ((gate, True), (up, True), (down, False)):
        copies = []
        rows, cols = (part, inner) if by_rows else (inner, part)
        for c in range(cols // COLS):
            for s in range(shards):
                if by_rows:
                    target = ref.at[pl.ds(s * part, part), pl.ds(c * COLS, COLS)]
                else:
                    target = ref.at[:, pl.ds(s * part + c * COLS, COLS)]
                copies.append(
                    pltpu.make_async_copy(packed.at[s, pl.ds(row, rows), :], target, sems.at[number])
                )
                number += 1
            row += rows
        groups.append(copies)
    for copies in groups:
        for copy in copies:
            copy.start()

    x = rows_in
    g = rows_grad
    low_up = dot(x[...], up_in[0], 1, 1).astype(BF16)
    back_low = dot(g[...], down_out[0], 1, 1).astype(BF16)
    for copies in groups:
        for copy in copies:
            copy.wait()
    for c in range(inner // COLS):
        cols = pl.ds(c * COLS, COLS)
        gate_pre = dot(x[...], gate[:, cols], 1, 0)
        up_sum = dot(x[...], up[:, cols], 1, 0) + SCALE * dot(low_up, up_out[0, :, cols], 1, 0)
        grad_hidden = dot(g[...], down[cols, :], 1, 1) + SCALE * dot(
            back_low, down_in[0, :, cols], 1, 0
        )
        sig = jax.nn.sigmoid(gate_pre)
        active = gate_pre * sig
        hidden[:, cols] = (active * up_sum).astype(BF16)
        grad_gate[:, cols] = (
            grad_hidden * up_sum * sig * (1.0 + gate_pre * (1.0 - sig))
        ).astype(BF16)
        grad_up[:, cols] = (grad_hidden * active).astype(BF16)
    low_down = dot(hidden[...], down_in[0], 1, 1).astype(BF16)
    up_low = dot(grad_up[...], up_out[0], 1, 1).astype(BF16)
    adapters[:, 0:width] = (SCALE * dot(up_low, x[...], 0, 0)).astype(BF16)
    adapters[:, width : 2 * width] = (SCALE * dot(low_down, g[...], 0, 0)).astype(BF16)
    adapters[:, 2 * width : 2 * width + inner] = (SCALE * dot(low_up, grad_up[...], 0, 0)).astype(BF16)
    adapters[:, 2 * width + inner :] = (SCALE * dot(back_low, hidden[...], 0, 0)).astype(BF16)
    for c in range(width // COLS):
        cols = pl.ds(c * COLS, COLS)
        slot_grad[:, cols] = (
            dot(grad_gate[...], gate[cols, :], 1, 1)
            + dot(grad_up[...], up[cols, :], 1, 1)
            + SCALE * dot(up_low, up_in[0, :, cols], 1, 0)
        ).astype(BF16)


def expert_backward(rows_in, rows_grad, packed, up_in, up_out, down_in, down_out):
    rows, width = rows_in.shape
    rank, inner = up_out.shape[1:]
    return pl.pallas_call(
        expert_kernel,
        out_shape=(
            jax.ShapeDtypeStruct((rows, width), BF16),
            jax.ShapeDtypeStruct((rank, 2 * (width + inner)), BF16),
        ),
        in_specs=[VMEM, VMEM, ANY] + [VMEM] * 4,
        out_specs=(VMEM, VMEM),
        scratch_shapes=[
            pltpu.VMEM((width, inner), BF16),
            pltpu.VMEM((width, inner), BF16),
            pltpu.VMEM((inner, width), BF16),
            pltpu.VMEM((rows, inner), BF16),
            pltpu.VMEM((rows, inner), BF16),
            pltpu.VMEM((rows, inner), BF16),
            pltpu.SemaphoreType.DMA((packed.size // (COLS * (width // packed.shape[0])),)),
        ],
        compiler_params=params(44),
        cost_estimate=pl.CostEstimate(
            flops=10 * rows * width * inner,
            bytes_accessed=6 * width * inner + 6 * rows * width,
            transcendentals=rows * inner,
        ),
        name="expert_backward",
    )(rows_in, rows_grad, packed, up_in, up_out, down_in, down_out)


def on_device(
    tokens, out_grad, gate_prob, routes, limits,
    w_gate, w_up, w_down, up_in, up_out, down_in, down_out,
):
    width = tokens.shape[1]
    inner = up_out.shape[2]
    experts = limits.shape[0]
    slot_rows = experts * CAP
    packed = lax.all_gather(pack_weights(w_gate, w_up, w_down), "rep")
    send, slots = place_rows(routes, gate_prob, limits, tokens, out_grad)
    recv = lax.all_to_all(send, ("grp", "exp"), split_axis=0, concat_axis=0, tiled=True)
    rows_in = recv[:, :CAP].reshape(slot_rows, width)
    rows_grad = recv[:, CAP:].reshape(slot_rows, width)
    slot_grad, adapters = expert_backward(
        rows_in, rows_grad, packed, up_in, up_out, down_in, down_out
    )
    adapters = lax.psum(adapters, "rep").astype(F32)
    back = lax.all_to_all(
        slot_grad.reshape(experts, CAP, width // LANES, LANES),
        ("grp", "exp"), split_axis=0, concat_axis=0, tiled=True,
    )
    token_grad = combine_rows(slots, back.reshape(slot_rows, width // LANES, LANES))
    return (
        token_grad.reshape(tokens.shape),
        adapters[None, :, 0:width],
        adapters[None, :, 2 * width : 2 * width + inner],
        adapters[None, :, 2 * width + inner :],
        adapters[None, :, width : 2 * width],
    )


def solution(mesh):
    rows = P(("rep", "grp", "exp"), None)
    owner = P(("grp", "exp"), None, None)
    return jax.shard_map(
        on_device,
        mesh=mesh,
        in_specs=(
            rows, rows, rows, rows, P(),
            P(("grp", "exp"), "rep", None),
            P(("grp", "exp"), "rep", None),
            P(("grp", "exp"), None, "rep"),
            owner, owner, owner, owner,
        ),
        out_specs=(rows, owner, owner, owner, owner),
        check_vma=False,
    )
```

time: 331 us -> 212 us (0.64)
  waiting for transfers between devices: 149 us -> 56.3 us
  local copies, waits for them, and re-layouts: 37.5 us -> 9.73 us
  matrix products: 27.4 us -> 0 us
  Pallas kernels: 0 us -> 23.1 us
  blocking collectives: 69.7 us -> 91 us
  other arithmetic: 13 us -> 1.03 us
    all_to_all x2 -> x1, waiting for transfers between devices: 46.8 us -> 0.01 us  [on_device(): lax.all_to_all(slot_grad.reshape(experts, CAP, width // LANES, LANES), ('...]
    psum x2 -> x1, waiting for transfers between devices: 100 us -> 55.3 us  [on_device(): adapters = lax.psum(adapters, 'rep').astype(F32)]
    dot_general x15 -> x0, matrix products: 27.4 us -> none  [gated_product(): lax.dot_general(left_side, right_side, (((left_dim,), (right_dim,)), ((),...]
    pallas_call x0 -> x4, Pallas kernels: none -> 23.1 us  [the longest x1 12.9 us: expert_backward(): pl.pallas_call(expert_kernel, out_shape=(jax.ShapeDtypeStruct((rows, widt...]
    all_to_all x1, blocking collectives: 69.7 us -> 91 us  [on_device(): lax.all_to_all(send, ('grp', 'exp'), split_axis=0, concat_axis=0, tiled=T...]
    reshape x5 -> x1, local copies, waits for them, and re-layouts: 17 us -> 1.02 us  [on_device(): rows_grad = recv[:, CAP:].reshape(slot_rows, width)]
    gather x5 -> x0, local copies, waits for them, and re-layouts: 13.8 us -> none  [the longest x2 7.13 us: on_device(): tokens[token_idx]]
    broadcast_in_dim x4 -> x0, other arithmetic: 6.14 us -> none  [the longest x1 1.62 us: on_device(): up_input_gradient[None]]
  transfers between devices with their start and end apart: 7 -> 3, of which waited for: 3 -> 2; matrix products, arithmetic and copies ran while one was open for 17% -> 2% of each run, Pallas kernels for 0% -> 3%
where the time goes in v1:
time: 212 us; the launch traced here: 210 us
  blocking collectives  91 us (43%)
  waiting for transfers between devices  56.3 us (27%)
  Pallas kernels  23.1 us (11%)
  starting transfers between devices  14.8 us (7%)
  between operations  14.2 us (7%)
  local copies, waits for them, and re-layouts  9.73 us (5%)
    all_to_all x1, blocking collectives, on_device(): lax.all_to_all(send, ('grp', 'exp'), split_axis=0, concat_axis=0, tiled=T...  91 us
    psum x1, waiting for transfers between devices, on_device(): adapters = lax.psum(adapters, 'rep').astype(F32)  55.3 us
    all_to_all x1, starting transfers between devices, on_device(): lax.all_to_all(slot_grad.reshape(experts, CAP, width // LANES, LANES), ('...  14.7 us
    pallas_call x1, Pallas kernels, expert_backward(): pl.pallas_call(expert_kernel, out_shape=(jax.ShapeDtypeStruct((rows, widt...  12.9 us
    pallas_call x1, Pallas kernels, place_rows(): pl.pallas_call(place_kernel, out_shape=(jax.ShapeDtypeStruct((experts, 2...  7.04 us
    unnamed x30, local copies, waits for them, and re-layouts  6.66 us
  transfers between devices with their start and end apart: 3, of which 2 were waited for; matrix products, arithmetic and copies ran while one was open for 2% of the time, Pallas kernels for 3%

profile of v1, /device:TPU:6, one launch (start us, length us, event | category | flops | bytes accessed | tf_op | source)
XLA Modules:
  0.0 210.2 jit_solution(14534252243297859966)
XLA Ops:
  7.2 1.1 copy-done
  8.3 1.1 copy-done.1
  9.5 1.1 copy-done.2
  10.6 1.5 pack_weights.1
  12.2 0.6 copy-done.10
  12.8 0.1 copy.17.routes
  12.8 0.1 copy.18.prob
  12.9 0.1 copy-done.8
  13.1 7.0 %place_rows.1 = (bf16[128,6,16,128]{3,2,1,0:T(8,128)(2,1)S(1)}, s32[32,8]{1,0:T(8,128)S(1)}) custom-call(s32[32,8]{1,0:T(8,128)S(1)} %copy.17.routes, f32[32,8]{1,0:T(8,128)S(1)} %copy.18.prob, s32[128]{0:T(128)S(1)} %copy-done.3, bf16[32,16,128]{2,1,0:T(8,128)(2,1)S(1)} %bitcast.31, bf16[32,16,128]{2,1,0:T(8,128)(2,1)S(1)} %bitcast.32), custom_call_target="tpu_custom_call" | custom-call | tf_op jit(solution)/shard_map/place_rows/pallas_call | solution.py:93
  20.2 91.0 %all_to_all.10 = bf16[128,6,16,128]{3,2,1,0:T(8,128)(2,1)S(1)} all-to-all(bf16[128,6,16,128]{3,2,1,0:T(8,128)(2,1)S(1)} %get-tuple-element.10), channel_id=1, replica_groups=mesh['rep'=4,'grp'=8,'exp'=16] {'grp','exp'}, dimensions={0} | all-to-all | bytes 6291456 | tf_op jit(solution)/shard_map/all_to_all | solution.py:243
  111.1 0.5 fusion
  111.7 1.0 copy_bitcast_fusion
  112.8 0.3 all-gather.3.cloned.1.call-done
  113.1 12.9 %expert_backward.1 = (bf16[384,2048]{1,0:T(8,128)(2,1)S(1)}, bf16[32,5632]{1,0:T(8,128)(2,1)}) custom-call(bf16[384,2048]{1,0:T(8,128)(2,1)S(1)} %get-tuple-element.20.rows_in, bf16[384,2048]{1,0:T(8,128)(2,1)S(1)} %get-tuple-element.19.rows_grad, bf16[4,4608,256]{2,1,0:T(8,128)(2,1)} %bitcast.39, bf16[1,32,2048]{2,1,0:T(8,128)(2,1)S(1)} %copy-done.4, ...), custom_call_target="tpu_custom_call" | custom-call | flops 6039797760 | bytes 14155776 | tf_op jit(solution)/shard_map/expert_backward/pallas_call | solution.py:206
  126.0 1.6 copy.23
  127.6 14.7 %all-to-all-start.1 = ((bf16[128,3,16,128]{3,2,1,0:T(8,128)(2,1)}), bf16[128,3,16,128]{3,2,1,0:T(8,128)(2,1)S(1)}, u32[]{:S(2)}, u32[]{:S(2)}) async-start(bf16[128,3,16,128]{3,2,1,0:T(8,128)(2,1)} %bitcast.18), calls=%async_computation.1 | async-start | bytes 3145728 | tf_op jit(solution)/shard_map/all_to_all | solution.py:250
  142.3 0.0 all-reduce.2.cloned.1.call-start
  142.4 0.7 all-reduce.2.cloned.1.call-update
  143.1 55.3 %all-reduce.2.cloned.1.call-done = bf16[32,5632]{1,0:T(8,128)(2,1)} async-done(((bf16[32,5632]{1,0:T(8,128)(2,1)}), bf16[32,5632]{1,0:T(8,128)(2,1)}) %all-reduce.2.cloned.1.call-update) | async-done | bytes 360464 | tf_op jit(solution)/shard_map/psum | solution.py:249
  198.4 1.0 convert_element_type.3
  199.4 0.7 slice_bitcast_fusion.2
  200.1 0.8 slice_bitcast_fusion
  201.0 1.7 combine_rows.1
  202.6 0.7 copy.28
  (24 shorter events, 0.2 us)
Async XLA Ops:
  7.2 105.9 %all-gather.3.cloned.1.call-start = ((), (), s32[]{:S(2)}) async-start(), calls=%async_computation.3 | async-start | bytes 11796480 | tf_op jit(solution)/shard_map/all_gather | solution.py:241
  7.2 1.1 copy-start
  8.3 1.1 copy-start.1
  9.5 1.1 copy-start.2
  12.1 0.7 copy-start.10
  12.1 0.8 copy-start.11
  12.1 0.9 copy-start.8
  12.1 1.0 copy-start.9
  12.1 1.0 copy-start.3
  111.7 1.4 copy-start.4
  111.7 1.4 copy-start.5
  111.7 1.4 copy-start.6
  111.7 1.4 copy-start.7
  127.6 73.4 %all-to-all-start.1 = ((bf16[128,3,16,128]{3,2,1,0:T(8,128)(2,1)}), bf16[128,3,16,128]{3,2,1,0:T(8,128)(2,1)S(1)}, u32[]{:S(2)}, u32[]{:S(2)}) async-start(bf16[128,3,16,128]{3,2,1,0:T(8,128)(2,1)} %bitcast.18), calls=%async_computation.1 | async-start | bytes 3145728 | tf_op jit(solution)/shard_map/all_to_all | solution.py:250
  142.3 56.1 %all-reduce.2.cloned.1.call-start = ((), (), s32[]{:S(2)}) async-start(), calls=%async_computation.2 | async-start | bytes 720896 | tf_op jit(solution)/shard_map/psum | solution.py:249
Sparse Core Ops, SparseCore 0:
  12.3 100.7 all-gather.2
  145.5 52.8 all-reduce.1

commit v2 on v1

--- a/solution.py
+++ b/solution.py
@@ -50,21 +50,21 @@
         in_specs=[ANY] * 3,
         out_specs=ANY,
         scratch_shapes=[pltpu.SemaphoreType.DMA((blocks,))],
-        compiler_params=params(8),
+        compiler_params=params(56),
         cost_estimate=pl.CostEstimate(flops=0, bytes_accessed=4 * size, transcendentals=0),
         name="pack_weights",
     )(w_gate, w_up, w_down)
 
 
-def place_kernel(routes, prob, limits, tokens, grads, send, slots, count):
-    experts = send.shape[0]
-    send[...] = jnp.zeros_like(send)
+def place_kernel(routes, prob, limits, tokens, grads, send, slots, count, staged):
+    total = send.shape[0]
+    staged[...] = jnp.zeros_like(staged)
 
     def clear(e, carry):
         count[e] = 0
         return carry
 
-    lax.fori_loop(0, experts, clear, 0)
+    lax.fori_loop(0, limits.shape[0], clear, 0, unroll=8)
 
     def one_token(t, carry):
         row = tokens[t]
@@ -75,30 +75,32 @@
             count[e] = rank + 1
             kept = rank < limits[e]
             slots[t, k] = jnp.where(kept, e * CAP + rank, -1)
-
-            @pl.when(kept)
-            def _():
-                send[e, rank] = row
-                send[e, CAP + rank] = (prob[t, k] * grad).astype(BF16)
-
+            place = jnp.where(kept, e * (2 * CAP) + rank, total)
+            staged[place] = row
+            staged[place + CAP] = (prob[t, k] * grad).astype(BF16)
         return carry
 
     lax.fori_loop(0, routes.shape[0], one_token, 0)
+    send[...] = staged[0:total]
 
 
 def place_rows(routes, prob, limits, tokens, grads):
     count, width = tokens.shape
     subs = width // LANES
     experts = limits.shape[0]
+    total = experts * 2 * CAP
     return pl.pallas_call(
         place_kernel,
         out_shape=(
-            jax.ShapeDtypeStruct((experts, 2 * CAP, subs, LANES), BF16),
+            jax.ShapeDtypeStruct((total, subs, LANES), BF16),
             jax.ShapeDtypeStruct(routes.shape, jnp.int32),
         ),
         in_specs=[SMEM, SMEM, SMEM, VMEM, VMEM],
         out_specs=(VMEM, SMEM),
-        scratch_shapes=[pltpu.SMEM((experts,), jnp.int32)],
+        scratch_shapes=[
+            pltpu.SMEM((experts,), jnp.int32),
+            pltpu.VMEM((total + 2 * CAP, subs, LANES), BF16),
+        ],
         compiler_params=params(16),
         name="place_rows",
     )(routes, prob, limits, tokens.reshape(count, subs, LANES), grads.reshape(count, subs, LANES))
@@ -134,49 +136,52 @@
     )
 
 
-def expert_kernel(
+def slot_kernel(
     rows_in, rows_grad, packed, up_in, up_out, down_in, down_out,
-    slot_grad, adapters,
-    gate, up, down, hidden, grad_gate, grad_up, sems,
+    slot_grad, hidden, grad_up, low_up, back_low, up_low,
+    gate, up, down, grad_gate, sems,
 ):
     width, inner = gate.shape
     shards = packed.shape[0]
     part = width // shards
-    groups = []
-    row = 0
+    chunks = inner // COLS
+    steps = []
     number = 0
-    for ref, by_rows in ((gate, True), (up, True), (down, False)):
+    for c in range(chunks):
+        cols = pl.ds(c * COLS, COLS)
+        moves = []
+        for s in range(shards):
+            for base, ref in ((0, gate), (chunks * part, up)):
+                moves.append(
+                    (packed.at[s, pl.ds(base + c * part, part), :], ref.at[pl.ds(s * part, part), cols])
+                )
+        for s in range(shards):
+            for m in range(part // COLS):
+                row = 2 * chunks * part + m * inner + c * COLS
+                moves.append(
+                    (packed.at[s, pl.ds(row, COLS), :], down.at[cols, pl.ds(s * part + m * COLS, COLS)])
+                )
         copies = []
-        rows, cols = (part, inner) if by_rows else (inner, part)
-        for c in range(cols // COLS):
-            for s in range(shards):
-                if by_rows:
-                    target = ref.at[pl.ds(s * part, part), pl.ds(c * COLS, COLS)]
-                else:
-                    target = ref.at[:, pl.ds(s * part + c * COLS, COLS)]
-                copies.append(
-                    pltpu.make_async_copy(packed.at[s, pl.ds(row, rows), :], target, sems.at[number])
-                )
-                number += 1
-            row += rows
-        groups.append(copies)
-    for copies in groups:
+        for source, target in moves:
+            copies.append(pltpu.make_async_copy(source, target, sems.at[number]))
+            number += 1
+        steps.append(copies)
+    for copies in steps:
         for copy in copies:
             copy.start()
 
     x = rows_in
     g = rows_grad
-    low_up = dot(x[...], up_in[0], 1, 1).astype(BF16)
-    back_low = dot(g[...], down_out[0], 1, 1).astype(BF16)
-    for copies in groups:
-        for copy in copies:
+    low_up[...] = dot(x[...], up_in[0], 1, 1).astype(BF16)
+    back_low[...] = dot(g[...], down_out[0], 1, 1).astype(BF16)
+    for c in range(chunks):
+        cols = pl.ds(c * COLS, COLS)
+        for copy in steps[c]:
             copy.wait()
-    for c in range(inner // COLS):
-        cols = pl.ds(c * COLS, COLS)
         gate_pre = dot(x[...], gate[:, cols], 1, 0)
-        up_sum = dot(x[...], up[:, cols], 1, 0) + SCALE * dot(low_up, up_out[0, :, cols], 1, 0)
+        up_sum = dot(x[...], up[:, cols], 1, 0) + SCALE * dot(low_up[...], up_out[0, :, cols], 1, 0)
         grad_hidden = dot(g[...], down[cols, :], 1, 1) + SCALE * dot(
-            back_low, down_in[0, :, cols], 1, 0
+            back_low[...], down_in[0, :, cols], 1, 0
         )
         sig = jax.nn.sigmoid(gate_pre)
         active = gate_pre * sig
@@ -185,40 +190,55 @@
             grad_hidden * up_sum * sig * (1.0 + gate_pre * (1.0 - sig))
         ).astype(BF16)
         grad_up[:, cols] = (grad_hidden * active).astype(BF16)
-    low_down = dot(hidden[...], down_in[0], 1, 1).astype(BF16)
-    up_low = dot(grad_up[...], up_out[0], 1, 1).astype(BF16)
-    adapters[:, 0:width] = (SCALE * dot(up_low, x[...], 0, 0)).astype(BF16)
-    adapters[:, width : 2 * width] = (SCALE * dot(low_down, g[...], 0, 0)).astype(BF16)
-    adapters[:, 2 * width : 2 * width + inner] = (SCALE * dot(low_up, grad_up[...], 0, 0)).astype(BF16)
-    adapters[:, 2 * width + inner :] = (SCALE * dot(back_low, hidden[...], 0, 0)).astype(BF16)
+    up_low[...] = dot(grad_up[...], up_out[0], 1, 1).astype(BF16)
     for c in range(width // COLS):
         cols = pl.ds(c * COLS, COLS)
         slot_grad[:, cols] = (
             dot(grad_gate[...], gate[cols, :], 1, 1)
             + dot(grad_up[...], up[cols, :], 1, 1)
-            + SCALE * dot(up_low, up_in[0, :, cols], 1, 0)
+            + SCALE * dot(up_low[...], up_in[0, :, cols], 1, 0)
         ).astype(BF16)
 
 
-def expert_backward(rows_in, rows_grad, packed, up_in, up_out, down_in, down_out):
+def adapter_kernel(rows_in, rows_grad, hidden, grad_up, low_up, back_low, up_low, down_in, adapters):
+    width, inner = rows_in.shape[1], hidden.shape[1]
+    low_down = dot(hidden[...], down_in[0], 1, 1).astype(BF16)
+    at = 0
+    for left, right in (
+        (up_low[...], rows_in),
+        (low_down, rows_grad),
+        (low_up[...], grad_up),
+        (back_low[...], hidden),
+    ):
+        for c in range(right.shape[1] // COLS):
+            piece = dot(left, right[:, pl.ds(c * COLS, COLS)], 0, 0)
+            adapters[:, pl.ds(at, COLS)] = (SCALE * piece).astype(BF16)
+            at += COLS
+
+
+def expert_slots(rows_in, rows_grad, packed, up_in, up_out, down_in, down_out):
     rows, width = rows_in.shape
     rank, inner = up_out.shape[1:]
-    return pl.pallas_call(
-        expert_kernel,
+    shards = packed.shape[0]
+    part = width // shards
+    return pl.pallas_call(
+        slot_kernel,
         out_shape=(
             jax.ShapeDtypeStruct((rows, width), BF16),
-            jax.ShapeDtypeStruct((rank, 2 * (width + inner)), BF16),
+            jax.ShapeDtypeStruct((rows, inner), BF16),
+            jax.ShapeDtypeStruct((rows, inner), BF16),
+            jax.ShapeDtypeStruct((rows, rank), BF16),
+            jax.ShapeDtypeStruct((rows, rank), BF16),
+            jax.ShapeDtypeStruct((rows, rank), BF16),
         ),
         in_specs=[VMEM, VMEM, ANY] + [VMEM] * 4,
-        out_specs=(VMEM, VMEM),
+        out_specs=(VMEM,) * 6,
         scratch_shapes=[
             pltpu.VMEM((width, inner), BF16),
             pltpu.VMEM((width, inner), BF16),
             pltpu.VMEM((inner, width), BF16),
             pltpu.VMEM((rows, inner), BF16),
-            pltpu.VMEM((rows, inner), BF16),
-            pltpu.VMEM((rows, inner), BF16),
-            pltpu.SemaphoreType.DMA((packed.size // (COLS * (width // packed.shape[0])),)),
+            pltpu.SemaphoreType.DMA((shards * (2 + part // COLS) * (inner // COLS),)),
         ],
         compiler_params=params(44),
         cost_estimate=pl.CostEstimate(
@@ -226,8 +246,36 @@
             bytes_accessed=6 * width * inner + 6 * rows * width,
             transcendentals=rows * inner,
         ),
-        name="expert_backward",
+        name="expert_slots",
     )(rows_in, rows_grad, packed, up_in, up_out, down_in, down_out)
+
+
+def adapter_grads(rows_in, rows_grad, hidden, grad_up, low_up, back_low, up_low, down_in):
+    rows, width = rows_in.shape
+    inner = hidden.shape[1]
+    rank = up_low.shape[1]
+    return pl.pallas_call(
+        adapter_kernel,
+        out_shape=jax.ShapeDtypeStruct((rank, 2 * (width + inner)), BF16),
+        in_specs=[VMEM] * 8,
+        out_specs=VMEM,
+        compiler_params=params(24),
+        cost_estimate=pl.CostEstimate(
+            flops=4 * rows * rank * (width + inner),
+            bytes_accessed=4 * rows * (width + inner),
+            transcendentals=0,
+        ),
+        name="adapter_grads",
+    )(rows_in, rows_grad, hidden, grad_up, low_up, back_low, up_low, down_in)
+
+
+def replica_sum(own, axis):
+    count = lax.axis_size(axis)
+    total = own.astype(F32)
+    for shift in range(1, count):
+        pairs = [(i, (i + shift) % count) for i in range(count)]
+        total += lax.ppermute(own, axis, pairs).astype(F32)
+    return total
 
 
 def on_device(
@@ -240,13 +288,12 @@
     slot_rows = experts * CAP
     packed = lax.all_gather(pack_weights(w_gate, w_up, w_down), "rep")
     send, slots = place_rows(routes, gate_prob, limits, tokens, out_grad)
+    send = send.reshape(experts, 2 * CAP, width // LANES, LANES)
     recv = lax.all_to_all(send, ("grp", "exp"), split_axis=0, concat_axis=0, tiled=True)
     rows_in = recv[:, :CAP].reshape(slot_rows, width)
     rows_grad = recv[:, CAP:].reshape(slot_rows, width)
-    slot_grad, adapters = expert_backward(
-        rows_in, rows_grad, packed, up_in, up_out, down_in, down_out
-    )
-    adapters = lax.psum(adapters, "rep").astype(F32)
+    slot_grad, *kept = expert_slots(rows_in, rows_grad, packed, up_in, up_out, down_in, down_out)
+    adapters = replica_sum(adapter_grads(rows_in, rows_grad, *kept, down_in), "rep")
     back = lax.all_to_all(
         slot_grad.reshape(experts, CAP, width // LANES, LANES),
         ("grp", "exp"), split_axis=0, concat_axis=0, tiled=True,

time: 212 us -> 263 us (1.24)
  Pallas kernels: 23.1 us -> 91 us
  waiting for transfers between devices: 56.3 us -> 27.8 us
  starting transfers between devices: 14.8 us -> 25.5 us
    pallas_call x1, Pallas kernels: 1.45 us -> 72.6 us  [pack_weights(): pl.pallas_call(pack_kernel, out_shape=jax.ShapeDtypeStruct((size // COLS,...]
    psum x1 -> x0, waiting for transfers between devices: 55.3 us -> none  [on_device(): adapters = lax.psum(adapters, 'rep').astype(F32)]
    ppermute x0 -> x3, waiting for transfers between devices: none -> 12.5 us  [replica_sum(): total += lax.ppermute(own, axis, pairs).astype(F32)]
    all_to_all x1, waiting for transfers between devices: 0.01 us -> 12.1 us  [on_device(): lax.all_to_all(slot_grad.reshape(experts, CAP, width // LANES, LANES), ('...]
    ppermute x0 -> x3, starting transfers between devices: none -> 10.7 us  [replica_sum(): total += lax.ppermute(own, axis, pairs).astype(F32)]
    pallas_call x2 -> x3, Pallas kernels: 19.9 us -> 16.7 us  [the longest x1 11.5 us: expert_slots(): pl.pallas_call(slot_kernel, out_shape=(jax.ShapeDtypeStruct((rows, width)...]
    all_gather x1, waiting for transfers between devices: 0.31 us -> 3.13 us  [on_device(): packed = lax.all_gather(pack_weights(w_gate, w_up, w_down), 'rep')]
    unnamed x30 -> x36, local copies, waits for them, and re-layouts: 6.66 us -> 8.62 us
  transfers between devices with their start and end apart: 3 -> 5, of which waited for: 2 -> 4; matrix products, arithmetic and copies ran while one was open for 2% -> 1% of each run, Pallas kernels for 3% -> 2%
where the time goes in v2:
time: 263 us; the launch traced here: 261 us
  Pallas kernels  91 us (35%)
  blocking collectives  91 us (35%)
  waiting for transfers between devices  27.8 us (11%)
  starting transfers between devices  25.5 us (10%)
  between operations  14.2 us (5%)
  local copies, waits for them, and re-layouts  11.7 us (4%)
    all_to_all x1, blocking collectives, on_device(): lax.all_to_all(send, ('grp', 'exp'), split_axis=0, concat_axis=0, tiled=T...  91 us
    pallas_call x1, Pallas kernels, pack_weights(): pl.pallas_call(pack_kernel, out_shape=jax.ShapeDtypeStruct((size // COLS,...  72.6 us
    all_to_all x1, starting transfers between devices, on_device(): lax.all_to_all(slot_grad.reshape(experts, CAP, width // LANES, LANES), ('...  14.7 us
    ppermute x3, waiting for transfers between devices, replica_sum(): total += lax.ppermute(own, axis, pairs).astype(F32)  12.5 us
    all_to_all x1, waiting for transfers between devices, on_device(): lax.all_to_all(slot_grad.reshape(experts, CAP, width // LANES, LANES), ('...  12.1 us
    pallas_call x1, Pallas kernels, expert_slots(): pl.pallas_call(slot_kernel, out_shape=(jax.ShapeDtypeStruct((rows, width)...  11.5 us
    ppermute x3, starting transfers between devices, replica_sum(): total += lax.ppermute(own, axis, pairs).astype(F32)  10.7 us
    unnamed x36, local copies, waits for them, and re-layouts  8.62 us
  transfers between devices with their start and end apart: 5, of which 4 were waited for; matrix products, arithmetic and copies ran while one was open for 1% of the time, Pallas kernels for 2%

profile of v2, /device:TPU:6, one launch (start us, length us, event | category | flops | bytes accessed | tf_op | source)
XLA Modules:
  0.0 261.4 jit_solution(5246387108866322244)
XLA Ops:
  7.2 72.6 %pack_weights.1 = bf16[4608,256]{1,0:T(8,128)(2,1)} custom-call(bf16[1,512,768]{2,1,0:T(8,128)(2,1)} %gate.1, bf16[1,512,768]{2,1,0:T(8,128)(2,1)} %up.1, bf16[1,768,512]{2,1,0:T(8,128)(2,1)} %down.1), custom_call_target="tpu_custom_call" | custom-call | bytes 4718592 | tf_op jit(solution)/shard_map/pack_weights/pallas_call | solution.py:47
  80.9 4.2 %place_rows.1 = (bf16[768,16,128]{2,1,0:T(8,128)(2,1)S(1)}, s32[32,8]{1,0:T(8,128)S(1)}) custom-call(s32[32,8]{1,0:T(8,128)S(1)} %copy.17.routes, f32[32,8]{1,0:T(8,128)S(1)} %copy.18.prob, s32[128]{0:T(128)S(1)} %copy-done.7, bf16[32,16,128]{2,1,0:T(8,128)(2,1)S(1)} %bitcast.33, bf16[32,16,128]{2,1,0:T(8,128)(2,1)S(1)} %bitcast.34), custom_call_target="tpu_custom_call" | custom-call | tf_op jit(solution)/shard_map/place_rows/pallas_call | solution.py:92
  85.1 91.0 %all_to_all.10 = bf16[128,6,16,128]{3,2,1,0:T(8,128)(2,1)S(1)} all-to-all(bf16[128,6,16,128]{3,2,1,0:T(8,128)(2,1)S(1)} %bitcast.31), channel_id=1, replica_groups=mesh['rep'=4,'grp'=8,'exp'=16] {'grp','exp'}, dimensions={0} | all-to-all | bytes 6291456 | tf_op jit(solution)/shard_map/all_to_all | solution.py:292
  176.7 1.0 copy_bitcast_fusion
  177.7 3.1 %all-gather.3.cloned.1.call-done = bf16[18432,256]{1,0:T(8,128)(2,1)} async-done(((bf16[4608,256]{1,0:T(8,128)(2,1)}), bf16[18432,256]{1,0:T(8,128)(2,1)}) %all-gather.3.cloned.1.call-update) | async-done | bytes 9437200 | tf_op jit(solution)/shard_map/all_gather | solution.py:289
  180.9 0.9 copy-done.8
  181.8 0.9 copy-done.9
  182.7 11.5 %expert_slots.1 = (bf16[384,2048]{1,0:T(8,128)(2,1)S(1)}, bf16[384,768]{1,0:T(8,128)(2,1)S(1)}, bf16[384,768]{1,0:T(8,128)(2,1)S(1)}, bf16[384,32]{1,0:T(8,128)(...) custom-call(bf16[384,2048]{1,0:T(8,128)(2,1)S(1)} %get-tuple-element.28.rows_in, ...), custom_call_target="tpu_custom_call" | custom-call | flops 6039797760 | bytes 14155776 | tf_op jit(solution)/shard_map/expert_slots/pallas_call | solution.py:224
  194.2 1.6 copy.23
  195.8 14.7 %all-to-all-start.1 = ((bf16[128,3,16,128]{3,2,1,0:T(8,128)(2,1)}), bf16[128,3,16,128]{3,2,1,0:T(8,128)(2,1)S(1)}, u32[]{:S(2)}, u32[]{:S(2)}) async-start(bf16[128,3,16,128]{3,2,1,0:T(8,128)(2,1)} %bitcast.36), calls=%async_computation.1 | async-start | bytes 3145728 | tf_op jit(solution)/shard_map/all_to_all | solution.py:297
  210.6 1.4 copy-done.1
  212.0 1.1 copy-done.3
  213.0 1.1 copy-done.5
  214.1 1.0 adapter_grads.1
  215.1 3.4 %collective-permute-start.2 = (bf16[32,5632]{1,0:T(8,128)(2,1)S(1)}, bf16[32,5632]{1,0:T(8,128)(2,1)S(1)}, u32[]{:S(2)}, u32[]{:S(2)}) collective-permute-start(bf16[32,5632]{1,0:T(8,128)(2,1)S(1)} %adapter_grads.1), channel_id=1, source_target_pairs={{0,384},{128,0},{256,128},{384,256},{1,385},{129,1},{257,129},{385... | collective-permute-start | bytes 1081352 | tf_op jit(solution)/shard_map/ppermute | solution.py:277
  218.5 3.3 %collective-permute-start.1 = (bf16[32,5632]{1,0:T(8,128)(2,1)S(1)}, bf16[32,5632]{1,0:T(8,128)(2,1)S(1)}, u32[]{:S(2)}, u32[]{:S(2)}) collective-permute-start(bf16[32,5632]{1,0:T(8,128)(2,1)S(1)} %adapter_grads.1), channel_id=1, source_target_pairs={{0,256},{128,384},{256,0},{384,128},{1,257},{129,385},{257,1},{385... | collective-permute-start | bytes 1081352 | tf_op jit(solution)/shard_map/ppermute | solution.py:277
  221.9 4.0 %collective-permute-start = (bf16[32,5632]{1,0:T(8,128)(2,1)S(1)}, bf16[32,5632]{1,0:T(8,128)(2,1)S(1)}, u32[]{:S(2)}, u32[]{:S(2)}) collective-permute-start(bf16[32,5632]{1,0:T(8,128)(2,1)S(1)} %adapter_grads.1), channel_id=1, source_target_pairs={{0,128},{128,256},{256,384},{384,0},{1,129},{129,257},{257,385},{3... | collective-permute-start | bytes 1081352 | tf_op jit(solution)/shard_map/ppermute | solution.py:277
  225.9 10.0 %collective-permute-done.2 = bf16[32,5632]{1,0:T(8,128)(2,1)S(1)} collective-permute-done((bf16[32,5632]{1,0:T(8,128)(2,1)S(1)}, bf16[32,5632]{1,0:T(8,128)(2,1)S(1)}, u32[]{:S(2)}, u32[]{:S(2)}) %collective-permute-start.2) | collective-permute-done | bytes 360480 | tf_op jit(solution)/shard_map/ppermute | solution.py:277
  235.9 2.5 collective-permute-done
  238.6 0.7 slice_bitcast_fusion.2
  239.3 0.8 slice_bitcast_fusion
  240.1 12.1 %all-to-all-done.1 = bf16[128,3,16,128]{3,2,1,0:T(8,128)(2,1)S(1)} async-done(((bf16[128,3,16,128]{3,2,1,0:T(8,128)(2,1)}), bf16[128,3,16,128]{3,2,1,0:T(8,128)(2,1)S(1)}, u32[]{:S(2)}, u32[]{:S(2)}) %all-to-all-start.1) | async-done | bytes 1572896 | tf_op jit(solution)/shard_map/all_to_all | solution.py:297
  252.2 1.7 combine_rows.1
  253.8 0.7 copy.28
  (34 shorter events, 1.8 us)
Async XLA Ops:
  7.2 173.7 %all-gather.3.cloned.1.call-start = ((), (), s32[]{:S(2)}) async-start(), calls=%async_computation.2 | async-start | bytes 11796480 | tf_op jit(solution)/shard_map/all_gather | solution.py:289
  79.9 0.7 copy-start.13
  79.9 0.8 copy-start.14
  79.9 0.9 copy-start.11
  79.9 1.0 copy-start.12
  79.9 1.0 copy-start.7
  176.7 4.2 %copy-start.6 = (bf16[1,32,768]{2,1,0:T(8,128)(2,1)S(1)}, bf16[1,32,768]{2,1,0:T(8,128)(2,1)}, u32[]{:S(2)}) copy-start(bf16[1,32,768]{2,1,0:T(8,128)(2,1)} %down_in.3) | copy-start | bytes 147460
  176.7 4.2 %copy-start.10 = (bf16[1,32,768]{2,1,0:T(8,128)(2,1)S(1)}, bf16[1,32,768]{2,1,0:T(8,128)(2,1)}, u32[]{:S(2)}) copy-start(bf16[1,32,768]{2,1,0:T(8,128)(2,1)} %up_out.1) | copy-start | bytes 147460
  177.7 16.5 %copy-start = (bf16[384,2048]{1,0:T(8,128)(2,1)}, bf16[384,2048]{1,0:T(8,128)(2,1)S(1)}, u32[]{:S(2)}) copy-start(bf16[384,2048]{1,0:T(8,128)(2,1)S(1)} %get-tuple-element.28.rows_in) | copy-start | bytes 4718596
  180.9 0.9 copy-start.8
  181.8 0.9 copy-start.9
  194.2 1.6 copy-start.2
  194.2 1.6 copy-start.4
  195.8 56.4 %all-to-all-start.1 = ((bf16[128,3,16,128]{3,2,1,0:T(8,128)(2,1)}), bf16[128,3,16,128]{3,2,1,0:T(8,128)(2,1)S(1)}, u32[]{:S(2)}, u32[]{:S(2)}) async-start(bf16[128,3,16,128]{3,2,1,0:T(8,128)(2,1)} %bitcast.36), calls=%async_computation.1 | async-start | bytes 3145728 | tf_op jit(solution)/shard_map/all_to_all | solution.py:297
  210.6 1.4 copy-start.1
  212.0 1.1 copy-start.3
  213.0 1.1 copy-start.5
  215.1 20.8 %collective-permute-start.2 = (bf16[32,5632]{1,0:T(8,128)(2,1)S(1)}, bf16[32,5632]{1,0:T(8,128)(2,1)S(1)}, u32[]{:S(2)}, u32[]{:S(2)}) collective-permute-start(bf16[32,5632]{1,0:T(8,128)(2,1)S(1)} %adapter_grads.1), channel_id=1, source_target_pairs={{0,384},{128,0},{256,128},{384,256},{1,385},{129,1},{257,129},{385... | collective-permute-start | bytes 1081352 | tf_op jit(solution)/shard_map/ppermute | solution.py:277
  218.5 17.4 %collective-permute-start.1 = (bf16[32,5632]{1,0:T(8,128)(2,1)S(1)}, bf16[32,5632]{1,0:T(8,128)(2,1)S(1)}, u32[]{:S(2)}, u32[]{:S(2)}) collective-permute-start(bf16[32,5632]{1,0:T(8,128)(2,1)S(1)} %adapter_grads.1), channel_id=1, source_target_pairs={{0,256},{128,384},{256,0},{384,128},{1,257},{129,385},{257,1},{385... | collective-permute-start | bytes 1081352 | tf_op jit(solution)/shard_map/ppermute | solution.py:277
  221.9 16.5 %collective-permute-start = (bf16[32,5632]{1,0:T(8,128)(2,1)S(1)}, bf16[32,5632]{1,0:T(8,128)(2,1)S(1)}, u32[]{:S(2)}, u32[]{:S(2)}) collective-permute-start(bf16[32,5632]{1,0:T(8,128)(2,1)S(1)} %adapter_grads.1), channel_id=1, source_target_pairs={{0,128},{128,256},{256,384},{384,0},{1,129},{129,257},{257,385},{3... | collective-permute-start | bytes 1081352 | tf_op jit(solution)/shard_map/ppermute | solution.py:277
Sparse Core Ops, SparseCore 0:
  80.1 100.7 all-gather.2

commit v3 on v2

--- a/solution.py
+++ b/solution.py
@@ -14,46 +14,53 @@
 
 VMEM = pl.BlockSpec(memory_space=pltpu.VMEM)
 SMEM = pl.BlockSpec(memory_space=pltpu.SMEM)
-ANY = pl.BlockSpec(memory_space=pl.ANY)
+HBM = pl.BlockSpec(memory_space=pltpu.HBM)
 
 
 def params(mib):
     return pltpu.CompilerParams(vmem_limit_bytes=mib * 1024 * 1024)
 
 
-def pack_kernel(gate, up, down, packed, sems):
-    copies = []
+def pack_kernel(gate, up, packed, staged, sems):
+    moves = []
     row = 0
-    for ref in (gate, up, down):
+    for ref in (gate, up):
         rows, cols = ref.shape[1:]
         for c in range(cols // COLS):
-            copies.append(
-                pltpu.make_async_copy(
-                    ref.at[0, :, pl.ds(c * COLS, COLS)],
-                    packed.at[pl.ds(row, rows), :],
-                    sems.at[len(copies)],
+            place = pl.ds(row, rows)
+            i = len(moves)
+            moves.append(
+                (
+                    pltpu.make_async_copy(ref.at[0, :, pl.ds(c * COLS, COLS)], staged.at[place, :], sems.at[0, i]),
+                    pltpu.make_async_copy(staged.at[place, :], packed.at[place, :], sems.at[1, i]),
                 )
             )
             row += rows
-    for copy in copies:
-        copy.start()
-    for copy in copies:
-        copy.wait()
-
-
-def pack_weights(w_gate, w_up, w_down):
-    size = w_gate.size + w_up.size + w_down.size
-    blocks = (w_gate.shape[2] + w_up.shape[2] + w_down.shape[2]) // COLS
+    for load, _ in moves:
+        load.start()
+    for load, store in moves:
+        load.wait()
+        store.start()
+    for _, store in moves:
+        store.wait()
+
+
+def pack_weights(w_gate, w_up):
+    size = w_gate.size + w_up.size
+    blocks = (w_gate.shape[2] + w_up.shape[2]) // COLS
     return pl.pallas_call(
         pack_kernel,
         out_shape=jax.ShapeDtypeStruct((size // COLS, COLS), BF16),
-        in_specs=[ANY] * 3,
-        out_specs=ANY,
-        scratch_shapes=[pltpu.SemaphoreType.DMA((blocks,))],
+        in_specs=[HBM] * 2,
+        out_specs=HBM,
+        scratch_shapes=[
+            pltpu.VMEM((size // COLS, COLS), BF16),
+            pltpu.SemaphoreType.DMA((2, blocks)),
+        ],
         compiler_params=params(56),
         cost_estimate=pl.CostEstimate(flops=0, bytes_accessed=4 * size, transcendentals=0),
         name="pack_weights",
-    )(w_gate, w_up, w_down)
+    )(w_gate, w_up)
 
 
 def place_kernel(routes, prob, limits, tokens, grads, send, slots, count, staged):
@@ -137,16 +144,21 @@
 
 
 def slot_kernel(
-    rows_in, rows_grad, packed, up_in, up_out, down_in, down_out,
+    mine, rows_in, rows_grad, packed, down_0, down_1, down_2, down_3,
+    up_in_far, up_out_far, down_in_far, down_out_far,
     slot_grad, hidden, grad_up, low_up, back_low, up_low,
-    gate, up, down, grad_gate, sems,
+    gate, up, down, grad_gate, up_in, up_out, down_in, down_out, sems,
 ):
     width, inner = gate.shape
     shards = packed.shape[0]
     part = width // shards
     chunks = inner // COLS
     steps = []
+    small = []
     number = 0
+    for source, target in ((up_in_far, up_in), (down_out_far, down_out), (up_out_far, up_out), (down_in_far, down_in)):
+        small.append(pltpu.make_async_copy(source, target, sems.at[number]))
+        number += 1
     for c in range(chunks):
         cols = pl.ds(c * COLS, COLS)
         moves = []
@@ -155,23 +167,23 @@
                 moves.append(
                     (packed.at[s, pl.ds(base + c * part, part), :], ref.at[pl.ds(s * part, part), cols])
                 )
-        for s in range(shards):
-            for m in range(part // COLS):
-                row = 2 * chunks * part + m * inner + c * COLS
-                moves.append(
-                    (packed.at[s, pl.ds(row, COLS), :], down.at[cols, pl.ds(s * part + m * COLS, COLS)])
-                )
+        for s, ref in enumerate((down_0, down_1, down_2, down_3)):
+            owner = lax.rem(mine[0] + (shards - s), shards)
+            place = pl.multiple_of(owner * part, part)
+            moves.append((ref.at[0, cols, :], down.at[cols, pl.ds(place, part)]))
         copies = []
         for source, target in moves:
             copies.append(pltpu.make_async_copy(source, target, sems.at[number]))
             number += 1
         steps.append(copies)
-    for copies in steps:
+    for copies in [small] + steps:
         for copy in copies:
             copy.start()
 
     x = rows_in
     g = rows_grad
+    for copy in small:
+        copy.wait()
     low_up[...] = dot(x[...], up_in[0], 1, 1).astype(BF16)
     back_low[...] = dot(g[...], down_out[0], 1, 1).astype(BF16)
     for c in range(chunks):
@@ -216,7 +228,7 @@
             at += COLS
 
 
-def expert_slots(rows_in, rows_grad, packed, up_in, up_out, down_in, down_out):
+def expert_slots(mine, rows_in, rows_grad, packed, downs, up_in, up_out, down_in, down_out):
     rows, width = rows_in.shape
     rank, inner = up_out.shape[1:]
     shards = packed.shape[0]
@@ -231,23 +243,27 @@
             jax.ShapeDtypeStruct((rows, rank), BF16),
             jax.ShapeDtypeStruct((rows, rank), BF16),
         ),
-        in_specs=[VMEM, VMEM, ANY] + [VMEM] * 4,
+        in_specs=[SMEM, VMEM, VMEM] + [HBM] * 9,
         out_specs=(VMEM,) * 6,
         scratch_shapes=[
             pltpu.VMEM((width, inner), BF16),
             pltpu.VMEM((width, inner), BF16),
             pltpu.VMEM((inner, width), BF16),
             pltpu.VMEM((rows, inner), BF16),
-            pltpu.SemaphoreType.DMA((shards * (2 + part // COLS) * (inner // COLS),)),
+            pltpu.VMEM((1, rank, width), BF16),
+            pltpu.VMEM((1, rank, inner), BF16),
+            pltpu.VMEM((1, rank, inner), BF16),
+            pltpu.VMEM((1, rank, width), BF16),
+            pltpu.SemaphoreType.DMA((4 + 3 * shards * (inner // COLS),)),
         ],
-        compiler_params=params(44),
+        compiler_params=params(54),
         cost_estimate=pl.CostEstimate(
             flops=10 * rows * width * inner,
             bytes_accessed=6 * width * inner + 6 * rows * width,
             transcendentals=rows * inner,
         ),
         name="expert_slots",
-    )(rows_in, rows_grad, packed, up_in, up_out, down_in, down_out)
+    )(mine, rows_in, rows_grad, packed, *downs, up_in, up_out, down_in, down_out)
 
 
 def adapter_grads(rows_in, rows_grad, hidden, grad_up, low_up, back_low, up_low, down_in):
@@ -269,12 +285,18 @@
     )(rows_in, rows_grad, hidden, grad_up, low_up, back_low, up_low, down_in)
 
 
+def messages(own, axis):
+    count = lax.axis_size(axis)
+    return [
+        lax.ppermute(own, axis, [(i, (i + shift) % count) for i in range(count)])
+        for shift in range(1, count)
+    ]
+
+
 def replica_sum(own, axis):
-    count = lax.axis_size(axis)
     total = own.astype(F32)
-    for shift in range(1, count):
-        pairs = [(i, (i + shift) % count) for i in range(count)]
-        total += lax.ppermute(own, axis, pairs).astype(F32)
+    for other in messages(own, axis):
+        total += other.astype(F32)
     return total
 
 
@@ -286,13 +308,15 @@
     inner = up_out.shape[2]
     experts = limits.shape[0]
     slot_rows = experts * CAP
-    packed = lax.all_gather(pack_weights(w_gate, w_up, w_down), "rep")
+    packed = lax.all_gather(pack_weights(w_gate, w_up), "rep")
+    downs = [w_down] + messages(w_down, "rep")
     send, slots = place_rows(routes, gate_prob, limits, tokens, out_grad)
     send = send.reshape(experts, 2 * CAP, width // LANES, LANES)
     recv = lax.all_to_all(send, ("grp", "exp"), split_axis=0, concat_axis=0, tiled=True)
     rows_in = recv[:, :CAP].reshape(slot_rows, width)
     rows_grad = recv[:, CAP:].reshape(slot_rows, width)
-    slot_grad, *kept = expert_slots(rows_in, rows_grad, packed, up_in, up_out, down_in, down_out)
+    mine = lax.axis_index("rep").astype(jnp.int32).reshape(1)
+    slot_grad, *kept = expert_slots(mine, rows_in, rows_grad, packed, downs, up_in, up_out, down_in, down_out)
     adapters = replica_sum(adapter_grads(rows_in, rows_grad, *kept, down_in), "rep")
     back = lax.all_to_all(
         slot_grad.reshape(experts, CAP, width // LANES, LANES),

time: 263 us -> 203 us (0.77)
  blocking collectives: 91 us -> 0 us
  waiting for transfers between devices: 27.8 us -> 96.9 us
  Pallas kernels: 91 us -> 24.4 us
  starting transfers between devices: 25.5 us -> 52.3 us
    all_to_all x1 -> x0, blocking collectives: 91 us -> none  [on_device(): lax.all_to_all(send, ('grp', 'exp'), split_axis=0, concat_axis=0, tiled=T...]
    pallas_call x1, Pallas kernels: 72.6 us -> 2.2 us  [pack_weights(): pl.pallas_call(pack_kernel, out_shape=jax.ShapeDtypeStruct((size // COLS,...]
    all_to_all x0 -> x1, waiting for transfers between devices: none -> 64.5 us  [on_device(): lax.all_to_all(send, ('grp', 'exp'), split_axis=0, concat_axis=0, tiled=T...]
    all_to_all x0 -> x1, starting transfers between devices: none -> 17.8 us  [on_device(): lax.all_to_all(send, ('grp', 'exp'), split_axis=0, concat_axis=0, tiled=T...]
    ppermute x3 -> x6, starting transfers between devices: 10.7 us -> 19.5 us  [messages(): lax.ppermute(own, axis, [(i, (i + shift) % count) for i in range(count)])]
    all_gather x1, waiting for transfers between devices: 3.13 us -> 7.75 us  [on_device(): packed = lax.all_gather(pack_weights(w_gate, w_up), 'rep')]
    pallas_call x1, Pallas kernels: 11.5 us -> 14.2 us  [expert_slots(): pl.pallas_call(slot_kernel, out_shape=(jax.ShapeDtypeStruct((rows, width)...]
    unnamed x36 -> x32, local copies, waits for them, and re-layouts: 8.62 us -> 8.22 us
  transfers between devices with their start and end apart: 5 -> 9, of which waited for: 4 -> 6; matrix products, arithmetic and copies ran while one was open for 1% -> 3% of each run, Pallas kernels for 2% -> 3%
where the time goes in v3:
time: 203 us; the launch traced here: 201 us
  waiting for transfers between devices  96.9 us (48%)
  starting transfers between devices  52.3 us (26%)
  Pallas kernels  24.4 us (12%)
  between operations  14.3 us (7%)
  local copies, waits for them, and re-layouts  13 us (6%)
    all_to_all x1, waiting for transfers between devices, on_device(): lax.all_to_all(send, ('grp', 'exp'), split_axis=0, concat_axis=0, tiled=T...  64.5 us
    ppermute x6, starting transfers between devices, messages(): lax.ppermute(own, axis, [(i, (i + shift) % count) for i in range(count)])  19.5 us
    all_to_all x1, starting transfers between devices, on_device(): lax.all_to_all(send, ('grp', 'exp'), split_axis=0, concat_axis=0, tiled=T...  17.8 us
    all_to_all x1, starting transfers between devices, on_device(): lax.all_to_all(slot_grad.reshape(experts, CAP, width // LANES, LANES), ('...  14.9 us
    pallas_call x1, Pallas kernels, expert_slots(): pl.pallas_call(slot_kernel, out_shape=(jax.ShapeDtypeStruct((rows, width)...  14.2 us
    ppermute x6, waiting for transfers between devices, messages(): lax.ppermute(own, axis, [(i, (i + shift) % count) for i in range(count)])  12.6 us
    all_to_all x1, waiting for transfers between devices, on_device(): lax.all_to_all(slot_grad.reshape(experts, CAP, width // LANES, LANES), ('...  12 us
    unnamed x32, local copies, waits for them, and re-layouts  8.22 us
  transfers between devices with their start and end apart: 9, of which 6 were waited for; matrix products, arithmetic and copies ran while one was open for 3% of the time, Pallas kernels for 3%

profile of v3, /device:TPU:6, one launch (start us, length us, event | category | flops | bytes accessed | tf_op | source)
XLA Modules:
  0.0 200.9 jit_solution(6901260642639331200)
XLA Ops:
  7.2 2.2 %pack_weights.1 = bf16[3072,256]{1,0:T(8,128)(2,1)} custom-call(bf16[1,512,768]{2,1,0:T(8,128)(2,1)} %gate.1, bf16[1,512,768]{2,1,0:T(8,128)(2,1)} %up.1), custom_call_target="tpu_custom_call" | custom-call | bytes 3145728 | tf_op jit(solution)/shard_map/pack_weights/pallas_call | solution.py:51
  10.5 5.3 %place_rows.1 = (bf16[768,16,128]{2,1,0:T(8,128)(2,1)}, s32[32,8]{1,0:T(8,128)S(1)}) custom-call(s32[32,8]{1,0:T(8,128)S(1)} %copy.17.routes, f32[32,8]{1,0:T(8,128)S(1)} %copy.18.prob, s32[128]{0:T(128)S(1)} %copy-done.8, bf16[32,16,128]{2,1,0:T(8,128)(2,1)S(1)} %bitcast.32, bf16[32,16,128]{2,1,0:T(8,128)(2,1)S(1)} %bitcast.33), custom_call_target="tpu_custom_call" | custom-call | tf_op jit(solution)/shard_map/place_rows/pallas_call | solution.py:99
  15.8 17.8 %all-to-all-start = ((bf16[128,6,16,128]{3,2,1,0:T(8,128)(2,1)}), bf16[128,6,16,128]{3,2,1,0:T(8,128)(2,1)S(1)}, u32[]{:S(2)}, u32[]{:S(2)}) async-start(bf16[128,6,16,128]{3,2,1,0:T(8,128)(2,1)} %bitcast.1), calls=%async_computation | async-start | bytes 6291456 | tf_op jit(solution)/shard_map/all_to_all | solution.py:315
  33.6 2.4 %collective-permute-start = (bf16[1,768,512]{2,1,0:T(8,128)(2,1)}, bf16[1,768,512]{2,1,0:T(8,128)(2,1)}, u32[]{:S(2)}, u32[]{:S(2)}) collective-permute-start(bf16[1,768,512]{2,1,0:T(8,128)(2,1)} %down_0.1), channel_id=1, source_target_pairs={{0,128},{128,256},{256,384},{384,0},{1,129},{129,257},{257,385},{3... | collective-permute-start | bytes 2359304 | tf_op jit(solution)/shard_map/ppermute | solution.py:291
  36.0 4.3 %collective-permute-start.1 = (bf16[1,768,512]{2,1,0:T(8,128)(2,1)}, bf16[1,768,512]{2,1,0:T(8,128)(2,1)}, u32[]{:S(2)}, u32[]{:S(2)}) collective-permute-start(bf16[1,768,512]{2,1,0:T(8,128)(2,1)} %down_0.1), channel_id=1, source_target_pairs={{0,256},{128,384},{256,0},{384,128},{1,257},{129,385},{257,1},{385... | collective-permute-start | bytes 2359304 | tf_op jit(solution)/shard_map/ppermute | solution.py:291
  40.3 2.1 %collective-permute-start.2 = (bf16[1,768,512]{2,1,0:T(8,128)(2,1)}, bf16[1,768,512]{2,1,0:T(8,128)(2,1)}, u32[]{:S(2)}, u32[]{:S(2)}) collective-permute-start(bf16[1,768,512]{2,1,0:T(8,128)(2,1)} %down_0.1), channel_id=1, source_target_pairs={{0,384},{128,0},{256,128},{384,256},{1,385},{129,1},{257,129},{385... | collective-permute-start | bytes 2359304 | tf_op jit(solution)/shard_map/ppermute | solution.py:291
  42.4 64.5 %all-to-all-done = bf16[128,6,16,128]{3,2,1,0:T(8,128)(2,1)S(1)} async-done(((bf16[128,6,16,128]{3,2,1,0:T(8,128)(2,1)}), bf16[128,6,16,128]{3,2,1,0:T(8,128)(2,1)S(1)}, u32[]{:S(2)}, u32[]{:S(2)}) %all-to-all-start) | async-done | bytes 3145760 | tf_op jit(solution)/shard_map/all_to_all | solution.py:315
  107.5 2.7 %copy_bitcast_fusion = (bf16[384,2048]{1,0:T(8,128)(2,1)}, bf16[384,2048]{1,0:T(8,128)(2,1)}) fusion(bf16[48,8,16,128]{3,2,1,0:T(8,128)(2,1)S(1)} %bitcast.36, bf16[48,8,16,128]{3,2,1,0:T(8,128)(2,1)S(1)} %bitcast.37), kind=kLoop, calls=%fused_computation | loop fusion | bytes 6291456 | tf_op jit(solution)/shard_map/reshape | solution.py:317
  110.2 7.7 %all-gather.3.cloned.1.call-done = bf16[12288,256]{1,0:T(8,128)(2,1)} async-done(((bf16[3072,256]{1,0:T(8,128)(2,1)}), bf16[12288,256]{1,0:T(8,128)(2,1)}) %all-gather.3.cloned.1.call-update) | async-done | bytes 6291472 | tf_op jit(solution)/shard_map/all_gather | solution.py:311
  118.0 14.2 %expert_slots.1 = (bf16[384,2048]{1,0:T(8,128)(2,1)}, bf16[384,768]{1,0:T(8,128)(2,1)}, bf16[384,768]{1,0:T(8,128)(2,1)}, bf16[384,32]{1,0:T(8,128)(2,1)}, bf16[...) custom-call(s32[1]{0:T(128)} %bitcast.mine, bf16[384,2048]{1,0:T(8,128)(2,1)} %get-tuple-element.28.rows_in, ...), custom_call_target="tpu_custom_call" | custom-call | flops 6039797760 | bytes 14155776 | tf_op jit(solution)/shard_map/expert_slots/pallas_call | solution.py:236
  132.2 3.0 %copy.23 = bf16[48,8,16,128]{3,2,1,0:T(8,128)(2,1)} copy(bf16[48,8,16,128]{3,1,2,0:T(8,128)(2,1)} %bitcast.38) | data formatting | bytes 3145728
  135.2 14.9 %all-to-all-start.1 = ((bf16[128,3,16,128]{3,2,1,0:T(8,128)(2,1)}), bf16[128,3,16,128]{3,2,1,0:T(8,128)(2,1)S(1)}, u32[]{:S(2)}, u32[]{:S(2)}) async-start(bf16[128,3,16,128]{3,2,1,0:T(8,128)(2,1)} %bitcast.35), calls=%async_computation.1 | async-start | bytes 3145728 | tf_op jit(solution)/shard_map/all_to_all | solution.py:321
  150.2 1.4 copy-done.1
  151.6 1.1 copy-done.2
  152.7 1.1 copy-done.3
  153.7 1.0 adapter_grads.1
  154.7 3.4 %collective-permute-start.5 = (bf16[32,5632]{1,0:T(8,128)(2,1)S(1)}, bf16[32,5632]{1,0:T(8,128)(2,1)S(1)}, u32[]{:S(2)}, u32[]{:S(2)}) collective-permute-start(bf16[32,5632]{1,0:T(8,128)(2,1)S(1)} %adapter_grads.1), channel_id=1, source_target_pairs={{0,384},{128,0},{256,128},{384,256},{1,385},{129,1},{257,129},{385... | collective-permute-start | bytes 1081352 | tf_op jit(solution)/shard_map/ppermute | solution.py:291
  158.1 3.7 %collective-permute-start.4 = (bf16[32,5632]{1,0:T(8,128)(2,1)S(1)}, bf16[32,5632]{1,0:T(8,128)(2,1)S(1)}, u32[]{:S(2)}, u32[]{:S(2)}) collective-permute-start(bf16[32,5632]{1,0:T(8,128)(2,1)S(1)} %adapter_grads.1), channel_id=1, source_target_pairs={{0,256},{128,384},{256,0},{384,128},{1,257},{129,385},{257,1},{385... | collective-permute-start | bytes 1081352 | tf_op jit(solution)/shard_map/ppermute | solution.py:291
  161.8 3.7 %collective-permute-start.3 = (bf16[32,5632]{1,0:T(8,128)(2,1)S(1)}, bf16[32,5632]{1,0:T(8,128)(2,1)S(1)}, u32[]{:S(2)}, u32[]{:S(2)}) collective-permute-start(bf16[32,5632]{1,0:T(8,128)(2,1)S(1)} %adapter_grads.1), channel_id=1, source_target_pairs={{0,128},{128,256},{256,384},{384,0},{1,129},{129,257},{257,385},{3... | collective-permute-start | bytes 1081352 | tf_op jit(solution)/shard_map/ppermute | solution.py:291
  165.5 3.7 %collective-permute-done.5 = bf16[32,5632]{1,0:T(8,128)(2,1)S(1)} collective-permute-done((bf16[32,5632]{1,0:T(8,128)(2,1)S(1)}, bf16[32,5632]{1,0:T(8,128)(2,1)S(1)}, u32[]{:S(2)}, u32[]{:S(2)}) %collective-permute-start.5) | collective-permute-done | bytes 360480 | tf_op jit(solution)/shard_map/ppermute | solution.py:291
  169.1 6.3 %collective-permute-done.4 = bf16[32,5632]{1,0:T(8,128)(2,1)S(1)} collective-permute-done((bf16[32,5632]{1,0:T(8,128)(2,1)S(1)}, bf16[32,5632]{1,0:T(8,128)(2,1)S(1)}, u32[]{:S(2)}, u32[]{:S(2)}) %collective-permute-start.4) | collective-permute-done | bytes 360480 | tf_op jit(solution)/shard_map/ppermute | solution.py:291
  175.5 2.5 %collective-permute-done.3 = bf16[32,5632]{1,0:T(8,128)(2,1)S(1)} collective-permute-done((bf16[32,5632]{1,0:T(8,128)(2,1)S(1)}, bf16[32,5632]{1,0:T(8,128)(2,1)S(1)}, u32[]{:S(2)}, u32[]{:S(2)}) %collective-permute-start.3) | collective-permute-done | bytes 360480 | tf_op jit(solution)/shard_map/ppermute | solution.py:291
  179.7 12.0 %all-to-all-done.1 = bf16[128,3,16,128]{3,2,1,0:T(8,128)(2,1)S(1)} async-done(((bf16[128,3,16,128]{3,2,1,0:T(8,128)(2,1)}), bf16[128,3,16,128]{3,2,1,0:T(8,128)(2,1)S(1)}, u32[]{:S(2)}, u32[]{:S(2)}) %all-to-all-start.1) | async-done | bytes 1572896 | tf_op jit(solution)/shard_map/all_to_all | solution.py:321
  191.7 1.7 combine_rows.1
  (37 shorter events, 4.0 us)
Async XLA Ops:
  7.2 110.8 %all-gather.3.cloned.1.call-start = ((), (), s32[]{:S(2)}) async-start(), calls=%async_computation.2 | async-start | bytes 7864320 | tf_op jit(solution)/shard_map/all_gather | solution.py:311
  9.4 0.7 copy-start.11
  9.4 0.8 copy-start.12
  9.4 0.9 copy-start.9
  9.5 1.0 copy-start.10
  9.5 1.0 copy-start.8
  15.8 91.2 %all-to-all-start = ((bf16[128,6,16,128]{3,2,1,0:T(8,128)(2,1)}), bf16[128,6,16,128]{3,2,1,0:T(8,128)(2,1)S(1)}, u32[]{:S(2)}, u32[]{:S(2)}) async-start(bf16[128,6,16,128]{3,2,1,0:T(8,128)(2,1)} %bitcast.1), calls=%async_computation | async-start | bytes 6291456 | tf_op jit(solution)/shard_map/all_to_all | solution.py:315
  33.6 76.6 %collective-permute-start = (bf16[1,768,512]{2,1,0:T(8,128)(2,1)}, bf16[1,768,512]{2,1,0:T(8,128)(2,1)}, u32[]{:S(2)}, u32[]{:S(2)}) collective-permute-start(bf16[1,768,512]{2,1,0:T(8,128)(2,1)} %down_0.1), channel_id=1, source_target_pairs={{0,128},{128,256},{256,384},{384,0},{1,129},{129,257},{257,385},{3... | collective-permute-start | bytes 2359304 | tf_op jit(solution)/shard_map/ppermute | solution.py:291
  36.0 74.2 %collective-permute-start.1 = (bf16[1,768,512]{2,1,0:T(8,128)(2,1)}, bf16[1,768,512]{2,1,0:T(8,128)(2,1)}, u32[]{:S(2)}, u32[]{:S(2)}) collective-permute-start(bf16[1,768,512]{2,1,0:T(8,128)(2,1)} %down_0.1), channel_id=1, source_target_pairs={{0,256},{128,384},{256,0},{384,128},{1,257},{129,385},{257,1},{385... | collective-permute-start | bytes 2359304 | tf_op jit(solution)/shard_map/ppermute | solution.py:291
  40.3 69.9 %collective-permute-start.2 = (bf16[1,768,512]{2,1,0:T(8,128)(2,1)}, bf16[1,768,512]{2,1,0:T(8,128)(2,1)}, u32[]{:S(2)}, u32[]{:S(2)}) collective-permute-start(bf16[1,768,512]{2,1,0:T(8,128)(2,1)} %down_0.1), channel_id=1, source_target_pairs={{0,384},{128,0},{256,128},{384,256},{1,385},{129,1},{257,129},{385... | collective-permute-start | bytes 2359304 | tf_op jit(solution)/shard_map/ppermute | solution.py:291
  135.2 14.9 %copy-start = (bf16[384,2048]{1,0:T(8,128)(2,1)S(1)}, bf16[384,2048]{1,0:T(8,128)(2,1)}, u32[]{:S(2)}) copy-start(bf16[384,2048]{1,0:T(8,128)(2,1)} %get-tuple-element.27.rows_grad) | copy-start | bytes 4718596
  135.2 14.9 %copy-start.4 = (bf16[384,32]{1,0:T(8,128)(2,1)S(1)}, bf16[384,32]{1,0:T(8,128)(2,1)}, u32[]{:S(2)}) copy-start(bf16[384,32]{1,0:T(8,128)(2,1)} %get-tuple-element.18.low_up) | copy-start | bytes 73732
  135.2 14.9 %copy-start.5 = (bf16[384,32]{1,0:T(8,128)(2,1)S(1)}, bf16[384,32]{1,0:T(8,128)(2,1)}, u32[]{:S(2)}) copy-start(bf16[384,32]{1,0:T(8,128)(2,1)} %get-tuple-element.19.back_low) | copy-start | bytes 73732
  135.2 14.9 %copy-start.6 = (bf16[384,32]{1,0:T(8,128)(2,1)S(1)}, bf16[384,32]{1,0:T(8,128)(2,1)}, u32[]{:S(2)}) copy-start(bf16[384,32]{1,0:T(8,128)(2,1)} %get-tuple-element.20.up_low) | copy-start | bytes 73732
  135.2 15.0 %copy-start.7 = (bf16[1,32,768]{2,1,0:T(8,128)(2,1)S(1)}, bf16[1,32,768]{2,1,0:T(8,128)(2,1)}, u32[]{:S(2)}) copy-start(bf16[1,32,768]{2,1,0:T(8,128)(2,1)} %down_in.1) | copy-start | bytes 147460
  135.2 56.5 %all-to-all-start.1 = ((bf16[128,3,16,128]{3,2,1,0:T(8,128)(2,1)}), bf16[128,3,16,128]{3,2,1,0:T(8,128)(2,1)S(1)}, u32[]{:S(2)}, u32[]{:S(2)}) async-start(bf16[128,3,16,128]{3,2,1,0:T(8,128)(2,1)} %bitcast.35), calls=%async_computation.1 | async-start | bytes 3145728 | tf_op jit(solution)/shard_map/all_to_all | solution.py:321
  150.2 1.4 copy-start.1
  151.6 1.1 copy-start.2
  152.7 1.1 copy-start.3
  154.7 14.4 %collective-permute-start.5 = (bf16[32,5632]{1,0:T(8,128)(2,1)S(1)}, bf16[32,5632]{1,0:T(8,128)(2,1)S(1)}, u32[]{:S(2)}, u32[]{:S(2)}) collective-permute-start(bf16[32,5632]{1,0:T(8,128)(2,1)S(1)} %adapter_grads.1), channel_id=1, source_target_pairs={{0,384},{128,0},{256,128},{384,256},{1,385},{129,1},{257,129},{385... | collective-permute-start | bytes 1081352 | tf_op jit(solution)/shard_map/ppermute | solution.py:291
  158.1 17.4 %collective-permute-start.4 = (bf16[32,5632]{1,0:T(8,128)(2,1)S(1)}, bf16[32,5632]{1,0:T(8,128)(2,1)S(1)}, u32[]{:S(2)}, u32[]{:S(2)}) collective-permute-start(bf16[32,5632]{1,0:T(8,128)(2,1)S(1)} %adapter_grads.1), channel_id=1, source_target_pairs={{0,256},{128,384},{256,0},{384,128},{1,257},{129,385},{257,1},{385... | collective-permute-start | bytes 1081352 | tf_op jit(solution)/shard_map/ppermute | solution.py:291
  161.8 16.2 %collective-permute-start.3 = (bf16[32,5632]{1,0:T(8,128)(2,1)S(1)}, bf16[32,5632]{1,0:T(8,128)(2,1)S(1)}, u32[]{:S(2)}, u32[]{:S(2)}) collective-permute-start(bf16[32,5632]{1,0:T(8,128)(2,1)S(1)} %adapter_grads.1), channel_id=1, source_target_pairs={{0,128},{128,256},{256,384},{384,0},{1,129},{129,257},{257,385},{3... | collective-permute-start | bytes 1081352 | tf_op jit(solution)/shard_map/ppermute | solution.py:291
Sparse Core Ops, SparseCore 0:
  10.1 107.8 all-gather.2

commit v4 on v2

--- a/solution.py
+++ b/solution.py
@@ -14,31 +14,35 @@
 
 VMEM = pl.BlockSpec(memory_space=pltpu.VMEM)
 SMEM = pl.BlockSpec(memory_space=pltpu.SMEM)
-ANY = pl.BlockSpec(memory_space=pl.ANY)
+HBM = pl.BlockSpec(memory_space=pltpu.HBM)
 
 
 def params(mib):
     return pltpu.CompilerParams(vmem_limit_bytes=mib * 1024 * 1024)
 
 
-def pack_kernel(gate, up, down, packed, sems):
-    copies = []
+def pack_kernel(gate, up, down, packed, staged, sems):
+    moves = []
     row = 0
     for ref in (gate, up, down):
         rows, cols = ref.shape[1:]
         for c in range(cols // COLS):
-            copies.append(
-                pltpu.make_async_copy(
-                    ref.at[0, :, pl.ds(c * COLS, COLS)],
-                    packed.at[pl.ds(row, rows), :],
-                    sems.at[len(copies)],
+            place = pl.ds(row, rows)
+            i = len(moves)
+            moves.append(
+                (
+                    pltpu.make_async_copy(ref.at[0, :, pl.ds(c * COLS, COLS)], staged.at[place, :], sems.at[0, i]),
+                    pltpu.make_async_copy(staged.at[place, :], packed.at[place, :], sems.at[1, i]),
                 )
             )
             row += rows
-    for copy in copies:
-        copy.start()
-    for copy in copies:
-        copy.wait()
+    for load, _ in moves:
+        load.start()
+    for load, store in moves:
+        load.wait()
+        store.start()
+    for _, store in moves:
+        store.wait()
 
 
 def pack_weights(w_gate, w_up, w_down):
@@ -47,9 +51,12 @@
     return pl.pallas_call(
         pack_kernel,
         out_shape=jax.ShapeDtypeStruct((size // COLS, COLS), BF16),
-        in_specs=[ANY] * 3,
-        out_specs=ANY,
-        scratch_shapes=[pltpu.SemaphoreType.DMA((blocks,))],
+        in_specs=[HBM] * 3,
+        out_specs=HBM,
+        scratch_shapes=[
+            pltpu.VMEM((size // COLS, COLS), BF16),
+            pltpu.SemaphoreType.DMA((2, blocks)),
+        ],
         compiler_params=params(56),
         cost_estimate=pl.CostEstimate(flops=0, bytes_accessed=4 * size, transcendentals=0),
         name="pack_weights",
@@ -136,12 +143,39 @@
     )
 
 
+def low_kernel(rows_in, rows_grad, up_in, down_out, low_up, back_low, up_in_near):
+    low_up[...] = dot(rows_in[...], up_in[0], 1, 1).astype(BF16)
+    back_low[...] = dot(rows_grad[...], down_out[0], 1, 1).astype(BF16)
+    up_in_near[...] = up_in[0]
+
+
+def low_products(rows_in, rows_grad, up_in, down_out):
+    rows, width = rows_in.shape
+    rank = up_in.shape[1]
+    return pl.pallas_call(
+        low_kernel,
+        out_shape=(
+            jax.ShapeDtypeStruct((rows, rank), BF16),
+            jax.ShapeDtypeStruct((rows, rank), BF16),
+            jax.ShapeDtypeStruct((rank, width), BF16),
+        ),
+        in_specs=[VMEM] * 4,
+        out_specs=(VMEM,) * 3,
+        compiler_params=params(16),
+        cost_estimate=pl.CostEstimate(
+            flops=4 * rows * rank * width, bytes_accessed=4 * rows * width, transcendentals=0
+        ),
+        name="low_products",
+    )(rows_in, rows_grad, up_in, down_out)
+
+
 def slot_kernel(
-    rows_in, rows_grad, packed, up_in, up_out, down_in, down_out,
-    slot_grad, hidden, grad_up, low_up, back_low, up_low,
-    gate, up, down, grad_gate, sems,
+    rows_in, rows_grad, packed, low_up, back_low, up_in, up_out, down_in,
+    slot_grad, hidden, grad_up, up_low,
+    gate_up, down, grads, sems,
 ):
-    width, inner = gate.shape
+    width = gate_up.shape[0]
+    inner = hidden.shape[1]
     shards = packed.shape[0]
     part = width // shards
     chunks = inner // COLS
@@ -151,9 +185,12 @@
         cols = pl.ds(c * COLS, COLS)
         moves = []
         for s in range(shards):
-            for base, ref in ((0, gate), (chunks * part, up)):
+            for i in range(2):
                 moves.append(
-                    (packed.at[s, pl.ds(base + c * part, part), :], ref.at[pl.ds(s * part, part), cols])
+                    (
+                        packed.at[s, pl.ds((i * chunks + c) * part, part), :],
+                        gate_up.at[pl.ds(s * part, part), pl.ds(i * inner + c * COLS, COLS)],
+                    )
                 )
         for s in range(shards):
             for m in range(part // COLS):
@@ -172,31 +209,30 @@
 
     x = rows_in
     g = rows_grad
-    low_up[...] = dot(x[...], up_in[0], 1, 1).astype(BF16)
-    back_low[...] = dot(g[...], down_out[0], 1, 1).astype(BF16)
     for c in range(chunks):
         cols = pl.ds(c * COLS, COLS)
+        later = pl.ds(inner + c * COLS, COLS)
         for copy in steps[c]:
             copy.wait()
-        gate_pre = dot(x[...], gate[:, cols], 1, 0)
-        up_sum = dot(x[...], up[:, cols], 1, 0) + SCALE * dot(low_up[...], up_out[0, :, cols], 1, 0)
+        gate_pre = dot(x[...], gate_up[:, cols], 1, 0)
+        up_sum = dot(x[...], gate_up[:, later], 1, 0) + SCALE * dot(low_up[...], up_out[0, :, cols], 1, 0)
         grad_hidden = dot(g[...], down[cols, :], 1, 1) + SCALE * dot(
             back_low[...], down_in[0, :, cols], 1, 0
         )
         sig = jax.nn.sigmoid(gate_pre)
         active = gate_pre * sig
+        up_grad = (grad_hidden * active).astype(BF16)
         hidden[:, cols] = (active * up_sum).astype(BF16)
-        grad_gate[:, cols] = (
+        grads[:, cols] = (
             grad_hidden * up_sum * sig * (1.0 + gate_pre * (1.0 - sig))
         ).astype(BF16)
-        grad_up[:, cols] = (grad_hidden * active).astype(BF16)
+        grads[:, later] = up_grad
+        grad_up[:, cols] = up_grad
     up_low[...] = dot(grad_up[...], up_out[0], 1, 1).astype(BF16)
     for c in range(width // COLS):
         cols = pl.ds(c * COLS, COLS)
         slot_grad[:, cols] = (
-            dot(grad_gate[...], gate[cols, :], 1, 1)
-            + dot(grad_up[...], up[cols, :], 1, 1)
-            + SCALE * dot(up_low[...], up_in[0, :, cols], 1, 0)
+            dot(grads[...], gate_up[cols, :], 1, 1) + SCALE * dot(up_low[...], up_in[:, cols], 1, 0)
         ).astype(BF16)
 
 
@@ -216,7 +252,7 @@
             at += COLS
 
 
-def expert_slots(rows_in, rows_grad, packed, up_in, up_out, down_in, down_out):
+def expert_slots(rows_in, rows_grad, packed, low_up, back_low, up_in, up_out, down_in):
     rows, width = rows_in.shape
     rank, inner = up_out.shape[1:]
     shards = packed.shape[0]
@@ -228,26 +264,23 @@
             jax.ShapeDtypeStruct((rows, inner), BF16),
             jax.ShapeDtypeStruct((rows, inner), BF16),
             jax.ShapeDtypeStruct((rows, rank), BF16),
-            jax.ShapeDtypeStruct((rows, rank), BF16),
-            jax.ShapeDtypeStruct((rows, rank), BF16),
-        ),
-        in_specs=[VMEM, VMEM, ANY] + [VMEM] * 4,
-        out_specs=(VMEM,) * 6,
+        ),
+        in_specs=[VMEM, VMEM, HBM] + [VMEM] * 5,
+        out_specs=(VMEM,) * 4,
         scratch_shapes=[
-            pltpu.VMEM((width, inner), BF16),
-            pltpu.VMEM((width, inner), BF16),
+            pltpu.VMEM((width, 2 * inner), BF16),
             pltpu.VMEM((inner, width), BF16),
-            pltpu.VMEM((rows, inner), BF16),
+            pltpu.VMEM((rows, 2 * inner), BF16),
             pltpu.SemaphoreType.DMA((shards * (2 + part // COLS) * (inner // COLS),)),
         ],
-        compiler_params=params(44),
+        compiler_params=params(40),
         cost_estimate=pl.CostEstimate(
             flops=10 * rows * width * inner,
             bytes_accessed=6 * width * inner + 6 * rows * width,
             transcendentals=rows * inner,
         ),
         name="expert_slots",
-    )(rows_in, rows_grad, packed, up_in, up_out, down_in, down_out)
+    )(rows_in, rows_grad, packed, low_up, back_low, up_in, up_out, down_in)
 
 
 def adapter_grads(rows_in, rows_grad, hidden, grad_up, low_up, back_low, up_low, down_in):
@@ -292,8 +325,13 @@
     recv = lax.all_to_all(send, ("grp", "exp"), split_axis=0, concat_axis=0, tiled=True)
     rows_in = recv[:, :CAP].reshape(slot_rows, width)
     rows_grad = recv[:, CAP:].reshape(slot_rows, width)
-    slot_grad, *kept = expert_slots(rows_in, rows_grad, packed, up_in, up_out, down_in, down_out)
-    adapters = replica_sum(adapter_grads(rows_in, rows_grad, *kept, down_in), "rep")
+    low_up, back_low, up_in = low_products(rows_in, rows_grad, up_in, down_out)
+    slot_grad, hidden, grad_up, up_low = expert_slots(
+        rows_in, rows_grad, packed, low_up, back_low, up_in, up_out, down_in
+    )
+    adapters = replica_sum(
+        adapter_grads(rows_in, rows_grad, hidden, grad_up, low_up, back_low, up_low, down_in), "rep"
+    )
     back = lax.all_to_all(
         slot_grad.reshape(experts, CAP, width // LANES, LANES),
         ("grp", "exp"), split_axis=0, concat_axis=0, tiled=True,

time: 263 us -> 192 us (0.73)
  Pallas kernels: 91 us -> 22.1 us
    pallas_call x1, Pallas kernels: 72.6 us -> 2.53 us  [pack_weights(): pl.pallas_call(pack_kernel, out_shape=jax.ShapeDtypeStruct((size // COLS,...]
  transfers between devices with their start and end apart: 5 -> 5, of which waited for: 4 -> 4; matrix products, arithmetic and copies ran while one was open for 1% -> 2% of each run, Pallas kernels for 2% -> 3%
where the time goes in v4:
time: 192 us; the launch traced here: 191 us
  blocking collectives  91 us (47%)
  waiting for transfers between devices  27.3 us (14%)
  starting transfers between devices  26 us (14%)
  Pallas kernels  22.1 us (12%)
  between operations  14.3 us (7%)
  local copies, waits for them, and re-layouts  10 us (5%)
    all_to_all x1, blocking collectives, on_device(): lax.all_to_all(send, ('grp', 'exp'), split_axis=0, concat_axis=0, tiled=T...  91 us
    all_to_all x1, starting transfers between devices, on_device(): lax.all_to_all(slot_grad.reshape(experts, CAP, width // LANES, LANES), ('...  15.2 us
    all_to_all x1, waiting for transfers between devices, on_device(): lax.all_to_all(slot_grad.reshape(experts, CAP, width // LANES, LANES), ('...  13.2 us
    ppermute x3, waiting for transfers between devices, replica_sum(): total += lax.ppermute(own, axis, pairs).astype(F32)  12.5 us
    pallas_call x1, Pallas kernels, expert_slots(): pl.pallas_call(slot_kernel, out_shape=(jax.ShapeDtypeStruct((rows, width)...  11.1 us
    ppermute x3, starting transfers between devices, replica_sum(): total += lax.ppermute(own, axis, pairs).astype(F32)  10.7 us
    unnamed x36, local copies, waits for them, and re-layouts  6.93 us
    pallas_call x1, Pallas kernels, place_rows(): pl.pallas_call(place_kernel, out_shape=(jax.ShapeDtypeStruct((total, subs...  4.23 us
  transfers between devices with their start and end apart: 5, of which 4 were waited for; matrix products, arithmetic and copies ran while one was open for 2% of the time, Pallas kernels for 3%

profile of v4, /device:TPU:6, one launch (start us, length us, event | category | flops | bytes accessed | tf_op | source)
XLA Modules:
  0.0 190.8 jit_solution(7702067445342296249)
XLA Ops:
  7.2 2.5 %pack_weights.1 = bf16[4608,256]{1,0:T(8,128)(2,1)} custom-call(bf16[1,512,768]{2,1,0:T(8,128)(2,1)} %gate.1, bf16[1,512,768]{2,1,0:T(8,128)(2,1)} %up.1, bf16[1,768,512]{2,1,0:T(8,128)(2,1)} %down.1), custom_call_target="tpu_custom_call" | custom-call | bytes 4718592 | tf_op jit(solution)/shard_map/pack_weights/pallas_call | solution.py:51
  10.8 4.2 %place_rows.1 = (bf16[768,16,128]{2,1,0:T(8,128)(2,1)S(1)}, s32[32,8]{1,0:T(8,128)S(1)}) custom-call(s32[32,8]{1,0:T(8,128)S(1)} %copy.17.routes, f32[32,8]{1,0:T(8,128)S(1)} %copy.18.prob, s32[128]{0:T(128)S(1)} %copy-done.7, bf16[32,16,128]{2,1,0:T(8,128)(2,1)S(1)} %bitcast.32, bf16[32,16,128]{2,1,0:T(8,128)(2,1)S(1)} %bitcast.33), custom_call_target="tpu_custom_call" | custom-call | tf_op jit(solution)/shard_map/place_rows/pallas_call | solution.py:99
  15.0 91.0 %all_to_all.10 = bf16[128,6,16,128]{3,2,1,0:T(8,128)(2,1)S(1)} all-to-all(bf16[128,6,16,128]{3,2,1,0:T(8,128)(2,1)S(1)} %bitcast.30), channel_id=1, replica_groups=mesh['rep'=4,'grp'=8,'exp'=16] {'grp','exp'}, dimensions={0} | all-to-all | bytes 6291456 | tf_op jit(solution)/shard_map/all_to_all | solution.py:325
  106.6 1.0 copy_bitcast_fusion
  107.6 1.0 low_products.1
  108.6 0.6 copy-done.8
  109.3 1.6 all-gather.3.cloned.1.call-done
  110.9 0.9 copy-done.9
  111.8 11.1 %expert_slots.1 = (bf16[384,2048]{1,0:T(8,128)(2,1)S(1)}, bf16[384,768]{1,0:T(8,128)(2,1)S(1)}, bf16[384,768]{1,0:T(8,128)(2,1)S(1)}, bf16[384,32]{1,0:T(8,128)(2,1)S(1)}) custom-call(bf16[384,2048]{1,0:T(8,128)(2,1)S(1)} %get-tuple-element.30.rows_in, bf16[384,2048]{1,0:T(8,128)(2,1)S(1)} %get-tuple-element.29.rows_grad, bf16[4,4608,256]{2,1,0:T(8,128)(2,1)} %bitcast.41, ...), custom_call_target="tpu_custom_call" | custom-call | flops 6039797760 | bytes 14155776 | tf_op jit(solution)/shard_map/expert_slots/pallas_call | solution.py:260
  123.0 1.6 copy.23
  124.5 15.2 %all-to-all-start.1 = ((bf16[128,3,16,128]{3,2,1,0:T(8,128)(2,1)}), bf16[128,3,16,128]{3,2,1,0:T(8,128)(2,1)}, u32[]{:S(2)}, u32[]{:S(2)}) async-start(bf16[128,3,16,128]{3,2,1,0:T(8,128)(2,1)} %bitcast.35), calls=%async_computation.1 | async-start | bytes 3145728 | tf_op jit(solution)/shard_map/all_to_all | solution.py:335
  139.8 1.1 copy-done.1
  140.8 1.1 copy-done.3
  141.9 1.0 adapter_grads.1
  142.9 3.4 %collective-permute-start.2 = (bf16[32,5632]{1,0:T(8,128)(2,1)S(1)}, bf16[32,5632]{1,0:T(8,128)(2,1)S(1)}, u32[]{:S(2)}, u32[]{:S(2)}) collective-permute-start(bf16[32,5632]{1,0:T(8,128)(2,1)S(1)} %adapter_grads.1), channel_id=1, source_target_pairs={{0,384},{128,0},{256,128},{384,256},{1,385},{129,1},{257,129},{385... | collective-permute-start | bytes 1081352 | tf_op jit(solution)/shard_map/ppermute | solution.py:310
  146.3 3.4 %collective-permute-start.1 = (bf16[32,5632]{1,0:T(8,128)(2,1)S(1)}, bf16[32,5632]{1,0:T(8,128)(2,1)S(1)}, u32[]{:S(2)}, u32[]{:S(2)}) collective-permute-start(bf16[32,5632]{1,0:T(8,128)(2,1)S(1)} %adapter_grads.1), channel_id=1, source_target_pairs={{0,256},{128,384},{256,0},{384,128},{1,257},{129,385},{257,1},{385... | collective-permute-start | bytes 1081352 | tf_op jit(solution)/shard_map/ppermute | solution.py:310
  149.6 4.0 %collective-permute-start = (bf16[32,5632]{1,0:T(8,128)(2,1)S(1)}, bf16[32,5632]{1,0:T(8,128)(2,1)S(1)}, u32[]{:S(2)}, u32[]{:S(2)}) collective-permute-start(bf16[32,5632]{1,0:T(8,128)(2,1)S(1)} %adapter_grads.1), channel_id=1, source_target_pairs={{0,128},{128,256},{256,384},{384,0},{1,129},{129,257},{257,385},{3... | collective-permute-start | bytes 1081352 | tf_op jit(solution)/shard_map/ppermute | solution.py:310
  153.6 10.0 %collective-permute-done.2 = bf16[32,5632]{1,0:T(8,128)(2,1)S(1)} collective-permute-done((bf16[32,5632]{1,0:T(8,128)(2,1)S(1)}, bf16[32,5632]{1,0:T(8,128)(2,1)S(1)}, u32[]{:S(2)}, u32[]{:S(2)}) %collective-permute-start.2) | collective-permute-done | bytes 360480 | tf_op jit(solution)/shard_map/ppermute | solution.py:310
  163.6 2.5 %collective-permute-done = bf16[32,5632]{1,0:T(8,128)(2,1)S(1)} collective-permute-done((bf16[32,5632]{1,0:T(8,128)(2,1)S(1)}, bf16[32,5632]{1,0:T(8,128)(2,1)S(1)}, u32[]{:S(2)}, u32[]{:S(2)}) %collective-permute-start) | collective-permute-done | bytes 360480 | tf_op jit(solution)/shard_map/ppermute | solution.py:310
  166.3 0.7 slice_bitcast_fusion.2
  167.0 0.8 slice_bitcast_fusion
  167.8 13.2 %all-to-all-done.1 = bf16[128,3,16,128]{3,2,1,0:T(8,128)(2,1)} async-done(((bf16[128,3,16,128]{3,2,1,0:T(8,128)(2,1)}), bf16[128,3,16,128]{3,2,1,0:T(8,128)(2,1)}, u32[]{:S(2)}, u32[]{:S(2)}) %all-to-all-start.1) | async-done | bytes 1572896 | tf_op jit(solution)/shard_map/all_to_all | solution.py:335
  181.0 2.3 %combine_rows.1 = bf16[32,16,128]{2,1,0:T(8,128)(2,1)S(1)} custom-call(s32[32,8]{1,0:T(8,128)S(1)} %get-tuple-element.14.slots, bf16[384,16,128]{2,1,0:T(8,128)(2,1)} %bitcast.2.back), custom_call_target="tpu_custom_call" | custom-call | tf_op jit(solution)/shard_map/combine_rows/pallas_call | solution.py:130
  183.3 0.7 copy.28
  (35 shorter events, 1.8 us)
Async XLA Ops:
  7.2 103.7 %all-gather.3.cloned.1.call-start = ((), (), s32[]{:S(2)}) async-start(), calls=%async_computation.2 | async-start | bytes 11796480 | tf_op jit(solution)/shard_map/all_gather | solution.py:322
  9.7 0.7 copy-start.13
  9.8 0.8 copy-start.14
  9.8 0.9 copy-start.11
  9.8 1.0 copy-start.12
  9.8 1.0 copy-start.7
  106.5 1.1 copy-start.4
  106.6 1.1 copy-start.5
  107.6 3.3 %copy-start.6 = (bf16[1,32,768]{2,1,0:T(8,128)(2,1)S(1)}, bf16[1,32,768]{2,1,0:T(8,128)(2,1)}, u32[]{:S(2)}) copy-start(bf16[1,32,768]{2,1,0:T(8,128)(2,1)} %down_in.3) | copy-start | bytes 147460
  107.6 3.3 %copy-start.10 = (bf16[1,32,768]{2,1,0:T(8,128)(2,1)S(1)}, bf16[1,32,768]{2,1,0:T(8,128)(2,1)}, u32[]{:S(2)}) copy-start(bf16[1,32,768]{2,1,0:T(8,128)(2,1)} %up_out.1) | copy-start | bytes 147460
  108.6 0.7 copy-start.8
  110.9 0.9 copy-start.9
  122.9 1.6 copy-start
  122.9 1.6 copy-start.2
  124.5 56.5 %all-to-all-start.1 = ((bf16[128,3,16,128]{3,2,1,0:T(8,128)(2,1)}), bf16[128,3,16,128]{3,2,1,0:T(8,128)(2,1)}, u32[]{:S(2)}, u32[]{:S(2)}) async-start(bf16[128,3,16,128]{3,2,1,0:T(8,128)(2,1)} %bitcast.35), calls=%async_computation.1 | async-start | bytes 3145728 | tf_op jit(solution)/shard_map/all_to_all | solution.py:335
  139.8 1.1 copy-start.1
  140.8 1.1 copy-start.3
  142.9 20.7 %collective-permute-start.2 = (bf16[32,5632]{1,0:T(8,128)(2,1)S(1)}, bf16[32,5632]{1,0:T(8,128)(2,1)S(1)}, u32[]{:S(2)}, u32[]{:S(2)}) collective-permute-start(bf16[32,5632]{1,0:T(8,128)(2,1)S(1)} %adapter_grads.1), channel_id=1, source_target_pairs={{0,384},{128,0},{256,128},{384,256},{1,385},{129,1},{257,129},{385... | collective-permute-start | bytes 1081352 | tf_op jit(solution)/shard_map/ppermute | solution.py:310
  146.3 17.3 %collective-permute-start.1 = (bf16[32,5632]{1,0:T(8,128)(2,1)S(1)}, bf16[32,5632]{1,0:T(8,128)(2,1)S(1)}, u32[]{:S(2)}, u32[]{:S(2)}) collective-permute-start(bf16[32,5632]{1,0:T(8,128)(2,1)S(1)} %adapter_grads.1), channel_id=1, source_target_pairs={{0,256},{128,384},{256,0},{384,128},{1,257},{129,385},{257,1},{385... | collective-permute-start | bytes 1081352 | tf_op jit(solution)/shard_map/ppermute | solution.py:310
  149.6 16.5 %collective-permute-start = (bf16[32,5632]{1,0:T(8,128)(2,1)S(1)}, bf16[32,5632]{1,0:T(8,128)(2,1)S(1)}, u32[]{:S(2)}, u32[]{:S(2)}) collective-permute-start(bf16[32,5632]{1,0:T(8,128)(2,1)S(1)} %adapter_grads.1), channel_id=1, source_target_pairs={{0,128},{128,256},{256,384},{384,0},{1,129},{129,257},{257,385},{3... | collective-permute-start | bytes 1081352 | tf_op jit(solution)/shard_map/ppermute | solution.py:310
Sparse Core Ops, SparseCore 0:
  10.1 100.7 all-gather.2

commit v5 on v4

--- a/solution.py
+++ b/solution.py
@@ -19,48 +19,6 @@
 
 def params(mib):
     return pltpu.CompilerParams(vmem_limit_bytes=mib * 1024 * 1024)
-
-
-def pack_kernel(gate, up, down, packed, staged, sems):
-    moves = []
-    row = 0
-    for ref in (gate, up, down):
-        rows, cols = ref.shape[1:]
-        for c in range(cols // COLS):
-            place = pl.ds(row, rows)
-            i = len(moves)
-            moves.append(
-                (
-                    pltpu.make_async_copy(ref.at[0, :, pl.ds(c * COLS, COLS)], staged.at[place, :], sems.at[0, i]),
-                    pltpu.make_async_copy(staged.at[place, :], packed.at[place, :], sems.at[1, i]),
-                )
-            )
-            row += rows
-    for load, _ in moves:
-        load.start()
-    for load, store in moves:
-        load.wait()
-        store.start()
-    for _, store in moves:
-        store.wait()
-
-
-def pack_weights(w_gate, w_up, w_down):
-    size = w_gate.size + w_up.size + w_down.size
-    blocks = (w_gate.shape[2] + w_up.shape[2] + w_down.shape[2]) // COLS
-    return pl.pallas_call(
-        pack_kernel,
-        out_shape=jax.ShapeDtypeStruct((size // COLS, COLS), BF16),
-        in_specs=[HBM] * 3,
-        out_specs=HBM,
-        scratch_shapes=[
-            pltpu.VMEM((size // COLS, COLS), BF16),
-            pltpu.SemaphoreType.DMA((2, blocks)),
-        ],
-        compiler_params=params(56),
-        cost_estimate=pl.CostEstimate(flops=0, bytes_accessed=4 * size, transcendentals=0),
-        name="pack_weights",
-    )(w_gate, w_up, w_down)
 
 
 def place_kernel(routes, prob, limits, tokens, grads, send, slots, count, staged):
@@ -169,34 +127,50 @@
     )(rows_in, rows_grad, up_in, down_out)
 
 
+def pieces(mine, shards, own, left, right, top, bottom):
+    across = lax.rem(mine + 2, shards)
+    return (
+        (mine, 0, own),
+        (lax.rem(mine + shards - 1, shards), 0, left),
+        (lax.rem(mine + 1, shards), 0, right),
+        (across, 0, top),
+        (across, top.shape[1], bottom),
+    )
+
+
 def slot_kernel(
-    rows_in, rows_grad, packed, low_up, back_low, up_in, up_out, down_in,
-    slot_grad, hidden, grad_up, up_low,
-    gate_up, down, grads, sems,
+    rank, rows_in, rows_grad, low_up, back_low, up_in, up_out, down_in, *refs
 ):
+    gates, ups, downs = refs[0:5], refs[5:10], refs[10:15]
+    slot_grad, hidden, grad_up, up_low, gate_up, down, grads, sems = refs[15:]
     width = gate_up.shape[0]
     inner = hidden.shape[1]
-    shards = packed.shape[0]
-    part = width // shards
+    part = gates[0].shape[1]
+    shards = width // part
     chunks = inner // COLS
+    mine = rank[0]
     steps = []
     number = 0
     for c in range(chunks):
         cols = pl.ds(c * COLS, COLS)
         moves = []
-        for s in range(shards):
-            for i in range(2):
+        for i, refs_of in enumerate((gates, ups)):
+            for shard, first, ref in pieces(mine, shards, *refs_of):
+                rows = ref.shape[1]
+                place = pl.multiple_of(shard * part + first, rows)
+                moves.append(
+                    (ref.at[0, :, cols], gate_up.at[pl.ds(place, rows), pl.ds(i * inner + c * COLS, COLS)])
+                )
+        for shard, first, ref in pieces(mine, shards, *downs):
+            low = max(c * COLS, first)
+            high = min((c + 1) * COLS, first + ref.shape[1])
+            if low < high:
+                place = pl.multiple_of(shard * part, part)
                 moves.append(
                     (
-                        packed.at[s, pl.ds((i * chunks + c) * part, part), :],
-                        gate_up.at[pl.ds(s * part, part), pl.ds(i * inner + c * COLS, COLS)],
+                        ref.at[0, pl.ds(low - first, high - low), :],
+                        down.at[pl.ds(low, high - low), pl.ds(place, part)],
                     )
-                )
-        for s in range(shards):
-            for m in range(part // COLS):
-                row = 2 * chunks * part + m * inner + c * COLS
-                moves.append(
-                    (packed.at[s, pl.ds(row, COLS), :], down.at[cols, pl.ds(s * part + m * COLS, COLS)])
                 )
         copies = []
         for source, target in moves:
@@ -252,11 +226,10 @@
             at += COLS
 
 
-def expert_slots(rows_in, rows_grad, packed, low_up, back_low, up_in, up_out, down_in):
+def expert_slots(rows_in, rows_grad, gates, ups, downs, low_up, back_low, up_in, up_out, down_in):
     rows, width = rows_in.shape
     rank, inner = up_out.shape[1:]
-    shards = packed.shape[0]
-    part = width // shards
+    mine = lax.axis_index("rep").astype(jnp.int32).reshape(1)
     return pl.pallas_call(
         slot_kernel,
         out_shape=(
@@ -265,13 +238,13 @@
             jax.ShapeDtypeStruct((rows, inner), BF16),
             jax.ShapeDtypeStruct((rows, rank), BF16),
         ),
-        in_specs=[VMEM, VMEM, HBM] + [VMEM] * 5,
+        in_specs=[SMEM] + [VMEM] * 7 + [HBM] * 15,
         out_specs=(VMEM,) * 4,
         scratch_shapes=[
             pltpu.VMEM((width, 2 * inner), BF16),
             pltpu.VMEM((inner, width), BF16),
             pltpu.VMEM((rows, 2 * inner), BF16),
-            pltpu.SemaphoreType.DMA((shards * (2 + part // COLS) * (inner // COLS),)),
+            pltpu.SemaphoreType.DMA((15 * (inner // COLS),)),
         ],
         compiler_params=params(40),
         cost_estimate=pl.CostEstimate(
@@ -280,7 +253,7 @@
             transcendentals=rows * inner,
         ),
         name="expert_slots",
-    )(rows_in, rows_grad, packed, low_up, back_low, up_in, up_out, down_in)
+    )(mine, rows_in, rows_grad, low_up, back_low, up_in, up_out, down_in, *gates, *ups, *downs)
 
 
 def adapter_grads(rows_in, rows_grad, hidden, grad_up, low_up, back_low, up_low, down_in):
@@ -302,13 +275,23 @@
     )(rows_in, rows_grad, hidden, grad_up, low_up, back_low, up_low, down_in)
 
 
+def shifted(value, axis, shift):
+    count = lax.axis_size(axis)
+    return lax.ppermute(value, axis, [(i, (i + shift) % count) for i in range(count)])
+
+
 def replica_sum(own, axis):
-    count = lax.axis_size(axis)
     total = own.astype(F32)
-    for shift in range(1, count):
-        pairs = [(i, (i + shift) % count) for i in range(count)]
-        total += lax.ppermute(own, axis, pairs).astype(F32)
+    for shift in range(1, lax.axis_size(axis)):
+        total += shifted(own, axis, shift).astype(F32)
     return total
+
+
+def ring_gather(own, axis):
+    half = own.shape[1] // 2
+    left = shifted(own, axis, 1)
+    right = shifted(own, axis, -1)
+    return own, left, right, shifted(left[:, :half], axis, 1), shifted(right[:, half:], axis, -1)
 
 
 def on_device(
@@ -319,7 +302,7 @@
     inner = up_out.shape[2]
     experts = limits.shape[0]
     slot_rows = experts * CAP
-    packed = lax.all_gather(pack_weights(w_gate, w_up, w_down), "rep")
+    gates, ups, downs = (ring_gather(w, "rep") for w in (w_gate, w_up, w_down))
     send, slots = place_rows(routes, gate_prob, limits, tokens, out_grad)
     send = send.reshape(experts, 2 * CAP, width // LANES, LANES)
     recv = lax.all_to_all(send, ("grp", "exp"), split_axis=0, concat_axis=0, tiled=True)
@@ -327,7 +310,7 @@
     rows_grad = recv[:, CAP:].reshape(slot_rows, width)
     low_up, back_low, up_in = low_products(rows_in, rows_grad, up_in, down_out)
     slot_grad, hidden, grad_up, up_low = expert_slots(
-        rows_in, rows_grad, packed, low_up, back_low, up_in, up_out, down_in
+        rows_in, rows_grad, gates, ups, downs, low_up, back_low, up_in, up_out, down_in
     )
     adapters = replica_sum(
         adapter_grads(rows_in, rows_grad, hidden, grad_up, low_up, back_low, up_low, down_in), "rep"

time: 192 us -> 187 us (0.974)
  blocking collectives: 91 us -> 0 us
  starting transfers between devices: 26 us -> 78.4 us
  waiting for transfers between devices: 27.3 us -> 64.9 us
  between operations: 14.3 us -> 1.06 us
  local copies, waits for them, and re-layouts: 10 us -> 20.3 us
    all_to_all x1 -> x0, blocking collectives: 91 us -> none  [on_device(): lax.all_to_all(send, ('grp', 'exp'), split_axis=0, concat_axis=0, tiled=T...]
    ppermute x3 -> x15, starting transfers between devices: 10.7 us -> 49.2 us  [shifted(): lax.ppermute(value, axis, [(i, (i + shift) % count) for i in range(count)])]
    ppermute x3 -> x15, waiting for transfers between devices: 12.5 us -> 44.6 us  [shifted(): lax.ppermute(value, axis, [(i, (i + shift) % count) for i in range(count)])]
    all_to_all x0 -> x1, starting transfers between devices: none -> 18.3 us  [on_device(): lax.all_to_all(send, ('grp', 'exp'), split_axis=0, concat_axis=0, tiled=T...]
    all_to_all x0 -> x1, waiting for transfers between devices: none -> 7.13 us  [on_device(): lax.all_to_all(send, ('grp', 'exp'), split_axis=0, concat_axis=0, tiled=T...]
    slice x0 -> x6, local copies, waits for them, and re-layouts: none -> 5.68 us  [the longest x3 3.34 us: ring_gather(): right[:, half:]]
    all_to_all x1, starting transfers between devices: 15.2 us -> 11 us  [on_device(): lax.all_to_all(slot_grad.reshape(experts, CAP, width // LANES, LANES), ('...]
    unnamed x36 -> x50, local copies, waits for them, and re-layouts: 6.93 us -> 9.57 us
  transfers between devices with their start and end apart: 5 -> 17, of which waited for: 4 -> 10; matrix products, arithmetic and copies ran while one was open for 2% -> 6% of each run, Pallas kernels for 3% -> 1%
where the time goes in v5:
time: 187 us; the launch traced here: 186 us
  starting transfers between devices  78.4 us (42%)
  waiting for transfers between devices  64.9 us (35%)
  Pallas kernels  21.5 us (11%)
  local copies, waits for them, and re-layouts  20.3 us (11%)
    ppermute x15, starting transfers between devices, shifted(): lax.ppermute(value, axis, [(i, (i + shift) % count) for i in range(count)])  49.2 us
    ppermute x15, waiting for transfers between devices, shifted(): lax.ppermute(value, axis, [(i, (i + shift) % count) for i in range(count)])  44.6 us
    all_to_all x1, starting transfers between devices, on_device(): lax.all_to_all(send, ('grp', 'exp'), split_axis=0, concat_axis=0, tiled=T...  18.3 us
    all_to_all x1, waiting for transfers between devices, on_device(): lax.all_to_all(slot_grad.reshape(experts, CAP, width // LANES, LANES), ('...  13.2 us
    pallas_call x1, Pallas kernels, expert_slots(): pl.pallas_call(slot_kernel, out_shape=(jax.ShapeDtypeStruct((rows, width)...  12 us
    all_to_all x1, starting transfers between devices, on_device(): lax.all_to_all(slot_grad.reshape(experts, CAP, width // LANES, LANES), ('...  11 us
    unnamed x50, local copies, waits for them, and re-layouts  9.57 us
    all_to_all x1, waiting for transfers between devices, on_device(): lax.all_to_all(send, ('grp', 'exp'), split_axis=0, concat_axis=0, tiled=T...  7.13 us
  transfers between devices with their start and end apart: 17, of which 10 were waited for; matrix products, arithmetic and copies ran while one was open for 6% of the time, Pallas kernels for 1%

profile of v5, /device:TPU:6, one launch (start us, length us, event | category | flops | bytes accessed | tf_op | source)
XLA Modules:
  0.0 186.3 jit_solution(3485496954494600448)
XLA Ops:
  4.7 5.3 %place_rows.1 = (bf16[768,16,128]{2,1,0:T(8,128)(2,1)}, s32[32,8]{1,0:T(8,128)S(1)}) custom-call(s32[32,8]{1,0:T(8,128)S(1)} %copy.17.routes, f32[32,8]{1,0:T(8,128)S(1)} %copy.18.prob, s32[128]{0:T(128)S(1)} %copy-done.19, bf16[32,16,128]{2,1,0:T(8,128)(2,1)S(1)} %bitcast.31, bf16[32,16,128]{2,1,0:T(8,128)(2,1)S(1)} %bitcast.32), custom_call_target="tpu_custom_call" | custom-call | tf_op jit(solution)/shard_map/place_rows/pallas_call | solution.py:57
  9.9 18.3 %all-to-all-start = ((bf16[128,6,16,128]{3,2,1,0:T(8,128)(2,1)}), bf16[128,6,16,128]{3,2,1,0:T(8,128)(2,1)}, u32[]{:S(2)}, u32[]{:S(2)}) async-start(bf16[128,6,16,128]{3,2,1,0:T(8,128)(2,1)} %bitcast.1), calls=%async_computation | async-start | bytes 6291456 | tf_op jit(solution)/shard_map/all_to_all | solution.py:308
  30.6 3.5 %collective-permute-start.1 = (bf16[1,512,768]{2,1,0:T(8,128)(2,1)}, bf16[1,512,768]{2,1,0:T(8,128)(2,1)S(1)}, u32[]{:S(2)}, u32[]{:S(2)}) collective-permute-start(bf16[1,512,768]{2,1,0:T(8,128)(2,1)} %refs_0_.1), channel_id=1, source_target_pairs={{0,384},{128,0},{256,128},{384,256},{1,385},{129,1},{257,129},{385... | collective-permute-start | bytes 2359304 | tf_op jit(solution)/shard_map/ppermute | solution.py:280
  34.1 3.6 %collective-permute-start.4 = (bf16[1,512,768]{2,1,0:T(8,128)(2,1)}, bf16[1,512,768]{2,1,0:T(8,128)(2,1)S(1)}, u32[]{:S(2)}, u32[]{:S(2)}) collective-permute-start(bf16[1,512,768]{2,1,0:T(8,128)(2,1)} %refs_5_.1), channel_id=1, source_target_pairs={{0,128},{128,256},{256,384},{384,0},{1,129},{129,257},{257,385},{3... | collective-permute-start | bytes 2359304 | tf_op jit(solution)/shard_map/ppermute | solution.py:280
  40.0 4.8 %collective-permute-start.8 = (bf16[1,768,512]{2,1,0:T(8,128)(2,1)}, bf16[1,768,512]{2,1,0:T(8,128)(2,1)S(1)}, u32[]{:S(2)}, u32[]{:S(2)}) collective-permute-start(bf16[1,768,512]{2,1,0:T(8,128)(2,1)} %refs_10_.1), channel_id=1, source_target_pairs={{0,128},{128,256},{256,384},{384,0},{1,129},{129,257},{257,385},{3... | collective-permute-start | bytes 2359304 | tf_op jit(solution)/shard_map/ppermute | solution.py:280
  44.8 6.0 %collective-permute-done.refs_1_ = bf16[1,512,768]{2,1,0:T(8,128)(2,1)S(1)} collective-permute-done((bf16[1,512,768]{2,1,0:T(8,128)(2,1)}, bf16[1,512,768]{2,1,0:T(8,128)(2,1)S(1)}, u32[]{:S(2)}, u32[]{:S(2)}) %collective-permute-start) | collective-permute-done | bytes 786464 | tf_op jit(solution)/shard_map/ppermute | solution.py:280
  50.8 2.7 %collective-permute-start.9 = (bf16[1,768,512]{2,1,0:T(8,128)(2,1)}, bf16[1,768,512]{2,1,0:T(8,128)(2,1)}, u32[]{:S(2)}, u32[]{:S(2)}) collective-permute-start(bf16[1,768,512]{2,1,0:T(8,128)(2,1)} %refs_10_.1), channel_id=1, source_target_pairs={{0,384},{128,0},{256,128},{384,256},{1,385},{129,1},{257,129},{385... | collective-permute-start | bytes 2359304 | tf_op jit(solution)/shard_map/ppermute | solution.py:280
  55.3 4.3 %collective-permute-start.2 = (bf16[1,256,768]{2,1,0:T(8,128)(2,1)}, bf16[1,256,768]{2,1,0:T(8,128)(2,1)S(1)}, u32[]{:S(2)}, u32[]{:S(2)}) collective-permute-start(bf16[1,256,768]{2,1,0:T(8,128)(2,1)} %slice.50), channel_id=1, source_target_pairs={{0,128},{128,256},{256,384},{384,0},{1,129},{129,257},{257,385},{3... | collective-permute-start | bytes 1179656 | tf_op jit(solution)/shard_map/ppermute | solution.py:280
  60.4 7.3 %collective-permute-done.4.refs_6_ = bf16[1,512,768]{2,1,0:T(8,128)(2,1)S(1)} collective-permute-done((bf16[1,512,768]{2,1,0:T(8,128)(2,1)}, bf16[1,512,768]{2,1,0:T(8,128)(2,1)S(1)}, u32[]{:S(2)}, u32[]{:S(2)}) %collective-permute-start.4) | collective-permute-done | bytes 786464 | tf_op jit(solution)/shard_map/ppermute | solution.py:280
  67.7 2.7 %collective-permute-start.3 = (bf16[1,256,768]{2,1,0:T(8,128)(2,1)}, bf16[1,256,768]{2,1,0:T(8,128)(2,1)}, u32[]{:S(2)}, u32[]{:S(2)}) collective-permute-start(bf16[1,256,768]{2,1,0:T(8,128)(2,1)} %slice.51), channel_id=1, source_target_pairs={{0,384},{128,0},{256,128},{384,256},{1,385},{129,1},{257,129},{385... | collective-permute-start | bytes 1179656 | tf_op jit(solution)/shard_map/ppermute | solution.py:280
  71.3 4.2 %collective-permute-start.6 = (bf16[1,256,768]{2,1,0:T(8,128)(2,1)}, bf16[1,256,768]{2,1,0:T(8,128)(2,1)}, u32[]{:S(2)}, u32[]{:S(2)}) collective-permute-start(bf16[1,256,768]{2,1,0:T(8,128)(2,1)} %slice.52), channel_id=1, source_target_pairs={{0,128},{128,256},{256,384},{384,0},{1,129},{129,257},{257,385},{3... | collective-permute-start | bytes 1179656 | tf_op jit(solution)/shard_map/ppermute | solution.py:280
  76.3 8.3 %collective-permute-done.8.refs_11_ = bf16[1,768,512]{2,1,0:T(8,128)(2,1)S(1)} collective-permute-done((bf16[1,768,512]{2,1,0:T(8,128)(2,1)}, bf16[1,768,512]{2,1,0:T(8,128)(2,1)S(1)}, u32[]{:S(2)}, u32[]{:S(2)}) %collective-permute-start.8) | collective-permute-done | bytes 786464 | tf_op jit(solution)/shard_map/ppermute | solution.py:280
  84.5 2.7 %collective-permute-start.7 = (bf16[1,256,768]{2,1,0:T(8,128)(2,1)}, bf16[1,256,768]{2,1,0:T(8,128)(2,1)}, u32[]{:S(2)}, u32[]{:S(2)}) collective-permute-start(bf16[1,256,768]{2,1,0:T(8,128)(2,1)} %slice.53), channel_id=1, source_target_pairs={{0,384},{128,0},{256,128},{384,256},{1,385},{129,1},{257,129},{385... | collective-permute-start | bytes 1179656 | tf_op jit(solution)/shard_map/ppermute | solution.py:280
  88.2 4.1 %collective-permute-start.10 = (bf16[1,384,512]{2,1,0:T(8,128)(2,1)}, bf16[1,384,512]{2,1,0:T(8,128)(2,1)S(1)}, u32[]{:S(2)}, u32[]{:S(2)}) collective-permute-start(bf16[1,384,512]{2,1,0:T(8,128)(2,1)} %slice.54), channel_id=1, source_target_pairs={{0,128},{128,256},{256,384},{384,0},{1,129},{129,257},{257,385},{3... | collective-permute-start | bytes 1179656 | tf_op jit(solution)/shard_map/ppermute | solution.py:280
  94.1 7.1 %all-to-all-done = bf16[128,6,16,128]{3,2,1,0:T(8,128)(2,1)} async-done(((bf16[128,6,16,128]{3,2,1,0:T(8,128)(2,1)}), bf16[128,6,16,128]{3,2,1,0:T(8,128)(2,1)}, u32[]{:S(2)}, u32[]{:S(2)}) %all-to-all-start) | async-done | bytes 3145760 | tf_op jit(solution)/shard_map/all_to_all | solution.py:308
  103.7 2.9 %collective-permute-start.11 = (bf16[1,384,512]{2,1,0:T(8,128)(2,1)}, bf16[1,384,512]{2,1,0:T(8,128)(2,1)S(1)}, u32[]{:S(2)}, u32[]{:S(2)}) collective-permute-start(bf16[1,384,512]{2,1,0:T(8,128)(2,1)} %slice.55), channel_id=1, source_target_pairs={{0,384},{128,0},{256,128},{384,256},{1,385},{129,1},{257,129},{385... | collective-permute-start | bytes 1179656 | tf_op jit(solution)/shard_map/ppermute | solution.py:280
  108.9 8.5 %collective-permute-done.11.refs_14_ = bf16[1,384,512]{2,1,0:T(8,128)(2,1)S(1)} collective-permute-done((bf16[1,384,512]{2,1,0:T(8,128)(2,1)}, bf16[1,384,512]{2,1,0:T(8,128)(2,1)S(1)}, u32[]{:S(2)}, u32[]{:S(2)}) %collective-permute-start.11) | collective-permute-done | bytes 393248 | tf_op jit(solution)/shard_map/ppermute | solution.py:280
  117.5 12.0 %expert_slots.1 = (bf16[384,2048]{1,0:T(8,128)(2,1)S(1)}, bf16[384,768]{1,0:T(8,128)(2,1)S(1)}, bf16[384,768]{1,0:T(8,128)(2,1)S(1)}, bf16[384,32]{1,0:T(8,128)(2,1)S(1)}) custom-call(s32[1]{0:T(128)} %bitcast.rank, bf16[384,2048]{1,0:T(8,128)(2,1)S(1)} %get-tuple-element.30.rows_in, bf16[384,2048]{1,0:T(8,128)(2,1)} %copy-done, ...), custom_call_target="tpu_custom_call" | custom-call | flops 6039797760 | bytes 14155776 | tf_op jit(solution)/shard_map/expert_slots/pallas_call | solution.py:233
  131.1 11.0 %all-to-all-start.1 = ((bf16[128,3,16,128]{3,2,1,0:T(8,128)(2,1)}), bf16[128,3,16,128]{3,2,1,0:T(8,128)(2,1)}, u32[]{:S(2)}, u32[]{:S(2)}) async-start(bf16[128,3,16,128]{3,2,1,0:T(8,128)(2,1)} %bitcast.34), calls=%async_computation.1 | async-start | bytes 3145728 | tf_op jit(solution)/shard_map/all_to_all | solution.py:318
  147.2 3.0 %collective-permute-start.13 = (bf16[32,5632]{1,0:T(8,128)(2,1)S(1)}, bf16[32,5632]{1,0:T(8,128)(2,1)S(1)}, u32[]{:S(2)}, u32[]{:S(2)}) collective-permute-start(bf16[32,5632]{1,0:T(8,128)(2,1)S(1)} %adapter_grads.1), channel_id=1, source_target_pairs={{0,256},{128,384},{256,0},{384,128},{1,257},{129,385},{257,1},{385... | collective-permute-start | bytes 1081352 | tf_op jit(solution)/shard_map/ppermute | solution.py:280
  150.2 4.1 %collective-permute-start.12 = (bf16[32,5632]{1,0:T(8,128)(2,1)S(1)}, bf16[32,5632]{1,0:T(8,128)(2,1)S(1)}, u32[]{:S(2)}, u32[]{:S(2)}) collective-permute-start(bf16[32,5632]{1,0:T(8,128)(2,1)S(1)} %adapter_grads.1), channel_id=1, source_target_pairs={{0,128},{128,256},{256,384},{384,0},{1,129},{129,257},{257,385},{3... | collective-permute-start | bytes 1081352 | tf_op jit(solution)/shard_map/ppermute | solution.py:280
  154.3 11.7 %collective-permute-done.14 = bf16[32,5632]{1,0:T(8,128)(2,1)S(1)} collective-permute-done((bf16[32,5632]{1,0:T(8,128)(2,1)S(1)}, bf16[32,5632]{1,0:T(8,128)(2,1)S(1)}, u32[]{:S(2)}, u32[]{:S(2)}) %collective-permute-start.14) | collective-permute-done | bytes 360480 | tf_op jit(solution)/shard_map/ppermute | solution.py:280
  166.0 2.5 %collective-permute-done.12 = bf16[32,5632]{1,0:T(8,128)(2,1)S(1)} collective-permute-done((bf16[32,5632]{1,0:T(8,128)(2,1)S(1)}, bf16[32,5632]{1,0:T(8,128)(2,1)S(1)}, u32[]{:S(2)}, u32[]{:S(2)}) %collective-permute-start.12) | collective-permute-done | bytes 360480 | tf_op jit(solution)/shard_map/ppermute | solution.py:280
  170.2 13.2 %all-to-all-done.1 = bf16[128,3,16,128]{3,2,1,0:T(8,128)(2,1)} async-done(((bf16[128,3,16,128]{3,2,1,0:T(8,128)(2,1)}), bf16[128,3,16,128]{3,2,1,0:T(8,128)(2,1)}, u32[]{:S(2)}, u32[]{:S(2)}) %all-to-all-start.1) | async-done | bytes 1572896 | tf_op jit(solution)/shard_map/all_to_all | solution.py:318
  (76 shorter events, 31.5 us)
Async XLA Ops:
  9.9 91.3 %all-to-all-start = ((bf16[128,6,16,128]{3,2,1,0:T(8,128)(2,1)}), bf16[128,6,16,128]{3,2,1,0:T(8,128)(2,1)}, u32[]{:S(2)}, u32[]{:S(2)}) async-start(bf16[128,6,16,128]{3,2,1,0:T(8,128)(2,1)} %bitcast.1), calls=%async_computation | async-start | bytes 6291456 | tf_op jit(solution)/shard_map/all_to_all | solution.py:308
  28.2 22.6 %collective-permute-start = (bf16[1,512,768]{2,1,0:T(8,128)(2,1)}, bf16[1,512,768]{2,1,0:T(8,128)(2,1)S(1)}, u32[]{:S(2)}, u32[]{:S(2)}) collective-permute-start(bf16[1,512,768]{2,1,0:T(8,128)(2,1)} %refs_0_.1), channel_id=1, source_target_pairs={{0,128},{128,256},{256,384},{384,0},{1,129},{129,257},{257,385},{3... | collective-permute-start | bytes 2359304 | tf_op jit(solution)/shard_map/ppermute | solution.py:280
  30.6 24.7 %collective-permute-start.1 = (bf16[1,512,768]{2,1,0:T(8,128)(2,1)}, bf16[1,512,768]{2,1,0:T(8,128)(2,1)S(1)}, u32[]{:S(2)}, u32[]{:S(2)}) collective-permute-start(bf16[1,512,768]{2,1,0:T(8,128)(2,1)} %refs_0_.1), channel_id=1, source_target_pairs={{0,384},{128,0},{256,128},{384,256},{1,385},{129,1},{257,129},{385... | collective-permute-start | bytes 2359304 | tf_op jit(solution)/shard_map/ppermute | solution.py:280
  34.1 33.6 %collective-permute-start.4 = (bf16[1,512,768]{2,1,0:T(8,128)(2,1)}, bf16[1,512,768]{2,1,0:T(8,128)(2,1)S(1)}, u32[]{:S(2)}, u32[]{:S(2)}) collective-permute-start(bf16[1,512,768]{2,1,0:T(8,128)(2,1)} %refs_5_.1), channel_id=1, source_target_pairs={{0,128},{128,256},{256,384},{384,0},{1,129},{129,257},{257,385},{3... | collective-permute-start | bytes 2359304 | tf_op jit(solution)/shard_map/ppermute | solution.py:280
  37.7 33.6 %collective-permute-start.5 = (bf16[1,512,768]{2,1,0:T(8,128)(2,1)}, bf16[1,512,768]{2,1,0:T(8,128)(2,1)S(1)}, u32[]{:S(2)}, u32[]{:S(2)}) collective-permute-start(bf16[1,512,768]{2,1,0:T(8,128)(2,1)} %refs_5_.1), channel_id=1, source_target_pairs={{0,384},{128,0},{256,128},{384,256},{1,385},{129,1},{257,129},{385... | collective-permute-start | bytes 2359304 | tf_op jit(solution)/shard_map/ppermute | solution.py:280
  40.0 44.6 %collective-permute-start.8 = (bf16[1,768,512]{2,1,0:T(8,128)(2,1)}, bf16[1,768,512]{2,1,0:T(8,128)(2,1)S(1)}, u32[]{:S(2)}, u32[]{:S(2)}) collective-permute-start(bf16[1,768,512]{2,1,0:T(8,128)(2,1)} %refs_10_.1), channel_id=1, source_target_pairs={{0,128},{128,256},{256,384},{384,0},{1,129},{129,257},{257,385},{3... | collective-permute-start | bytes 2359304 | tf_op jit(solution)/shard_map/ppermute | solution.py:280
  50.8 37.4 %collective-permute-start.9 = (bf16[1,768,512]{2,1,0:T(8,128)(2,1)}, bf16[1,768,512]{2,1,0:T(8,128)(2,1)}, u32[]{:S(2)}, u32[]{:S(2)}) collective-permute-start(bf16[1,768,512]{2,1,0:T(8,128)(2,1)} %refs_10_.1), channel_id=1, source_target_pairs={{0,384},{128,0},{256,128},{384,256},{1,385},{129,1},{257,129},{385... | collective-permute-start | bytes 2359304 | tf_op jit(solution)/shard_map/ppermute | solution.py:280
  55.3 32.7 %copy-start.8 = (bf16[1,512,768]{2,1,0:T(8,128)(2,1)}, bf16[1,512,768]{2,1,0:T(8,128)(2,1)S(1)}, u32[]{:S(2)}) copy-start(bf16[1,512,768]{2,1,0:T(8,128)(2,1)S(1)} %collective-permute-done.1.refs_2_) | copy-start | bytes 2359300
  55.3 48.4 %collective-permute-start.2 = (bf16[1,256,768]{2,1,0:T(8,128)(2,1)}, bf16[1,256,768]{2,1,0:T(8,128)(2,1)S(1)}, u32[]{:S(2)}, u32[]{:S(2)}) collective-permute-start(bf16[1,256,768]{2,1,0:T(8,128)(2,1)} %slice.50), channel_id=1, source_target_pairs={{0,128},{128,256},{256,384},{384,0},{1,129},{129,257},{257,385},{3... | collective-permute-start | bytes 1179656 | tf_op jit(solution)/shard_map/ppermute | solution.py:280
  67.7 26.5 %copy-start.10 = (bf16[1,512,768]{2,1,0:T(8,128)(2,1)}, bf16[1,512,768]{2,1,0:T(8,128)(2,1)S(1)}, u32[]{:S(2)}) copy-start(bf16[1,512,768]{2,1,0:T(8,128)(2,1)S(1)} %collective-permute-done.4.refs_6_) | copy-start | bytes 2359300
  67.7 41.3 %collective-permute-start.3 = (bf16[1,256,768]{2,1,0:T(8,128)(2,1)}, bf16[1,256,768]{2,1,0:T(8,128)(2,1)}, u32[]{:S(2)}, u32[]{:S(2)}) collective-permute-start(bf16[1,256,768]{2,1,0:T(8,128)(2,1)} %slice.51), channel_id=1, source_target_pairs={{0,384},{128,0},{256,128},{384,256},{1,385},{129,1},{257,129},{385... | collective-permute-start | bytes 1179656 | tf_op jit(solution)/shard_map/ppermute | solution.py:280
  71.3 32.4 %copy-start.12 = (bf16[1,512,768]{2,1,0:T(8,128)(2,1)}, bf16[1,512,768]{2,1,0:T(8,128)(2,1)S(1)}, u32[]{:S(2)}) copy-start(bf16[1,512,768]{2,1,0:T(8,128)(2,1)S(1)} %collective-permute-done.5.refs_7_) | copy-start | bytes 2359300
  71.3 37.7 %collective-permute-start.6 = (bf16[1,256,768]{2,1,0:T(8,128)(2,1)}, bf16[1,256,768]{2,1,0:T(8,128)(2,1)}, u32[]{:S(2)}, u32[]{:S(2)}) collective-permute-start(bf16[1,256,768]{2,1,0:T(8,128)(2,1)} %slice.52), channel_id=1, source_target_pairs={{0,128},{128,256},{256,384},{384,0},{1,129},{129,257},{257,385},{3... | collective-permute-start | bytes 1179656 | tf_op jit(solution)/shard_map/ppermute | solution.py:280
  84.5 19.2 %copy-start.14 = (bf16[1,768,512]{2,1,0:T(8,128)(2,1)}, bf16[1,768,512]{2,1,0:T(8,128)(2,1)S(1)}, u32[]{:S(2)}) copy-start(bf16[1,768,512]{2,1,0:T(8,128)(2,1)S(1)} %collective-permute-done.8.refs_11_) | copy-start | bytes 2359300
  84.5 24.4 %collective-permute-start.7 = (bf16[1,256,768]{2,1,0:T(8,128)(2,1)}, bf16[1,256,768]{2,1,0:T(8,128)(2,1)}, u32[]{:S(2)}, u32[]{:S(2)}) collective-permute-start(bf16[1,256,768]{2,1,0:T(8,128)(2,1)} %slice.53), channel_id=1, source_target_pairs={{0,384},{128,0},{256,128},{384,256},{1,385},{129,1},{257,129},{385... | collective-permute-start | bytes 1179656 | tf_op jit(solution)/shard_map/ppermute | solution.py:280
  88.2 20.7 %collective-permute-start.10 = (bf16[1,384,512]{2,1,0:T(8,128)(2,1)}, bf16[1,384,512]{2,1,0:T(8,128)(2,1)S(1)}, u32[]{:S(2)}, u32[]{:S(2)}) collective-permute-start(bf16[1,384,512]{2,1,0:T(8,128)(2,1)} %slice.54), channel_id=1, source_target_pairs={{0,128},{128,256},{256,384},{384,0},{1,129},{129,257},{257,385},{3... | collective-permute-start | bytes 1179656 | tf_op jit(solution)/shard_map/ppermute | solution.py:280
  103.7 13.7 %collective-permute-start.11 = (bf16[1,384,512]{2,1,0:T(8,128)(2,1)}, bf16[1,384,512]{2,1,0:T(8,128)(2,1)S(1)}, u32[]{:S(2)}, u32[]{:S(2)}) collective-permute-start(bf16[1,384,512]{2,1,0:T(8,128)(2,1)} %slice.55), channel_id=1, source_target_pairs={{0,384},{128,0},{256,128},{384,256},{1,385},{129,1},{257,129},{385... | collective-permute-start | bytes 1179656 | tf_op jit(solution)/shard_map/ppermute | solution.py:280
  106.7 10.8 %copy-start.15 = (bf16[1,768,512]{2,1,0:T(8,128)(2,1)S(1)}, bf16[1,768,512]{2,1,0:T(8,128)(2,1)}, u32[]{:S(2)}) copy-start(bf16[1,768,512]{2,1,0:T(8,128)(2,1)} %copy-done.14) | copy-start | bytes 2359300
  106.7 10.7 %copy-start.20 = (bf16[1,768,512]{2,1,0:T(8,128)(2,1)S(1)}, bf16[1,768,512]{2,1,0:T(8,128)(2,1)}, u32[]{:S(2)}) copy-start(bf16[1,768,512]{2,1,0:T(8,128)(2,1)} %refs_10_.1) | copy-start | bytes 2359300
  131.1 11.0 %copy-start.1 = (bf16[384,2048]{1,0:T(8,128)(2,1)S(1)}, bf16[384,2048]{1,0:T(8,128)(2,1)}, u32[]{:S(2)}) copy-start(bf16[384,2048]{1,0:T(8,128)(2,1)} %copy-done) | copy-start | bytes 4718596
  131.1 52.2 %all-to-all-start.1 = ((bf16[128,3,16,128]{3,2,1,0:T(8,128)(2,1)}), bf16[128,3,16,128]{3,2,1,0:T(8,128)(2,1)}, u32[]{:S(2)}, u32[]{:S(2)}) async-start(bf16[128,3,16,128]{3,2,1,0:T(8,128)(2,1)} %bitcast.34), calls=%async_computation.1 | async-start | bytes 3145728 | tf_op jit(solution)/shard_map/all_to_all | solution.py:318
  145.3 20.7 %collective-permute-start.14 = (bf16[32,5632]{1,0:T(8,128)(2,1)S(1)}, bf16[32,5632]{1,0:T(8,128)(2,1)S(1)}, u32[]{:S(2)}, u32[]{:S(2)}) collective-permute-start(bf16[32,5632]{1,0:T(8,128)(2,1)S(1)} %adapter_grads.1), channel_id=1, source_target_pairs={{0,384},{128,0},{256,128},{384,256},{1,385},{129,1},{257,129},{385... | collective-permute-start | bytes 1081352 | tf_op jit(solution)/shard_map/ppermute | solution.py:280
  147.2 18.8 %collective-permute-start.13 = (bf16[32,5632]{1,0:T(8,128)(2,1)S(1)}, bf16[32,5632]{1,0:T(8,128)(2,1)S(1)}, u32[]{:S(2)}, u32[]{:S(2)}) collective-permute-start(bf16[32,5632]{1,0:T(8,128)(2,1)S(1)} %adapter_grads.1), channel_id=1, source_target_pairs={{0,256},{128,384},{256,0},{384,128},{1,257},{129,385},{257,1},{385... | collective-permute-start | bytes 1081352 | tf_op jit(solution)/shard_map/ppermute | solution.py:280
  150.2 18.3 %collective-permute-start.12 = (bf16[32,5632]{1,0:T(8,128)(2,1)S(1)}, bf16[32,5632]{1,0:T(8,128)(2,1)S(1)}, u32[]{:S(2)}, u32[]{:S(2)}) collective-permute-start(bf16[32,5632]{1,0:T(8,128)(2,1)S(1)} %adapter_grads.1), channel_id=1, source_target_pairs={{0,128},{128,256},{256,384},{384,0},{1,129},{129,257},{257,385},{3... | collective-permute-start | bytes 1081352 | tf_op jit(solution)/shard_map/ppermute | solution.py:280
  (15 other events, 68.3 us)

commit v6 on v5

v6 whole, which is shorter than its diff:
```python
import jax
import jax.numpy as jnp
from jax import lax
from jax.experimental import pallas as pl
from jax.experimental.pallas import tpu as pltpu
from jax.sharding import PartitionSpec as P

CAP = 3
LANES = 128
COLS = 256
SCALE = 2.0
F32 = jnp.float32
BF16 = jnp.bfloat16

VMEM = pl.BlockSpec(memory_space=pltpu.VMEM)
SMEM = pl.BlockSpec(memory_space=pltpu.SMEM)
HBM = pl.BlockSpec(memory_space=pltpu.HBM)


def params(mib):
    return pltpu.CompilerParams(vmem_limit_bytes=mib * 1024 * 1024)


def block_rows(shapes):
    rows = []
    start = 0
    for weight, (height, cols) in enumerate(shapes):
        for c in range(cols // COLS):
            rows.append((weight, c, start, height))
            start += height
    return rows, start


def in_halves(first, last, half):
    parts = []
    for side in range(2):
        low = max(first, side * half)
        high = min(last, (side + 1) * half)
        if low < high:
            parts.append((side, low - side * half, low - first, high - low))
    return parts


def place_kernel(
    routes, prob, limits, tokens, grads, w_gate, w_up, w_down,
    send, slots, first_half, second_half,
    count, staged, token_rows, grad_rows, packed, sems,
):
    halves = (first_half, second_half)
    blocks, _ = block_rows([w.shape[1:] for w in (w_gate, w_up, w_down)])
    loads = []
    for i, (weight, c, start, height) in enumerate(blocks):
        ref = (w_gate, w_up, w_down)[weight]
        loads.append(
            pltpu.make_async_copy(
                ref.at[0, :, pl.ds(c * COLS, COLS)], packed.at[pl.ds(start, height), :], sems.at[i]
            )
        )
    for load in loads:
        load.start()

    total = send.shape[0]
    staged[...] = jnp.zeros_like(staged)
    token_rows[...] = tokens[...].reshape(token_rows.shape)
    grad_rows[...] = grads[...].reshape(grad_rows.shape)

    def clear(e, carry):
        count[e] = 0
        return carry

    lax.fori_loop(0, limits.shape[0], clear, 0, unroll=8)
    for load in loads:
        load.wait()
    half = packed.shape[0] // 2
    stores = [
        pltpu.make_async_copy(packed.at[pl.ds(i * half, half), :], halves[i], sems.at[len(blocks) + i])
        for i in range(2)
    ]
    for store in stores:
        store.start()

    def one_token(t, carry):
        row = token_rows[t]
        grad = grad_rows[t].astype(F32)
        for k in range(routes.shape[0]):
            e = routes[k, t]
            rank = count[e]
            count[e] = rank + 1
            kept = rank < limits[e]
            slots[k, t] = jnp.where(kept, e * CAP + rank, -1)
            place = jnp.where(kept, e * (2 * CAP) + rank, total)
            staged[place] = row
            staged[place + CAP] = (prob[k, t] * grad).astype(BF16)
        return carry

    lax.fori_loop(0, routes.shape[1], one_token, 0)
    send[...] = staged[0:total]
    for store in stores:
        store.wait()


def place_rows(routes, prob, limits, tokens, grads, w_gate, w_up, w_down):
    count, width = tokens.shape
    subs = width // LANES
    experts = limits.shape[0]
    total = experts * 2 * CAP
    blocks, rows = block_rows([w.shape[1:] for w in (w_gate, w_up, w_down)])
    return pl.pallas_call(
        place_kernel,
        out_shape=(
            jax.ShapeDtypeStruct((total, subs, LANES), BF16),
            jax.ShapeDtypeStruct(routes.shape, jnp.int32),
            jax.ShapeDtypeStruct((rows // 2, COLS), BF16),
            jax.ShapeDtypeStruct((rows // 2, COLS), BF16),
        ),
        in_specs=[SMEM, SMEM, SMEM, VMEM, VMEM, HBM, HBM, HBM],
        out_specs=(VMEM, SMEM, HBM, HBM),
        scratch_shapes=[
            pltpu.SMEM((experts,), jnp.int32),
            pltpu.VMEM((total + 2 * CAP, subs, LANES), BF16),
            pltpu.VMEM((count, subs, LANES), BF16),
            pltpu.VMEM((count, subs, LANES), BF16),
            pltpu.VMEM((rows, COLS), BF16),
            pltpu.SemaphoreType.DMA((len(blocks) + 2,)),
        ],
        compiler_params=params(56),
        name="place_rows",
    )(routes, prob, limits, tokens, grads, w_gate, w_up, w_down)


def combine_kernel(slots, back, out, rows):
    def one_token(t, carry):
        total = jnp.zeros(rows.shape[1:], F32)
        for k in range(slots.shape[0]):
            slot = slots[k, t]
            row = back[jnp.maximum(slot, 0)].astype(F32)
            total += jnp.where(slot >= 0, row, 0.0)
        rows[t] = total.astype(BF16)
        return carry

    lax.fori_loop(0, slots.shape[1], one_token, 0)
    out[...] = rows[...].reshape(out.shape)


def combine_rows(slots, back):
    count = slots.shape[1]
    subs, lanes = back.shape[1:]
    return pl.pallas_call(
        combine_kernel,
        out_shape=jax.ShapeDtypeStruct((count, subs * lanes), BF16),
        in_specs=[SMEM, VMEM],
        out_specs=VMEM,
        scratch_shapes=[pltpu.VMEM((count, subs, lanes), BF16)],
        compiler_params=params(16),
        name="combine_rows",
    )(slots, back)


def dot(left, right, left_dim, right_dim):
    return lax.dot_general(
        left, right, (((left_dim,), (right_dim,)), ((), ())), preferred_element_type=F32
    )


def low_kernel(recv, up_in, down_out, rows_in, rows_grad, low_up, back_low, up_in_near):
    x = recv[:, :CAP].reshape(rows_in.shape)
    rows_in[...] = x
    low_up[...] = dot(x, up_in[0], 1, 1).astype(BF16)
    g = recv[:, CAP:].reshape(rows_grad.shape)
    rows_grad[...] = g
    back_low[...] = dot(g, down_out[0], 1, 1).astype(BF16)
    up_in_near[...] = up_in[0]


def low_products(recv, up_in, down_out):
    rows = recv.shape[0] * CAP
    rank, width = up_in.shape[1:]
    return pl.pallas_call(
        low_kernel,
        out_shape=(
            jax.ShapeDtypeStruct((rows, width), BF16),
            jax.ShapeDtypeStruct((rows, width), BF16),
            jax.ShapeDtypeStruct((rows, rank), BF16),
            jax.ShapeDtypeStruct((rows, rank), BF16),
            jax.ShapeDtypeStruct((rank, width), BF16),
        ),
        in_specs=[VMEM] * 3,
        out_specs=(VMEM,) * 5,
        compiler_params=params(24),
        cost_estimate=pl.CostEstimate(
            flops=4 * rows * rank * width, bytes_accessed=8 * rows * width, transcendentals=0
        ),
        name="low_products",
    )(recv, up_in, down_out)


def slot_kernel(rank, rows_in, rows_grad, low_up, back_low, up_in, up_out, down_in, *refs):
    owners = (refs[0:2], refs[2:4], refs[4:6], refs[6:8])
    slot_grad, hidden, grad_up, up_low, gate_up, down, grads, slot_rows, sems = refs[8:]
    width = gate_up.shape[0]
    inner = hidden.shape[1]
    shards = len(owners)
    part = width // shards
    chunks = inner // COLS
    half = owners[0][0].shape[0]
    blocks, _ = block_rows([(part, inner), (part, inner), (inner, part)])
    mine = rank[0]
    shifts = (0, shards - 1, 1, 2)
    steps = []
    number = 0
    for c in range(chunks):
        moves = []
        for shift, pair in zip(shifts, owners):
            place = pl.multiple_of(lax.rem(mine + shift, shards) * part, part)
            for weight, block, start, height in blocks:
                if weight < 2 and block != c:
                    continue
                if weight == 2:
                    start, height = start + c * COLS, COLS
                for side, at, skip, rows in in_halves(start, start + height, half):
                    if weight < 2:
                        target = gate_up.at[
                            pl.ds(pl.multiple_of(place + skip, COLS), rows),
                            pl.ds(weight * inner + c * COLS, COLS),
                        ]
                    else:
                        target = down.at[
                            pl.ds(c * COLS + skip, rows),
                            pl.ds(pl.multiple_of(place + block * COLS, COLS), COLS),
                        ]
                    moves.append((pair[side].at[pl.ds(at, rows), :], target))
        copies = []
        for source, target in moves:
            copies.append(pltpu.make_async_copy(source, target, sems.at[number]))
            number += 1
        steps.append(copies)
    for copies in steps:
        for copy in copies:
            copy.start()

    x = rows_in
    g = rows_grad
    for c in range(chunks):
        cols = pl.ds(c * COLS, COLS)
        later = pl.ds(inner + c * COLS, COLS)
        for copy in steps[c]:
            copy.wait()
        gate_pre = dot(x[...], gate_up[:, cols], 1, 0)
        up_sum = dot(x[...], gate_up[:, later], 1, 0) + SCALE * dot(low_up[...], up_out[0, :, cols], 1, 0)
        grad_hidden = dot(g[...], down[cols, :], 1, 1) + SCALE * dot(
            back_low[...], down_in[0, :, cols], 1, 0
        )
        sig = jax.nn.sigmoid(gate_pre)
        active = gate_pre * sig
        up_grad = (grad_hidden * active).astype(BF16)
        hidden[:, cols] = (active * up_sum).astype(BF16)
        grads[:, cols] = (
            grad_hidden * up_sum * sig * (1.0 + gate_pre * (1.0 - sig))
        ).astype(BF16)
        grads[:, later] = up_grad
        grad_up[:, cols] = up_grad
    up_low[...] = dot(grad_up[...], up_out[0], 1, 1).astype(BF16)
    for c in range(width // COLS):
        cols = pl.ds(c * COLS, COLS)
        slot_rows[:, cols] = (
            dot(grads[...], gate_up[cols, :], 1, 1) + SCALE * dot(up_low[...], up_in[:, cols], 1, 0)
        ).astype(BF16)
    slot_grad[...] = slot_rows[...].reshape(slot_grad.shape)


def adapter_kernel(rows_in, rows_grad, hidden, grad_up, low_up, back_low, up_low, down_in, adapters):
    width, inner = rows_in.shape[1], hidden.shape[1]
    low_down = dot(hidden[...], down_in[0], 1, 1).astype(BF16)
    at = 0
    for left, right in (
        (up_low[...], rows_in),
        (low_down, rows_grad),
        (low_up[...], grad_up),
        (back_low[...], hidden),
    ):
        for c in range(right.shape[1] // COLS):
            piece = dot(left, right[:, pl.ds(c * COLS, COLS)], 0, 0)
            adapters[:, pl.ds(at, COLS)] = (SCALE * piece).astype(BF16)
            at += COLS


def expert_slots(rows_in, rows_grad, weights, low_up, back_low, up_in, up_out, down_in):
    rows, width = rows_in.shape
    rank, inner = up_out.shape[1:]
    mine = lax.axis_index("rep").astype(jnp.int32).reshape(1)
    return pl.pallas_call(
        slot_kernel,
        out_shape=(
            jax.ShapeDtypeStruct((rows, width // LANES, LANES), BF16),
            jax.ShapeDtypeStruct((rows, inner), BF16),
            jax.ShapeDtypeStruct((rows, inner), BF16),
            jax.ShapeDtypeStruct((rows, rank), BF16),
        ),
        in_specs=[SMEM] + [VMEM] * 7 + [HBM] * 8,
        out_specs=(VMEM,) * 4,
        scratch_shapes=[
            pltpu.VMEM((width, 2 * inner), BF16),
            pltpu.VMEM((inner, width), BF16),
            pltpu.VMEM((rows, 2 * inner), BF16),
            pltpu.VMEM((rows, width), BF16),
            pltpu.SemaphoreType.DMA((72,)),
        ],
        compiler_params=params(40),
        cost_estimate=pl.CostEstimate(
            flops=10 * rows * width * inner,
            bytes_accessed=6 * width * inner + 6 * rows * width,
            transcendentals=rows * inner,
        ),
        name="expert_slots",
    )(mine, rows_in, rows_grad, low_up, back_low, up_in, up_out, down_in, *weights)


def adapter_grads(rows_in, rows_grad, hidden, grad_up, low_up, back_low, up_low, down_in):
    rows, width = rows_in.shape
    inner = hidden.shape[1]
    rank = up_low.shape[1]
    return pl.pallas_call(
        adapter_kernel,
        out_shape=jax.ShapeDtypeStruct((rank, 2 * (width + inner)), BF16),
        in_specs=[VMEM] * 8,
        out_specs=VMEM,
        compiler_params=params(24),
        cost_estimate=pl.CostEstimate(
            flops=4 * rows * rank * (width + inner),
            bytes_accessed=4 * rows * (width + inner),
            transcendentals=0,
        ),
        name="adapter_grads",
    )(rows_in, rows_grad, hidden, grad_up, low_up, back_low, up_low, down_in)


def shifted(value, axis, shift):
    count = lax.axis_size(axis)
    return lax.ppermute(value, axis, [(i, (i + shift) % count) for i in range(count)])


def replica_sum(own, axis):
    total = own.astype(F32)
    for shift in range(1, lax.axis_size(axis)):
        total += shifted(own, axis, shift).astype(F32)
    return total


def ring_gather(first, second, axis):
    left_first = shifted(first, axis, 1)
    right_second = shifted(second, axis, -1)
    right_first = shifted(first, axis, -1)
    left_second = shifted(second, axis, 1)
    far_first = shifted(left_first, axis, 1)
    far_second = shifted(right_second, axis, -1)
    return first, second, left_first, left_second, right_first, right_second, far_first, far_second


def on_device(
    tokens, out_grad, gate_prob, routes, limits,
    w_gate, w_up, w_down, up_in, up_out, down_in, down_out,
):
    width = tokens.shape[1]
    inner = up_out.shape[2]
    experts = limits.shape[0]
    slot_rows = experts * CAP
    send, slots, *own = place_rows(
        routes.T, gate_prob.T, limits, tokens, out_grad, w_gate, w_up, w_down
    )
    weights = ring_gather(*own, "rep")
    recv = lax.all_to_all(
        send.reshape(experts, 2 * CAP, width // LANES, LANES),
        ("grp", "exp"), split_axis=0, concat_axis=0, tiled=True,
    )
    rows_in, rows_grad, low_up, back_low, up_in = low_products(recv, up_in, down_out)
    slot_grad, hidden, grad_up, up_low = expert_slots(
        rows_in, rows_grad, weights, low_up, back_low, up_in, up_out, down_in
    )
    adapters = replica_sum(
        adapter_grads(rows_in, rows_grad, hidden, grad_up, low_up, back_low, up_low, down_in), "rep"
    )
    back = lax.all_to_all(
        slot_grad.reshape(experts, CAP, width // LANES, LANES),
        ("grp", "exp"), split_axis=0, concat_axis=0, tiled=True,
    )
    token_grad = combine_rows(slots, back.reshape(slot_rows, width // LANES, LANES))
    return (
        token_grad,
        adapters[None, :, 0:width],
        adapters[None, :, 2 * width : 2 * width + inner],
        adapters[None, :, 2 * width + inner :],
        adapters[None, :, width : 2 * width],
    )


def solution(mesh):
    rows = P(("rep", "grp", "exp"), None)
    owner = P(("grp", "exp"), None, None)
    return jax.shard_map(
        on_device,
        mesh=mesh,
        in_specs=(
            rows, rows, rows, rows, P(),
            P(("grp", "exp"), "rep", None),
            P(("grp", "exp"), "rep", None),
            P(("grp", "exp"), None, "rep"),
            owner, owner, owner, owner,
        ),
        out_specs=(rows, owner, owner, owner, owner),
        check_vma=False,
    )
```

time: 187 us -> 183 us (0.979)
  waiting for transfers between devices: 64.9 us -> 88.1 us
  starting transfers between devices: 78.4 us -> 60.8 us
  local copies, waits for them, and re-layouts: 20.3 us -> 9.05 us
  Pallas kernels: 21.5 us -> 23.4 us
    all_to_all x1, waiting for transfers between devices: 7.13 us -> 36.4 us  [on_device(): lax.all_to_all(send.reshape(experts, 2 * CAP, width // LANES, LANES), ('g...]
    ppermute x15 -> x9, starting transfers between devices: 49.2 us -> 28.3 us  [shifted(): lax.ppermute(value, axis, [(i, (i + shift) % count) for i in range(count)])]
    slice x7 -> x0, local copies, waits for them, and re-layouts: 8.13 us -> none  [the longest x3 3.34 us: ring_gather(): right[:, half:]]
    ppermute x15 -> x9, waiting for transfers between devices: 44.6 us -> 39.7 us  [shifted(): lax.ppermute(value, axis, [(i, (i + shift) % count) for i in range(count)])]
    all_to_all x1, starting transfers between devices: 11 us -> 14.6 us  [on_device(): lax.all_to_all(slot_grad.reshape(experts, CAP, width // LANES, LANES), ('...]
    unnamed x50 -> x36, local copies, waits for them, and re-layouts: 9.57 us -> 7.53 us
  transfers between devices with their start and end apart: 17 -> 11, of which waited for: 10 -> 7; matrix products, arithmetic and copies ran while one was open for 6% -> 1% of each run, Pallas kernels for 1% -> 1%
where the time goes in v6:
time: 183 us; the launch traced here: 182 us
  waiting for transfers between devices  88.1 us (48%)
  starting transfers between devices  60.8 us (33%)
  Pallas kernels  23.4 us (13%)
  local copies, waits for them, and re-layouts  9.05 us (5%)
    ppermute x9, waiting for transfers between devices, shifted(): lax.ppermute(value, axis, [(i, (i + shift) % count) for i in range(count)])  39.7 us
    all_to_all x1, waiting for transfers between devices, on_device(): lax.all_to_all(send.reshape(experts, 2 * CAP, width // LANES, LANES), ('g...  36.4 us
    ppermute x9, starting transfers between devices, shifted(): lax.ppermute(value, axis, [(i, (i + shift) % count) for i in range(count)])  28.3 us
    all_to_all x1, starting transfers between devices, on_device(): lax.all_to_all(send.reshape(experts, 2 * CAP, width // LANES, LANES), ('g...  18 us
    all_to_all x1, starting transfers between devices, on_device(): lax.all_to_all(slot_grad.reshape(experts, CAP, width // LANES, LANES), ('...  14.6 us
    pallas_call x1, Pallas kernels, expert_slots(): pl.pallas_call(slot_kernel, out_shape=(jax.ShapeDtypeStruct((rows, width...  12.7 us
    all_to_all x1, waiting for transfers between devices, on_device(): lax.all_to_all(slot_grad.reshape(experts, CAP, width // LANES, LANES), ('...  12.1 us
    unnamed x36, local copies, waits for them, and re-layouts  7.53 us
  transfers between devices with their start and end apart: 11, of which 7 were waited for; matrix products, arithmetic and copies ran while one was open for 1% of the time, Pallas kernels for 1%

profile of v6, /device:TPU:6, one launch (start us, length us, event | category | flops | bytes accessed | tf_op | source)
XLA Modules:
  0.0 182.4 jit_solution(1457096093578764420)
XLA Ops:
  0.6 6.2 %place_rows.1 = (bf16[768,16,128]{2,1,0:T(8,128)(2,1)}, s32[8,32]{1,0:T(8,128)}, bf16[2304,256]{1,0:T(8,128)(2,1)}, bf16[2304,256]{1,0:T(8,128)(2,1)}) custom-call(s32[8,32]{1,0:T(8,128)} %bitcast.17, f32[8,32]{1,0:T(8,128)} %bitcast.18, s32[128]{0:T(128)} %limits.1, bf16[32,2048]{1,0:T(8,128)(2,1)} %tokens.1, bf16[32,2048]{1,0:T(8,128)(2,1)} %grads.1, ...), custom_call_target="tpu_custom_call" | custom-call | tf_op jit(solution)/shard_map/place_rows/pallas_call | solution.py:108
  6.9 18.0 %all-to-all-start = ((bf16[128,6,16,128]{3,2,1,0:T(8,128)(2,1)}), bf16[128,6,16,128]{3,2,1,0:T(8,128)(2,1)S(1)}, u32[]{:S(2)}, u32[]{:S(2)}) async-start(bf16[128,6,16,128]{3,2,1,0:T(8,128)(2,1)} %bitcast.16), calls=%async_computation | async-start | bytes 6291456 | tf_op jit(solution)/shard_map/all_to_all | solution.py:371
  24.9 2.4 %collective-permute-start = (bf16[2304,256]{1,0:T(8,128)(2,1)}, bf16[2304,256]{1,0:T(8,128)(2,1)}, u32[]{:S(2)}, u32[]{:S(2)}) collective-permute-start(bf16[2304,256]{1,0:T(8,128)(2,1)} %get-tuple-element.25.refs_0_), channel_id=1, source_target_pairs={{0,128},{128,256},{256,384},{384,0},{1,129},{129,257},{257,385},{3... | collective-permute-start | bytes 3538952 | tf_op jit(solution)/shard_map/ppermute | solution.py:339
  27.3 3.5 %collective-permute-start.3 = (bf16[2304,256]{1,0:T(8,128)(2,1)}, bf16[2304,256]{1,0:T(8,128)(2,1)}, u32[]{:S(2)}, u32[]{:S(2)}) collective-permute-start(bf16[2304,256]{1,0:T(8,128)(2,1)} %get-tuple-element.26.refs_1_), channel_id=1, source_target_pairs={{0,384},{128,0},{256,128},{384,256},{1,385},{129,1},{257,129},{385... | collective-permute-start | bytes 3538952 | tf_op jit(solution)/shard_map/ppermute | solution.py:339
  30.7 2.7 %collective-permute-start.2 = (bf16[2304,256]{1,0:T(8,128)(2,1)}, bf16[2304,256]{1,0:T(8,128)(2,1)}, u32[]{:S(2)}, u32[]{:S(2)}) collective-permute-start(bf16[2304,256]{1,0:T(8,128)(2,1)} %get-tuple-element.25.refs_0_), channel_id=1, source_target_pairs={{0,384},{128,0},{256,128},{384,256},{1,385},{129,1},{257,129},{385... | collective-permute-start | bytes 3538952 | tf_op jit(solution)/shard_map/ppermute | solution.py:339
  33.5 4.3 %collective-permute-start.1 = (bf16[2304,256]{1,0:T(8,128)(2,1)}, bf16[2304,256]{1,0:T(8,128)(2,1)}, u32[]{:S(2)}, u32[]{:S(2)}) collective-permute-start(bf16[2304,256]{1,0:T(8,128)(2,1)} %get-tuple-element.26.refs_1_), channel_id=1, source_target_pairs={{0,128},{128,256},{256,384},{384,0},{1,129},{129,257},{257,385},{3... | collective-permute-start | bytes 3538952 | tf_op jit(solution)/shard_map/ppermute | solution.py:339
  37.8 18.2 %collective-permute-done.refs_2_ = bf16[2304,256]{1,0:T(8,128)(2,1)} collective-permute-done((bf16[2304,256]{1,0:T(8,128)(2,1)}, bf16[2304,256]{1,0:T(8,128)(2,1)}, u32[]{:S(2)}, u32[]{:S(2)}) %collective-permute-start) | collective-permute-done | bytes 1179680 | tf_op jit(solution)/shard_map/ppermute | solution.py:339
  56.0 3.6 %collective-permute-start.4 = (bf16[2304,256]{1,0:T(8,128)(2,1)}, bf16[2304,256]{1,0:T(8,128)(2,1)}, u32[]{:S(2)}, u32[]{:S(2)}) collective-permute-start(bf16[2304,256]{1,0:T(8,128)(2,1)} %collective-permute-done.refs_2_), channel_id=1, source_target_pairs={{0,128},{128,256},{256,384},{384,0},{1,129},{129,257},{257,385},{3... | collective-permute-start | bytes 3538952 | tf_op jit(solution)/shard_map/ppermute | solution.py:339
  59.6 2.2 %collective-permute-start.5 = (bf16[2304,256]{1,0:T(8,128)(2,1)}, bf16[2304,256]{1,0:T(8,128)(2,1)}, u32[]{:S(2)}, u32[]{:S(2)}) collective-permute-start(bf16[2304,256]{1,0:T(8,128)(2,1)} %collective-permute-done.3.refs_5_), channel_id=1, source_target_pairs={{0,384},{128,0},{256,128},{384,256},{1,385},{129,1},{257,129},{385... | collective-permute-start | bytes 3538952 | tf_op jit(solution)/shard_map/ppermute | solution.py:339
  61.8 36.4 %all-to-all-done.recv = bf16[128,6,16,128]{3,2,1,0:T(8,128)(2,1)S(1)} async-done(((bf16[128,6,16,128]{3,2,1,0:T(8,128)(2,1)}), bf16[128,6,16,128]{3,2,1,0:T(8,128)(2,1)S(1)}, u32[]{:S(2)}, u32[]{:S(2)}) %all-to-all-start) | async-done | bytes 3145760 | tf_op jit(solution)/shard_map/all_to_all | solution.py:371
  98.3 1.3 low_products.1
  99.5 1.2 copy-done.2
  100.7 4.4 %collective-permute-done.4.refs_6_ = bf16[2304,256]{1,0:T(8,128)(2,1)} collective-permute-done((bf16[2304,256]{1,0:T(8,128)(2,1)}, bf16[2304,256]{1,0:T(8,128)(2,1)}, u32[]{:S(2)}, u32[]{:S(2)}) %collective-permute-start.4) | collective-permute-done | bytes 1179680 | tf_op jit(solution)/shard_map/ppermute | solution.py:339
  105.1 3.3 %collective-permute-done.5.refs_7_ = bf16[2304,256]{1,0:T(8,128)(2,1)} collective-permute-done((bf16[2304,256]{1,0:T(8,128)(2,1)}, bf16[2304,256]{1,0:T(8,128)(2,1)}, u32[]{:S(2)}, u32[]{:S(2)}) %collective-permute-start.5) | collective-permute-done | bytes 1179680 | tf_op jit(solution)/shard_map/ppermute | solution.py:339
  108.5 12.7 %expert_slots.1 = (bf16[384,16,128]{2,1,0:T(8,128)(2,1)S(1)}, bf16[384,768]{1,0:T(8,128)(2,1)S(1)}, bf16[384,768]{1,0:T(8,128)(2,1)S(1)}, bf16[384,32]{1,0:T(8,128)(2,1)S(1)}) custom-call(s32[1]{0:T(128)} %bitcast.2.rank, bf16[384,2048]{1,0:T(8,128)(2,1)S(1)} %get-tuple-element.20.rows_in, bf16[384,2048]{1,0:T(8,128)(2,1)} %copy-done.2, ...), custom_call_target="tpu_custom_call" | custom-call | flops 6039797760 | bytes 14155776 | tf_op jit(solution)/shard_map/expert_slots/pallas_call | solution.py:291
  123.9 14.6 %all-to-all-start.1 = ((bf16[128,3,16,128]{3,2,1,0:T(8,128)(2,1)}), bf16[128,3,16,128]{3,2,1,0:T(8,128)(2,1)S(1)}, u32[]{:S(2)}, u32[]{:S(2)}) async-start(bf16[128,3,16,128]{3,2,1,0:T(8,128)(2,1)} %bitcast.15), calls=%async_computation.1 | async-start | bytes 3145728 | tf_op jit(solution)/shard_map/all_to_all | solution.py:382
  138.6 1.4 copy-done.3
  143.1 2.2 %collective-permute-start.8 = (bf16[32,5632]{1,0:T(8,128)(2,1)S(1)}, bf16[32,5632]{1,0:T(8,128)(2,1)S(1)}, u32[]{:S(2)}, u32[]{:S(2)}) collective-permute-start(bf16[32,5632]{1,0:T(8,128)(2,1)S(1)} %adapter_grads.1), channel_id=1, source_target_pairs={{0,384},{128,0},{256,128},{384,256},{1,385},{129,1},{257,129},{385... | collective-permute-start | bytes 1081352 | tf_op jit(solution)/shard_map/ppermute | solution.py:339
  145.3 3.3 %collective-permute-start.7 = (bf16[32,5632]{1,0:T(8,128)(2,1)S(1)}, bf16[32,5632]{1,0:T(8,128)(2,1)S(1)}, u32[]{:S(2)}, u32[]{:S(2)}) collective-permute-start(bf16[32,5632]{1,0:T(8,128)(2,1)S(1)} %adapter_grads.1), channel_id=1, source_target_pairs={{0,256},{128,384},{256,0},{384,128},{1,257},{129,385},{257,1},{385... | collective-permute-start | bytes 1081352 | tf_op jit(solution)/shard_map/ppermute | solution.py:339
  148.6 4.0 %collective-permute-start.6 = (bf16[32,5632]{1,0:T(8,128)(2,1)S(1)}, bf16[32,5632]{1,0:T(8,128)(2,1)S(1)}, u32[]{:S(2)}, u32[]{:S(2)}) collective-permute-start(bf16[32,5632]{1,0:T(8,128)(2,1)S(1)} %adapter_grads.1), channel_id=1, source_target_pairs={{0,128},{128,256},{256,384},{384,0},{1,129},{129,257},{257,385},{3... | collective-permute-start | bytes 1081352 | tf_op jit(solution)/shard_map/ppermute | solution.py:339
  152.7 11.2 %collective-permute-done.8 = bf16[32,5632]{1,0:T(8,128)(2,1)S(1)} collective-permute-done((bf16[32,5632]{1,0:T(8,128)(2,1)S(1)}, bf16[32,5632]{1,0:T(8,128)(2,1)S(1)}, u32[]{:S(2)}, u32[]{:S(2)}) %collective-permute-start.8) | collective-permute-done | bytes 360480 | tf_op jit(solution)/shard_map/ppermute | solution.py:339
  163.8 2.5 %collective-permute-done.6 = bf16[32,5632]{1,0:T(8,128)(2,1)S(1)} collective-permute-done((bf16[32,5632]{1,0:T(8,128)(2,1)S(1)}, bf16[32,5632]{1,0:T(8,128)(2,1)S(1)}, u32[]{:S(2)}, u32[]{:S(2)}) %collective-permute-start.6) | collective-permute-done | bytes 360480 | tf_op jit(solution)/shard_map/ppermute | solution.py:339
  168.1 12.1 %all-to-all-done.1 = bf16[128,3,16,128]{3,2,1,0:T(8,128)(2,1)S(1)} async-done(((bf16[128,3,16,128]{3,2,1,0:T(8,128)(2,1)}), bf16[128,3,16,128]{3,2,1,0:T(8,128)(2,1)S(1)}, u32[]{:S(2)}, u32[]{:S(2)}) %all-to-all-start.1) | async-done | bytes 1572896 | tf_op jit(solution)/shard_map/all_to_all | solution.py:382
  180.1 2.2 %combine_rows.1 = bf16[32,2048]{1,0:T(8,128)(2,1)} custom-call(s32[8,32]{1,0:T(8,128)S(1)} %copy-done.14, bf16[384,16,128]{2,1,0:T(8,128)(2,1)S(1)} %bitcast.14), custom_call_target="tpu_custom_call" | custom-call | tf_op jit(solution)/shard_map/combine_rows/pallas_call | solution.py:148
  (42 shorter events, 7.7 us)
Async XLA Ops:
  6.9 91.4 %copy-start.9 = (bf16[1,32,2048]{2,1,0:T(8,128)(2,1)S(1)}, bf16[1,32,2048]{2,1,0:T(8,128)(2,1)}, u32[]{:S(2)}) copy-start(bf16[1,32,2048]{2,1,0:T(8,128)(2,1)} %up_in.1) | copy-start | bytes 393220
  6.9 91.4 %copy-start.10 = (bf16[1,32,2048]{2,1,0:T(8,128)(2,1)S(1)}, bf16[1,32,2048]{2,1,0:T(8,128)(2,1)}, u32[]{:S(2)}) copy-start(bf16[1,32,2048]{2,1,0:T(8,128)(2,1)} %down_out.1) | copy-start | bytes 393220
  6.9 91.3 %all-to-all-start = ((bf16[128,6,16,128]{3,2,1,0:T(8,128)(2,1)}), bf16[128,6,16,128]{3,2,1,0:T(8,128)(2,1)S(1)}, u32[]{:S(2)}, u32[]{:S(2)}) async-start(bf16[128,6,16,128]{3,2,1,0:T(8,128)(2,1)} %bitcast.16), calls=%async_computation | async-start | bytes 6291456 | tf_op jit(solution)/shard_map/all_to_all | solution.py:371
  24.9 31.1 %collective-permute-start = (bf16[2304,256]{1,0:T(8,128)(2,1)}, bf16[2304,256]{1,0:T(8,128)(2,1)}, u32[]{:S(2)}, u32[]{:S(2)}) collective-permute-start(bf16[2304,256]{1,0:T(8,128)(2,1)} %get-tuple-element.25.refs_0_), channel_id=1, source_target_pairs={{0,128},{128,256},{256,384},{384,0},{1,129},{129,257},{257,385},{3... | collective-permute-start | bytes 3538952 | tf_op jit(solution)/shard_map/ppermute | solution.py:339
  27.3 32.3 %collective-permute-start.3 = (bf16[2304,256]{1,0:T(8,128)(2,1)}, bf16[2304,256]{1,0:T(8,128)(2,1)}, u32[]{:S(2)}, u32[]{:S(2)}) collective-permute-start(bf16[2304,256]{1,0:T(8,128)(2,1)} %get-tuple-element.26.refs_1_), channel_id=1, source_target_pairs={{0,384},{128,0},{256,128},{384,256},{1,385},{129,1},{257,129},{385... | collective-permute-start | bytes 3538952 | tf_op jit(solution)/shard_map/ppermute | solution.py:339
  30.7 70.0 %collective-permute-start.2 = (bf16[2304,256]{1,0:T(8,128)(2,1)}, bf16[2304,256]{1,0:T(8,128)(2,1)}, u32[]{:S(2)}, u32[]{:S(2)}) collective-permute-start(bf16[2304,256]{1,0:T(8,128)(2,1)} %get-tuple-element.25.refs_0_), channel_id=1, source_target_pairs={{0,384},{128,0},{256,128},{384,256},{1,385},{129,1},{257,129},{385... | collective-permute-start | bytes 3538952 | tf_op jit(solution)/shard_map/ppermute | solution.py:339
  33.5 67.2 %collective-permute-start.1 = (bf16[2304,256]{1,0:T(8,128)(2,1)}, bf16[2304,256]{1,0:T(8,128)(2,1)}, u32[]{:S(2)}, u32[]{:S(2)}) collective-permute-start(bf16[2304,256]{1,0:T(8,128)(2,1)} %get-tuple-element.26.refs_1_), channel_id=1, source_target_pairs={{0,128},{128,256},{256,384},{384,0},{1,129},{129,257},{257,385},{3... | collective-permute-start | bytes 3538952 | tf_op jit(solution)/shard_map/ppermute | solution.py:339
  56.0 49.2 %collective-permute-start.4 = (bf16[2304,256]{1,0:T(8,128)(2,1)}, bf16[2304,256]{1,0:T(8,128)(2,1)}, u32[]{:S(2)}, u32[]{:S(2)}) collective-permute-start(bf16[2304,256]{1,0:T(8,128)(2,1)} %collective-permute-done.refs_2_), channel_id=1, source_target_pairs={{0,128},{128,256},{256,384},{384,0},{1,129},{129,257},{257,385},{3... | collective-permute-start | bytes 3538952 | tf_op jit(solution)/shard_map/ppermute | solution.py:339
  59.6 48.9 %collective-permute-start.5 = (bf16[2304,256]{1,0:T(8,128)(2,1)}, bf16[2304,256]{1,0:T(8,128)(2,1)}, u32[]{:S(2)}, u32[]{:S(2)}) collective-permute-start(bf16[2304,256]{1,0:T(8,128)(2,1)} %collective-permute-done.3.refs_5_), channel_id=1, source_target_pairs={{0,384},{128,0},{256,128},{384,256},{1,385},{129,1},{257,129},{385... | collective-permute-start | bytes 3538952 | tf_op jit(solution)/shard_map/ppermute | solution.py:339
  61.8 46.6 %copy-start.13 = (bf16[1,32,768]{2,1,0:T(8,128)(2,1)S(1)}, bf16[1,32,768]{2,1,0:T(8,128)(2,1)}, u32[]{:S(2)}) copy-start(bf16[1,32,768]{2,1,0:T(8,128)(2,1)} %down_in.3) | copy-start | bytes 147460
  98.2 10.2 %copy-start.15 = (bf16[2304,256]{1,0:T(8,128)(2,1)S(1)}, bf16[2304,256]{1,0:T(8,128)(2,1)}, u32[]{:S(2)}) copy-start(bf16[2304,256]{1,0:T(8,128)(2,1)} %get-tuple-element.25.refs_0_) | copy-start | bytes 3538948
  98.2 10.2 %copy-start.16 = (bf16[2304,256]{1,0:T(8,128)(2,1)S(1)}, bf16[2304,256]{1,0:T(8,128)(2,1)}, u32[]{:S(2)}) copy-start(bf16[2304,256]{1,0:T(8,128)(2,1)} %get-tuple-element.26.refs_1_) | copy-start | bytes 3538948
  98.2 10.2 %copy-start.17 = (bf16[1,32,768]{2,1,0:T(8,128)(2,1)S(1)}, bf16[1,32,768]{2,1,0:T(8,128)(2,1)}, u32[]{:S(2)}) copy-start(bf16[1,32,768]{2,1,0:T(8,128)(2,1)} %up_out.1) | copy-start | bytes 147460
  99.5 1.2 copy-start.2
  100.7 20.4 %copy-start = (bf16[384,2048]{1,0:T(8,128)(2,1)}, bf16[384,2048]{1,0:T(8,128)(2,1)S(1)}, u32[]{:S(2)}) copy-start(bf16[384,2048]{1,0:T(8,128)(2,1)S(1)} %get-tuple-element.20.rows_in) | copy-start | bytes 4718596
  100.7 20.4 %copy-start.11 = (bf16[384,32]{1,0:T(8,128)(2,1)}, bf16[384,32]{1,0:T(8,128)(2,1)S(1)}, u32[]{:S(2)}) copy-start(bf16[384,32]{1,0:T(8,128)(2,1)S(1)} %get-tuple-element.23.back_low) | copy-start | bytes 73732
  123.9 14.6 %copy-start.1 = (bf16[384,2048]{1,0:T(8,128)(2,1)S(1)}, bf16[384,2048]{1,0:T(8,128)(2,1)}, u32[]{:S(2)}) copy-start(bf16[384,2048]{1,0:T(8,128)(2,1)} %copy-done) | copy-start | bytes 4718596
  123.9 14.6 %copy-start.12 = (bf16[384,32]{1,0:T(8,128)(2,1)S(1)}, bf16[384,32]{1,0:T(8,128)(2,1)}, u32[]{:S(2)}) copy-start(bf16[384,32]{1,0:T(8,128)(2,1)} %copy-done.11) | copy-start | bytes 73732
  123.9 56.2 %all-to-all-start.1 = ((bf16[128,3,16,128]{3,2,1,0:T(8,128)(2,1)}), bf16[128,3,16,128]{3,2,1,0:T(8,128)(2,1)S(1)}, u32[]{:S(2)}, u32[]{:S(2)}) async-start(bf16[128,3,16,128]{3,2,1,0:T(8,128)(2,1)} %bitcast.15), calls=%async_computation.1 | async-start | bytes 3145728 | tf_op jit(solution)/shard_map/all_to_all | solution.py:382
  138.5 1.4 copy-start.3
  143.1 20.8 %collective-permute-start.8 = (bf16[32,5632]{1,0:T(8,128)(2,1)S(1)}, bf16[32,5632]{1,0:T(8,128)(2,1)S(1)}, u32[]{:S(2)}, u32[]{:S(2)}) collective-permute-start(bf16[32,5632]{1,0:T(8,128)(2,1)S(1)} %adapter_grads.1), channel_id=1, source_target_pairs={{0,384},{128,0},{256,128},{384,256},{1,385},{129,1},{257,129},{385... | collective-permute-start | bytes 1081352 | tf_op jit(solution)/shard_map/ppermute | solution.py:339
  145.3 18.5 %collective-permute-start.7 = (bf16[32,5632]{1,0:T(8,128)(2,1)S(1)}, bf16[32,5632]{1,0:T(8,128)(2,1)S(1)}, u32[]{:S(2)}, u32[]{:S(2)}) collective-permute-start(bf16[32,5632]{1,0:T(8,128)(2,1)S(1)} %adapter_grads.1), channel_id=1, source_target_pairs={{0,256},{128,384},{256,0},{384,128},{1,257},{129,385},{257,1},{385... | collective-permute-start | bytes 1081352 | tf_op jit(solution)/shard_map/ppermute | solution.py:339
  148.6 17.7 %collective-permute-start.6 = (bf16[32,5632]{1,0:T(8,128)(2,1)S(1)}, bf16[32,5632]{1,0:T(8,128)(2,1)S(1)}, u32[]{:S(2)}, u32[]{:S(2)}) collective-permute-start(bf16[32,5632]{1,0:T(8,128)(2,1)S(1)} %adapter_grads.1), channel_id=1, source_target_pairs={{0,128},{128,256},{256,384},{384,0},{1,129},{129,257},{257,385},{3... | collective-permute-start | bytes 1081352 | tf_op jit(solution)/shard_map/ppermute | solution.py:339
  166.5 13.6 %copy-start.14 = (s32[8,32]{1,0:T(8,128)S(1)}, s32[8,32]{1,0:T(8,128)}, u32[]{:S(2)}) copy-start(s32[8,32]{1,0:T(8,128)} %get-tuple-element.18.slots) | copy-start | bytes 3076
  (5 other events, 4.9 us)

commit v7 on v6

--- a/solution.py
+++ b/solution.py
@@ -8,6 +8,7 @@
 CAP = 3
 LANES = 128
 COLS = 256
+ROW_STEPS = 4
 SCALE = 2.0
 F32 = jnp.float32
 BF16 = jnp.bfloat16
@@ -194,9 +195,10 @@
     )(recv, up_in, down_out)
 
 
-def slot_kernel(rank, rows_in, rows_grad, low_up, back_low, up_in, up_out, down_in, *refs):
+def slot_kernel(rank, rows_in_far, rows_grad_far, low_up, back_low, up_in, up_out, down_in, *refs):
     owners = (refs[0:2], refs[2:4], refs[4:6], refs[6:8])
-    slot_grad, hidden, grad_up, up_low, gate_up, down, grads, slot_rows, sems = refs[8:]
+    slot_far, hidden_far, grad_up_far, up_low = refs[8:12]
+    gate_up, down, grads, slot_rows, slot_grad, hidden, grad_up, x, g, sems, out_sems = refs[12:]
     width = gate_up.shape[0]
     inner = hidden.shape[1]
     shards = len(owners)
@@ -209,7 +211,10 @@
     steps = []
     number = 0
     for c in range(chunks):
-        moves = []
+        moves = ([], [])
+        if c == 0:
+            moves[0].append((rows_in_far, x))
+            moves[1].append((rows_grad_far, g))
         for shift, pair in zip(shifts, owners):
             place = pl.multiple_of(lax.rem(mine + shift, shards) * part, part)
             for weight, block, start, height in blocks:
@@ -228,25 +233,26 @@
                             pl.ds(c * COLS + skip, rows),
                             pl.ds(pl.multiple_of(place + block * COLS, COLS), COLS),
                         ]
-                    moves.append((pair[side].at[pl.ds(at, rows), :], target))
-        copies = []
-        for source, target in moves:
-            copies.append(pltpu.make_async_copy(source, target, sems.at[number]))
-            number += 1
-        steps.append(copies)
+                    moves[weight // 2].append((pair[side].at[pl.ds(at, rows), :], target))
+        for kind in moves:
+            copies = []
+            for source, target in kind:
+                copies.append(pltpu.make_async_copy(source, target, sems.at[number]))
+                number += 1
+            steps.append(copies)
     for copies in steps:
         for copy in copies:
             copy.start()
 
-    x = rows_in
-    g = rows_grad
     for c in range(chunks):
         cols = pl.ds(c * COLS, COLS)
         later = pl.ds(inner + c * COLS, COLS)
-        for copy in steps[c]:
+        for copy in steps[2 * c]:
             copy.wait()
         gate_pre = dot(x[...], gate_up[:, cols], 1, 0)
         up_sum = dot(x[...], gate_up[:, later], 1, 0) + SCALE * dot(low_up[...], up_out[0, :, cols], 1, 0)
+        for copy in steps[2 * c + 1]:
+            copy.wait()
         grad_hidden = dot(g[...], down[cols, :], 1, 1) + SCALE * dot(
             back_low[...], down_in[0, :, cols], 1, 0
         )
@@ -259,13 +265,27 @@
         ).astype(BF16)
         grads[:, later] = up_grad
         grad_up[:, cols] = up_grad
+    stores = [
+        pltpu.make_async_copy(hidden, hidden_far, out_sems.at[0]),
+        pltpu.make_async_copy(grad_up, grad_up_far, out_sems.at[1]),
+    ]
+    for store in stores:
+        store.start()
     up_low[...] = dot(grad_up[...], up_out[0], 1, 1).astype(BF16)
     for c in range(width // COLS):
         cols = pl.ds(c * COLS, COLS)
         slot_rows[:, cols] = (
             dot(grads[...], gate_up[cols, :], 1, 1) + SCALE * dot(up_low[...], up_in[:, cols], 1, 0)
         ).astype(BF16)
-    slot_grad[...] = slot_rows[...].reshape(slot_grad.shape)
+    step = slot_grad.shape[0] // ROW_STEPS
+    for i in range(ROW_STEPS):
+        rows = pl.ds(i * step, step)
+        slot_grad[rows] = slot_rows[rows, :].reshape((step,) + slot_grad.shape[1:])
+        store = pltpu.make_async_copy(slot_grad.at[rows], slot_far.at[rows], out_sems.at[2 + i])
+        store.start()
+        stores.append(store)
+    for store in stores:
+        store.wait()
 
 
 def adapter_kernel(rows_in, rows_grad, hidden, grad_up, low_up, back_low, up_low, down_in, adapters):
@@ -296,16 +316,22 @@
             jax.ShapeDtypeStruct((rows, inner), BF16),
             jax.ShapeDtypeStruct((rows, rank), BF16),
         ),
-        in_specs=[SMEM] + [VMEM] * 7 + [HBM] * 8,
-        out_specs=(VMEM,) * 4,
+        in_specs=[SMEM, HBM, HBM] + [VMEM] * 5 + [HBM] * 8,
+        out_specs=(HBM, HBM, HBM, VMEM),
         scratch_shapes=[
             pltpu.VMEM((width, 2 * inner), BF16),
             pltpu.VMEM((inner, width), BF16),
             pltpu.VMEM((rows, 2 * inner), BF16),
             pltpu.VMEM((rows, width), BF16),
+            pltpu.VMEM((rows, width // LANES, LANES), BF16),
+            pltpu.VMEM((rows, inner), BF16),
+            pltpu.VMEM((rows, inner), BF16),
+            pltpu.VMEM((rows, width), BF16),
+            pltpu.VMEM((rows, width), BF16),
             pltpu.SemaphoreType.DMA((72,)),
+            pltpu.SemaphoreType.DMA((2 + ROW_STEPS,)),
         ],
-        compiler_params=params(40),
+        compiler_params=params(57),
         cost_estimate=pl.CostEstimate(
             flops=10 * rows * width * inner,
             bytes_accessed=6 * width * inner + 6 * rows * width,

time: 183 us -> 183 us (level)
  Pallas kernels: 23.4 us -> 26.6 us
  waiting for transfers between devices: 88.1 us -> 84.9 us
    pallas_call x1, Pallas kernels: 12.7 us -> 15.8 us  [expert_slots(): pl.pallas_call(slot_kernel, out_shape=(jax.ShapeDtypeStruct((rows, width...]
    ppermute x9, waiting for transfers between devices: 39.7 us -> 36.6 us  [shifted(): lax.ppermute(value, axis, [(i, (i + shift) % count) for i in range(count)])]
    unnamed x36 -> x32, local copies, waits for them, and re-layouts: 7.53 us -> 7.83 us
where the time goes in v7:
time: 183 us
  waiting for transfers between devices  84.9 us (46%)
  starting transfers between devices  60.8 us (33%)
  Pallas kernels  26.6 us (15%)
  local copies, waits for them, and re-layouts  9.34 us (5%)
    ppermute x9, waiting for transfers between devices, shifted(): lax.ppermute(value, axis, [(i, (i + shift) % count) for i in range(count)])  36.6 us
    all_to_all x1, waiting for transfers between devices, on_device(): lax.all_to_all(send.reshape(experts, 2 * CAP, width // LANES, LANES), ('g...  36.2 us
    ppermute x9, starting transfers between devices, shifted(): lax.ppermute(value, axis, [(i, (i + shift) % count) for i in range(count)])  28.5 us
    all_to_all x1, starting transfers between devices, on_device(): lax.all_to_all(send.reshape(experts, 2 * CAP, width // LANES, LANES), ('g...  18 us
    pallas_call x1, Pallas kernels, expert_slots(): pl.pallas_call(slot_kernel, out_shape=(jax.ShapeDtypeStruct((rows, width...  15.8 us
    all_to_all x1, starting transfers between devices, on_device(): lax.all_to_all(slot_grad.reshape(experts, CAP, width // LANES, LANES), ('...  14.4 us
    all_to_all x1, waiting for transfers between devices, on_device(): lax.all_to_all(slot_grad.reshape(experts, CAP, width // LANES, LANES), ('...  12 us
    unnamed x32, local copies, waits for them, and re-layouts  7.83 us
  transfers between devices with their start and end apart: 11, of which 7 were waited for; matrix products, arithmetic and copies ran while one was open for 1% of the time, Pallas kernels for 1%

profile of v7, /device:TPU:6, one launch (start us, length us, event | category | flops | bytes accessed | tf_op | source)
XLA Modules:
  0.0 182.6 jit_solution(18382049929948567592)
XLA Ops:
  0.6 6.2 %place_rows.1 = (bf16[768,16,128]{2,1,0:T(8,128)(2,1)}, s32[8,32]{1,0:T(8,128)}, bf16[2304,256]{1,0:T(8,128)(2,1)}, bf16[2304,256]{1,0:T(8,128)(2,1)}) custom-call(s32[8,32]{1,0:T(8,128)} %bitcast.17, f32[8,32]{1,0:T(8,128)} %bitcast.18, s32[128]{0:T(128)} %limits.1, bf16[32,2048]{1,0:T(8,128)(2,1)} %tokens.1, bf16[32,2048]{1,0:T(8,128)(2,1)} %grads.1, ...), custom_call_target="tpu_custom_call" | custom-call | tf_op jit(solution)/shard_map/place_rows/pallas_call | solution.py:109
  6.9 18.0 %all-to-all-start = ((bf16[128,6,16,128]{3,2,1,0:T(8,128)(2,1)}), bf16[128,6,16,128]{3,2,1,0:T(8,128)(2,1)S(1)}, u32[]{:S(2)}, u32[]{:S(2)}) async-start(bf16[128,6,16,128]{3,2,1,0:T(8,128)(2,1)} %bitcast.15), calls=%async_computation | async-start | bytes 6291456 | tf_op jit(solution)/shard_map/all_to_all | solution.py:397
  24.9 2.4 %collective-permute-start = (bf16[2304,256]{1,0:T(8,128)(2,1)}, bf16[2304,256]{1,0:T(8,128)(2,1)}, u32[]{:S(2)}, u32[]{:S(2)}) collective-permute-start(bf16[2304,256]{1,0:T(8,128)(2,1)} %get-tuple-element.25.refs_0_), channel_id=1, source_target_pairs={{0,128},{128,256},{256,384},{384,0},{1,129},{129,257},{257,385},{3... | collective-permute-start | bytes 3538952 | tf_op jit(solution)/shard_map/ppermute | solution.py:365
  27.3 3.5 %collective-permute-start.3 = (bf16[2304,256]{1,0:T(8,128)(2,1)}, bf16[2304,256]{1,0:T(8,128)(2,1)}, u32[]{:S(2)}, u32[]{:S(2)}) collective-permute-start(bf16[2304,256]{1,0:T(8,128)(2,1)} %get-tuple-element.26.refs_1_), channel_id=1, source_target_pairs={{0,384},{128,0},{256,128},{384,256},{1,385},{129,1},{257,129},{385... | collective-permute-start | bytes 3538952 | tf_op jit(solution)/shard_map/ppermute | solution.py:365
  30.7 2.7 %collective-permute-start.2 = (bf16[2304,256]{1,0:T(8,128)(2,1)}, bf16[2304,256]{1,0:T(8,128)(2,1)}, u32[]{:S(2)}, u32[]{:S(2)}) collective-permute-start(bf16[2304,256]{1,0:T(8,128)(2,1)} %get-tuple-element.25.refs_0_), channel_id=1, source_target_pairs={{0,384},{128,0},{256,128},{384,256},{1,385},{129,1},{257,129},{385... | collective-permute-start | bytes 3538952 | tf_op jit(solution)/shard_map/ppermute | solution.py:365
  33.5 4.3 %collective-permute-start.1 = (bf16[2304,256]{1,0:T(8,128)(2,1)}, bf16[2304,256]{1,0:T(8,128)(2,1)}, u32[]{:S(2)}, u32[]{:S(2)}) collective-permute-start(bf16[2304,256]{1,0:T(8,128)(2,1)} %get-tuple-element.26.refs_1_), channel_id=1, source_target_pairs={{0,128},{128,256},{256,384},{384,0},{1,129},{129,257},{257,385},{3... | collective-permute-start | bytes 3538952 | tf_op jit(solution)/shard_map/ppermute | solution.py:365
  37.8 18.2 %collective-permute-done.refs_2_ = bf16[2304,256]{1,0:T(8,128)(2,1)} collective-permute-done((bf16[2304,256]{1,0:T(8,128)(2,1)}, bf16[2304,256]{1,0:T(8,128)(2,1)}, u32[]{:S(2)}, u32[]{:S(2)}) %collective-permute-start) | collective-permute-done | bytes 1179680 | tf_op jit(solution)/shard_map/ppermute | solution.py:365
  56.0 3.6 %collective-permute-start.4 = (bf16[2304,256]{1,0:T(8,128)(2,1)}, bf16[2304,256]{1,0:T(8,128)(2,1)}, u32[]{:S(2)}, u32[]{:S(2)}) collective-permute-start(bf16[2304,256]{1,0:T(8,128)(2,1)} %collective-permute-done.refs_2_), channel_id=1, source_target_pairs={{0,128},{128,256},{256,384},{384,0},{1,129},{129,257},{257,385},{3... | collective-permute-start | bytes 3538952 | tf_op jit(solution)/shard_map/ppermute | solution.py:365
  59.6 2.4 %collective-permute-start.5 = (bf16[2304,256]{1,0:T(8,128)(2,1)}, bf16[2304,256]{1,0:T(8,128)(2,1)}, u32[]{:S(2)}, u32[]{:S(2)}) collective-permute-start(bf16[2304,256]{1,0:T(8,128)(2,1)} %collective-permute-done.3.refs_5_), channel_id=1, source_target_pairs={{0,384},{128,0},{256,128},{384,256},{1,385},{129,1},{257,129},{385... | collective-permute-start | bytes 3538952 | tf_op jit(solution)/shard_map/ppermute | solution.py:365
  62.0 36.2 %all-to-all-done.recv = bf16[128,6,16,128]{3,2,1,0:T(8,128)(2,1)S(1)} async-done(((bf16[128,6,16,128]{3,2,1,0:T(8,128)(2,1)}), bf16[128,6,16,128]{3,2,1,0:T(8,128)(2,1)S(1)}, u32[]{:S(2)}, u32[]{:S(2)}) %all-to-all-start) | async-done | bytes 3145760 | tf_op jit(solution)/shard_map/all_to_all | solution.py:397
  98.2 1.2 low_products.1
  99.5 1.2 copy-done
  103.8 1.4 collective-permute-done.4.refs_6_
  105.1 3.3 %collective-permute-done.5.refs_7_ = bf16[2304,256]{1,0:T(8,128)(2,1)} collective-permute-done((bf16[2304,256]{1,0:T(8,128)(2,1)}, bf16[2304,256]{1,0:T(8,128)(2,1)}, u32[]{:S(2)}, u32[]{:S(2)}) %collective-permute-start.5) | collective-permute-done | bytes 1179680 | tf_op jit(solution)/shard_map/ppermute | solution.py:365
  108.4 15.8 %expert_slots.1 = (bf16[384,16,128]{2,1,0:T(8,128)(2,1)}, bf16[384,768]{1,0:T(8,128)(2,1)}, bf16[384,768]{1,0:T(8,128)(2,1)}, bf16[384,32]{1,0:T(8,128)(2,1)}) custom-call(s32[1]{0:T(128)} %bitcast.2.rank, bf16[384,2048]{1,0:T(8,128)(2,1)} %copy-done, bf16[384,2048]{1,0:T(8,128)(2,1)} %copy-done.2, bf16[384,32]{1,0:T(8,128)(2,1)} %copy-done.8, ...), custom_call_target="tpu_custom_call" | custom-call | flops 6039797760 | bytes 14155776 | tf_op jit(solution)/shard_map/expert_slots/pallas_call | solution.py:311
  124.4 14.4 %all-to-all-start.1 = ((bf16[128,3,16,128]{3,2,1,0:T(8,128)(2,1)}), bf16[128,3,16,128]{3,2,1,0:T(8,128)(2,1)S(1)}, u32[]{:S(2)}, u32[]{:S(2)}) async-start(bf16[128,3,16,128]{3,2,1,0:T(8,128)(2,1)} %bitcast.16), calls=%async_computation.1 | async-start | bytes 3145728 | tf_op jit(solution)/shard_map/all_to_all | solution.py:408
  138.8 1.4 copy-done.3
  143.4 2.2 %collective-permute-start.8 = (bf16[32,5632]{1,0:T(8,128)(2,1)S(1)}, bf16[32,5632]{1,0:T(8,128)(2,1)S(1)}, u32[]{:S(2)}, u32[]{:S(2)}) collective-permute-start(bf16[32,5632]{1,0:T(8,128)(2,1)S(1)} %adapter_grads.1), channel_id=1, source_target_pairs={{0,384},{128,0},{256,128},{384,256},{1,385},{129,1},{257,129},{385... | collective-permute-start | bytes 1081352 | tf_op jit(solution)/shard_map/ppermute | solution.py:365
  145.6 3.3 %collective-permute-start.7 = (bf16[32,5632]{1,0:T(8,128)(2,1)S(1)}, bf16[32,5632]{1,0:T(8,128)(2,1)S(1)}, u32[]{:S(2)}, u32[]{:S(2)}) collective-permute-start(bf16[32,5632]{1,0:T(8,128)(2,1)S(1)} %adapter_grads.1), channel_id=1, source_target_pairs={{0,256},{128,384},{256,0},{384,128},{1,257},{129,385},{257,1},{385... | collective-permute-start | bytes 1081352 | tf_op jit(solution)/shard_map/ppermute | solution.py:365
  148.9 4.0 %collective-permute-start.6 = (bf16[32,5632]{1,0:T(8,128)(2,1)S(1)}, bf16[32,5632]{1,0:T(8,128)(2,1)S(1)}, u32[]{:S(2)}, u32[]{:S(2)}) collective-permute-start(bf16[32,5632]{1,0:T(8,128)(2,1)S(1)} %adapter_grads.1), channel_id=1, source_target_pairs={{0,128},{128,256},{256,384},{384,0},{1,129},{129,257},{257,385},{3... | collective-permute-start | bytes 1081352 | tf_op jit(solution)/shard_map/ppermute | solution.py:365
  152.9 11.2 %collective-permute-done.8 = bf16[32,5632]{1,0:T(8,128)(2,1)S(1)} collective-permute-done((bf16[32,5632]{1,0:T(8,128)(2,1)S(1)}, bf16[32,5632]{1,0:T(8,128)(2,1)S(1)}, u32[]{:S(2)}, u32[]{:S(2)}) %collective-permute-start.8) | collective-permute-done | bytes 360480 | tf_op jit(solution)/shard_map/ppermute | solution.py:365
  164.1 2.5 %collective-permute-done.6 = bf16[32,5632]{1,0:T(8,128)(2,1)S(1)} collective-permute-done((bf16[32,5632]{1,0:T(8,128)(2,1)S(1)}, bf16[32,5632]{1,0:T(8,128)(2,1)S(1)}, u32[]{:S(2)}, u32[]{:S(2)}) %collective-permute-start.6) | collective-permute-done | bytes 360480 | tf_op jit(solution)/shard_map/ppermute | solution.py:365
  168.3 12.0 %all-to-all-done.1 = bf16[128,3,16,128]{3,2,1,0:T(8,128)(2,1)S(1)} async-done(((bf16[128,3,16,128]{3,2,1,0:T(8,128)(2,1)}), bf16[128,3,16,128]{3,2,1,0:T(8,128)(2,1)S(1)}, u32[]{:S(2)}, u32[]{:S(2)}) %all-to-all-start.1) | async-done | bytes 1572896 | tf_op jit(solution)/shard_map/all_to_all | solution.py:408
  180.4 2.2 %combine_rows.1 = bf16[32,2048]{1,0:T(8,128)(2,1)} custom-call(s32[8,32]{1,0:T(8,128)S(1)} %copy-done.14, bf16[384,16,128]{2,1,0:T(8,128)(2,1)S(1)} %bitcast.14), custom_call_target="tpu_custom_call" | custom-call | tf_op jit(solution)/shard_map/combine_rows/pallas_call | solution.py:149
  (38 shorter events, 8.0 us)
Async XLA Ops:
  6.9 91.4 %copy-start.6 = (bf16[1,32,2048]{2,1,0:T(8,128)(2,1)S(1)}, bf16[1,32,2048]{2,1,0:T(8,128)(2,1)}, u32[]{:S(2)}) copy-start(bf16[1,32,2048]{2,1,0:T(8,128)(2,1)} %up_in.1) | copy-start | bytes 393220
  6.9 91.4 %copy-start.7 = (bf16[1,32,2048]{2,1,0:T(8,128)(2,1)S(1)}, bf16[1,32,2048]{2,1,0:T(8,128)(2,1)}, u32[]{:S(2)}) copy-start(bf16[1,32,2048]{2,1,0:T(8,128)(2,1)} %down_out.1) | copy-start | bytes 393220
  6.9 91.3 %all-to-all-start = ((bf16[128,6,16,128]{3,2,1,0:T(8,128)(2,1)}), bf16[128,6,16,128]{3,2,1,0:T(8,128)(2,1)S(1)}, u32[]{:S(2)}, u32[]{:S(2)}) async-start(bf16[128,6,16,128]{3,2,1,0:T(8,128)(2,1)} %bitcast.15), calls=%async_computation | async-start | bytes 6291456 | tf_op jit(solution)/shard_map/all_to_all | solution.py:397
  24.9 31.1 %collective-permute-start = (bf16[2304,256]{1,0:T(8,128)(2,1)}, bf16[2304,256]{1,0:T(8,128)(2,1)}, u32[]{:S(2)}, u32[]{:S(2)}) collective-permute-start(bf16[2304,256]{1,0:T(8,128)(2,1)} %get-tuple-element.25.refs_0_), channel_id=1, source_target_pairs={{0,128},{128,256},{256,384},{384,0},{1,129},{129,257},{257,385},{3... | collective-permute-start | bytes 3538952 | tf_op jit(solution)/shard_map/ppermute | solution.py:365
  27.3 32.3 %collective-permute-start.3 = (bf16[2304,256]{1,0:T(8,128)(2,1)}, bf16[2304,256]{1,0:T(8,128)(2,1)}, u32[]{:S(2)}, u32[]{:S(2)}) collective-permute-start(bf16[2304,256]{1,0:T(8,128)(2,1)} %get-tuple-element.26.refs_1_), channel_id=1, source_target_pairs={{0,384},{128,0},{256,128},{384,256},{1,385},{129,1},{257,129},{385... | collective-permute-start | bytes 3538952 | tf_op jit(solution)/shard_map/ppermute | solution.py:365
  30.7 73.0 %collective-permute-start.2 = (bf16[2304,256]{1,0:T(8,128)(2,1)}, bf16[2304,256]{1,0:T(8,128)(2,1)}, u32[]{:S(2)}, u32[]{:S(2)}) collective-permute-start(bf16[2304,256]{1,0:T(8,128)(2,1)} %get-tuple-element.25.refs_0_), channel_id=1, source_target_pairs={{0,384},{128,0},{256,128},{384,256},{1,385},{129,1},{257,129},{385... | collective-permute-start | bytes 3538952 | tf_op jit(solution)/shard_map/ppermute | solution.py:365
  33.5 70.3 %collective-permute-start.1 = (bf16[2304,256]{1,0:T(8,128)(2,1)}, bf16[2304,256]{1,0:T(8,128)(2,1)}, u32[]{:S(2)}, u32[]{:S(2)}) collective-permute-start(bf16[2304,256]{1,0:T(8,128)(2,1)} %get-tuple-element.26.refs_1_), channel_id=1, source_target_pairs={{0,128},{128,256},{256,384},{384,0},{1,129},{129,257},{257,385},{3... | collective-permute-start | bytes 3538952 | tf_op jit(solution)/shard_map/ppermute | solution.py:365
  56.0 49.2 %collective-permute-start.4 = (bf16[2304,256]{1,0:T(8,128)(2,1)}, bf16[2304,256]{1,0:T(8,128)(2,1)}, u32[]{:S(2)}, u32[]{:S(2)}) collective-permute-start(bf16[2304,256]{1,0:T(8,128)(2,1)} %collective-permute-done.refs_2_), channel_id=1, source_target_pairs={{0,128},{128,256},{256,384},{384,0},{1,129},{129,257},{257,385},{3... | collective-permute-start | bytes 3538952 | tf_op jit(solution)/shard_map/ppermute | solution.py:365
  59.6 48.9 %collective-permute-start.5 = (bf16[2304,256]{1,0:T(8,128)(2,1)}, bf16[2304,256]{1,0:T(8,128)(2,1)}, u32[]{:S(2)}, u32[]{:S(2)}) collective-permute-start(bf16[2304,256]{1,0:T(8,128)(2,1)} %collective-permute-done.3.refs_5_), channel_id=1, source_target_pairs={{0,384},{128,0},{256,128},{384,256},{1,385},{129,1},{257,129},{385... | collective-permute-start | bytes 3538952 | tf_op jit(solution)/shard_map/ppermute | solution.py:365
  99.5 1.2 copy-start
  100.7 1.1 copy-start.2
  124.3 14.5 %copy-start.1 = (bf16[384,2048]{1,0:T(8,128)(2,1)S(1)}, bf16[384,2048]{1,0:T(8,128)(2,1)}, u32[]{:S(2)}) copy-start(bf16[384,2048]{1,0:T(8,128)(2,1)} %copy-done) | copy-start | bytes 4718596
  124.3 14.5 %copy-start.9 = (bf16[384,32]{1,0:T(8,128)(2,1)S(1)}, bf16[384,32]{1,0:T(8,128)(2,1)}, u32[]{:S(2)}) copy-start(bf16[384,32]{1,0:T(8,128)(2,1)} %copy-done.8) | copy-start | bytes 73732
  124.3 14.5 %copy-start.11 = (bf16[384,32]{1,0:T(8,128)(2,1)S(1)}, bf16[384,32]{1,0:T(8,128)(2,1)}, u32[]{:S(2)}) copy-start(bf16[384,32]{1,0:T(8,128)(2,1)} %copy-done.10) | copy-start | bytes 73732
  124.3 14.5 %copy-start.12 = (bf16[384,32]{1,0:T(8,128)(2,1)S(1)}, bf16[384,32]{1,0:T(8,128)(2,1)}, u32[]{:S(2)}) copy-start(bf16[384,32]{1,0:T(8,128)(2,1)} %get-tuple-element.30.up_low) | copy-start | bytes 73732
  124.3 14.5 %copy-start.13 = (bf16[1,32,768]{2,1,0:T(8,128)(2,1)S(1)}, bf16[1,32,768]{2,1,0:T(8,128)(2,1)}, u32[]{:S(2)}) copy-start(bf16[1,32,768]{2,1,0:T(8,128)(2,1)} %down_in.3) | copy-start | bytes 147460
  124.4 56.0 %all-to-all-start.1 = ((bf16[128,3,16,128]{3,2,1,0:T(8,128)(2,1)}), bf16[128,3,16,128]{3,2,1,0:T(8,128)(2,1)S(1)}, u32[]{:S(2)}, u32[]{:S(2)}) async-start(bf16[128,3,16,128]{3,2,1,0:T(8,128)(2,1)} %bitcast.16), calls=%async_computation.1 | async-start | bytes 3145728 | tf_op jit(solution)/shard_map/all_to_all | solution.py:408
  138.8 1.4 copy-start.3
  140.2 1.1 copy-start.4
  141.3 1.1 copy-start.5
  143.4 20.8 %collective-permute-start.8 = (bf16[32,5632]{1,0:T(8,128)(2,1)S(1)}, bf16[32,5632]{1,0:T(8,128)(2,1)S(1)}, u32[]{:S(2)}, u32[]{:S(2)}) collective-permute-start(bf16[32,5632]{1,0:T(8,128)(2,1)S(1)} %adapter_grads.1), channel_id=1, source_target_pairs={{0,384},{128,0},{256,128},{384,256},{1,385},{129,1},{257,129},{385... | collective-permute-start | bytes 1081352 | tf_op jit(solution)/shard_map/ppermute | solution.py:365
  145.6 18.5 %collective-permute-start.7 = (bf16[32,5632]{1,0:T(8,128)(2,1)S(1)}, bf16[32,5632]{1,0:T(8,128)(2,1)S(1)}, u32[]{:S(2)}, u32[]{:S(2)}) collective-permute-start(bf16[32,5632]{1,0:T(8,128)(2,1)S(1)} %adapter_grads.1), channel_id=1, source_target_pairs={{0,256},{128,384},{256,0},{384,128},{1,257},{129,385},{257,1},{385... | collective-permute-start | bytes 1081352 | tf_op jit(solution)/shard_map/ppermute | solution.py:365
  148.9 17.7 %collective-permute-start.6 = (bf16[32,5632]{1,0:T(8,128)(2,1)S(1)}, bf16[32,5632]{1,0:T(8,128)(2,1)S(1)}, u32[]{:S(2)}, u32[]{:S(2)}) collective-permute-start(bf16[32,5632]{1,0:T(8,128)(2,1)S(1)} %adapter_grads.1), channel_id=1, source_target_pairs={{0,128},{128,256},{256,384},{384,0},{1,129},{129,257},{257,385},{3... | collective-permute-start | bytes 1081352 | tf_op jit(solution)/shard_map/ppermute | solution.py:365
  166.8 13.6 %copy-start.14 = (s32[8,32]{1,0:T(8,128)S(1)}, s32[8,32]{1,0:T(8,128)}, u32[]{:S(2)}) copy-start(s32[8,32]{1,0:T(8,128)} %get-tuple-element.18.slots) | copy-start | bytes 3076
  (3 other events, 1.9 us)

commit v8 on v6

--- a/solution.py
+++ b/solution.py
@@ -69,16 +69,6 @@
         return carry
 
     lax.fori_loop(0, limits.shape[0], clear, 0, unroll=8)
-    for load in loads:
-        load.wait()
-    half = packed.shape[0] // 2
-    stores = [
-        pltpu.make_async_copy(packed.at[pl.ds(i * half, half), :], halves[i], sems.at[len(blocks) + i])
-        for i in range(2)
-    ]
-    for store in stores:
-        store.start()
-
     def one_token(t, carry):
         row = token_rows[t]
         grad = grad_rows[t].astype(F32)
@@ -93,7 +83,18 @@
             staged[place + CAP] = (prob[k, t] * grad).astype(BF16)
         return carry
 
-    lax.fori_loop(0, routes.shape[1], one_token, 0)
+    tokens_here = routes.shape[1]
+    lax.fori_loop(0, tokens_here // 2, one_token, 0)
+    for load in loads:
+        load.wait()
+    half = packed.shape[0] // 2
+    stores = [
+        pltpu.make_async_copy(packed.at[pl.ds(i * half, half), :], halves[i], sems.at[len(blocks) + i])
+        for i in range(2)
+    ]
+    for store in stores:
+        store.start()
+    lax.fori_loop(tokens_here // 2, tokens_here, one_token, 0)
     send[...] = staged[0:total]
     for store in stores:
         store.wait()
@@ -138,7 +139,7 @@
         rows[t] = total.astype(BF16)
         return carry
 
-    lax.fori_loop(0, slots.shape[1], one_token, 0)
+    lax.fori_loop(0, slots.shape[1], one_token, 0, unroll=2)
     out[...] = rows[...].reshape(out.shape)
 
 
@@ -196,7 +197,7 @@
 
 def slot_kernel(rank, rows_in, rows_grad, low_up, back_low, up_in, up_out, down_in, *refs):
     owners = (refs[0:2], refs[2:4], refs[4:6], refs[6:8])
-    slot_grad, hidden, grad_up, up_low, gate_up, down, grads, slot_rows, sems = refs[8:]
+    slot_grad, adapters, hidden, grad_up, up_low, gate_up, down, grads, slot_rows, sems = refs[8:]
     width = gate_up.shape[0]
     inner = hidden.shape[1]
     shards = len(owners)
@@ -266,15 +267,11 @@
             dot(grads[...], gate_up[cols, :], 1, 1) + SCALE * dot(up_low[...], up_in[:, cols], 1, 0)
         ).astype(BF16)
     slot_grad[...] = slot_rows[...].reshape(slot_grad.shape)
-
-
-def adapter_kernel(rows_in, rows_grad, hidden, grad_up, low_up, back_low, up_low, down_in, adapters):
-    width, inner = rows_in.shape[1], hidden.shape[1]
     low_down = dot(hidden[...], down_in[0], 1, 1).astype(BF16)
     at = 0
     for left, right in (
-        (up_low[...], rows_in),
-        (low_down, rows_grad),
+        (up_low[...], x),
+        (low_down, g),
         (low_up[...], grad_up),
         (back_low[...], hidden),
     ):
@@ -292,13 +289,14 @@
         slot_kernel,
         out_shape=(
             jax.ShapeDtypeStruct((rows, width // LANES, LANES), BF16),
-            jax.ShapeDtypeStruct((rows, inner), BF16),
-            jax.ShapeDtypeStruct((rows, inner), BF16),
-            jax.ShapeDtypeStruct((rows, rank), BF16),
+            jax.ShapeDtypeStruct((rank, 2 * (width + inner)), BF16),
         ),
         in_specs=[SMEM] + [VMEM] * 7 + [HBM] * 8,
-        out_specs=(VMEM,) * 4,
+        out_specs=(VMEM,) * 2,
         scratch_shapes=[
+            pltpu.VMEM((rows, inner), BF16),
+            pltpu.VMEM((rows, inner), BF16),
+            pltpu.VMEM((rows, rank), BF16),
             pltpu.VMEM((width, 2 * inner), BF16),
             pltpu.VMEM((inner, width), BF16),
             pltpu.VMEM((rows, 2 * inner), BF16),
@@ -315,25 +313,6 @@
     )(mine, rows_in, rows_grad, low_up, back_low, up_in, up_out, down_in, *weights)
 
 
-def adapter_grads(rows_in, rows_grad, hidden, grad_up, low_up, back_low, up_low, down_in):
-    rows, width = rows_in.shape
-    inner = hidden.shape[1]
-    rank = up_low.shape[1]
-    return pl.pallas_call(
-        adapter_kernel,
-        out_shape=jax.ShapeDtypeStruct((rank, 2 * (width + inner)), BF16),
-        in_specs=[VMEM] * 8,
-        out_specs=VMEM,
-        compiler_params=params(24),
-        cost_estimate=pl.CostEstimate(
-            flops=4 * rows * rank * (width + inner),
-            bytes_accessed=4 * rows * (width + inner),
-            transcendentals=0,
-        ),
-        name="adapter_grads",
-    )(rows_in, rows_grad, hidden, grad_up, low_up, back_low, up_low, down_in)
-
-
 def shifted(value, axis, shift):
     count = lax.axis_size(axis)
     return lax.ppermute(value, axis, [(i, (i + shift) % count) for i in range(count)])
@@ -373,12 +352,10 @@
         ("grp", "exp"), split_axis=0, concat_axis=0, tiled=True,
     )
     rows_in, rows_grad, low_up, back_low, up_in = low_products(recv, up_in, down_out)
-    slot_grad, hidden, grad_up, up_low = expert_slots(
+    slot_grad, adapters = expert_slots(
         rows_in, rows_grad, weights, low_up, back_low, up_in, up_out, down_in
     )
-    adapters = replica_sum(
-        adapter_grads(rows_in, rows_grad, hidden, grad_up, low_up, back_low, up_low, down_in), "rep"
-    )
+    adapters = replica_sum(adapters, "rep")
     back = lax.all_to_all(
         slot_grad.reshape(experts, CAP, width // LANES, LANES),
         ("grp", "exp"), split_axis=0, concat_axis=0, tiled=True,

time: 183 us -> 181 us (0.989)
  local copies, waits for them, and re-layouts: 9.05 us -> 2.72 us
  waiting for transfers between devices: 88.1 us -> 92.5 us
    unnamed x36 -> x16, local copies, waits for them, and re-layouts: 7.53 us -> 1.2 us
    all_to_all x1, waiting for transfers between devices: 12.1 us -> 16.6 us  [on_device(): lax.all_to_all(slot_grad.reshape(experts, CAP, width // LANES, LANES), ('...]
where the time goes in v8:
time: 181 us; the launch traced here: 180 us
  waiting for transfers between devices  92.5 us (51%)
  starting transfers between devices  60.7 us (34%)
  Pallas kernels  23.2 us (13%)
  local copies, waits for them, and re-layouts  2.72 us (2%)
    ppermute x9, waiting for transfers between devices, shifted(): lax.ppermute(value, axis, [(i, (i + shift) % count) for i in range(count)])  39.7 us
    all_to_all x1, waiting for transfers between devices, on_device(): lax.all_to_all(send.reshape(experts, 2 * CAP, width // LANES, LANES), ('g...  36.2 us
    ppermute x9, starting transfers between devices, shifted(): lax.ppermute(value, axis, [(i, (i + shift) % count) for i in range(count)])  28.5 us
    all_to_all x1, starting transfers between devices, on_device(): lax.all_to_all(send.reshape(experts, 2 * CAP, width // LANES, LANES), ('g...  18 us
    all_to_all x1, waiting for transfers between devices, on_device(): lax.all_to_all(slot_grad.reshape(experts, CAP, width // LANES, LANES), ('...  16.6 us
    all_to_all x1, starting transfers between devices, on_device(): lax.all_to_all(slot_grad.reshape(experts, CAP, width // LANES, LANES), ('...  14.3 us
    pallas_call x1, Pallas kernels, expert_slots(): pl.pallas_call(slot_kernel, out_shape=(jax.ShapeDtypeStruct((rows, width...  14.1 us
    pallas_call x1, Pallas kernels, place_rows(): pl.pallas_call(place_kernel, out_shape=(jax.ShapeDtypeStruct((total, subs...  5.76 us
  transfers between devices with their start and end apart: 11, of which 7 were waited for; matrix products, arithmetic and copies ran while one was open for 1% of the time, Pallas kernels for 1%

profile of v8, /device:TPU:6, one launch (start us, length us, event | category | flops | bytes accessed | tf_op | source)
XLA Modules:
  0.0 180.1 jit_solution(9825085516080486229)
XLA Ops:
  0.6 5.8 %place_rows.1 = (bf16[768,16,128]{2,1,0:T(8,128)(2,1)}, s32[8,32]{1,0:T(8,128)}, bf16[2304,256]{1,0:T(8,128)(2,1)}, bf16[2304,256]{1,0:T(8,128)(2,1)}) custom-call(s32[8,32]{1,0:T(8,128)} %bitcast.16, f32[8,32]{1,0:T(8,128)} %bitcast.17, s32[128]{0:T(128)} %limits.1, bf16[32,2048]{1,0:T(8,128)(2,1)} %tokens.1, bf16[32,2048]{1,0:T(8,128)(2,1)} %grads.1, ...), custom_call_target="tpu_custom_call" | custom-call | tf_op jit(solution)/shard_map/place_rows/pallas_call | solution.py:109
  6.4 18.0 %all-to-all-start = ((bf16[128,6,16,128]{3,2,1,0:T(8,128)(2,1)}), bf16[128,6,16,128]{3,2,1,0:T(8,128)(2,1)S(1)}, u32[]{:S(2)}, u32[]{:S(2)}) async-start(bf16[128,6,16,128]{3,2,1,0:T(8,128)(2,1)} %bitcast.15), calls=%async_computation | async-start | bytes 6291456 | tf_op jit(solution)/shard_map/all_to_all | solution.py:350
  24.4 2.4 %collective-permute-start = (bf16[2304,256]{1,0:T(8,128)(2,1)}, bf16[2304,256]{1,0:T(8,128)(2,1)}, u32[]{:S(2)}, u32[]{:S(2)}) collective-permute-start(bf16[2304,256]{1,0:T(8,128)(2,1)} %get-tuple-element.23.refs_0_), channel_id=1, source_target_pairs={{0,128},{128,256},{256,384},{384,0},{1,129},{129,257},{257,385},{3... | collective-permute-start | bytes 3538952 | tf_op jit(solution)/shard_map/ppermute | solution.py:318
  26.8 3.5 %collective-permute-start.3 = (bf16[2304,256]{1,0:T(8,128)(2,1)}, bf16[2304,256]{1,0:T(8,128)(2,1)}, u32[]{:S(2)}, u32[]{:S(2)}) collective-permute-start(bf16[2304,256]{1,0:T(8,128)(2,1)} %get-tuple-element.24.refs_1_), channel_id=1, source_target_pairs={{0,384},{128,0},{256,128},{384,256},{1,385},{129,1},{257,129},{385... | collective-permute-start | bytes 3538952 | tf_op jit(solution)/shard_map/ppermute | solution.py:318
  30.2 2.7 %collective-permute-start.2 = (bf16[2304,256]{1,0:T(8,128)(2,1)}, bf16[2304,256]{1,0:T(8,128)(2,1)}, u32[]{:S(2)}, u32[]{:S(2)}) collective-permute-start(bf16[2304,256]{1,0:T(8,128)(2,1)} %get-tuple-element.23.refs_0_), channel_id=1, source_target_pairs={{0,384},{128,0},{256,128},{384,256},{1,385},{129,1},{257,129},{385... | collective-permute-start | bytes 3538952 | tf_op jit(solution)/shard_map/ppermute | solution.py:318
  33.0 4.3 %collective-permute-start.1 = (bf16[2304,256]{1,0:T(8,128)(2,1)}, bf16[2304,256]{1,0:T(8,128)(2,1)}, u32[]{:S(2)}, u32[]{:S(2)}) collective-permute-start(bf16[2304,256]{1,0:T(8,128)(2,1)} %get-tuple-element.24.refs_1_), channel_id=1, source_target_pairs={{0,128},{128,256},{256,384},{384,0},{1,129},{129,257},{257,385},{3... | collective-permute-start | bytes 3538952 | tf_op jit(solution)/shard_map/ppermute | solution.py:318
  37.3 18.2 %collective-permute-done.refs_2_ = bf16[2304,256]{1,0:T(8,128)(2,1)} collective-permute-done((bf16[2304,256]{1,0:T(8,128)(2,1)}, bf16[2304,256]{1,0:T(8,128)(2,1)}, u32[]{:S(2)}, u32[]{:S(2)}) %collective-permute-start) | collective-permute-done | bytes 1179680 | tf_op jit(solution)/shard_map/ppermute | solution.py:318
  55.5 3.6 %collective-permute-start.4 = (bf16[2304,256]{1,0:T(8,128)(2,1)}, bf16[2304,256]{1,0:T(8,128)(2,1)}, u32[]{:S(2)}, u32[]{:S(2)}) collective-permute-start(bf16[2304,256]{1,0:T(8,128)(2,1)} %collective-permute-done.refs_2_), channel_id=1, source_target_pairs={{0,128},{128,256},{256,384},{384,0},{1,129},{129,257},{257,385},{3... | collective-permute-start | bytes 3538952 | tf_op jit(solution)/shard_map/ppermute | solution.py:318
  59.1 2.4 %collective-permute-start.5 = (bf16[2304,256]{1,0:T(8,128)(2,1)}, bf16[2304,256]{1,0:T(8,128)(2,1)}, u32[]{:S(2)}, u32[]{:S(2)}) collective-permute-start(bf16[2304,256]{1,0:T(8,128)(2,1)} %collective-permute-done.3.refs_5_), channel_id=1, source_target_pairs={{0,384},{128,0},{256,128},{384,256},{1,385},{129,1},{257,129},{385... | collective-permute-start | bytes 3538952 | tf_op jit(solution)/shard_map/ppermute | solution.py:318
  61.6 36.2 %all-to-all-done.recv = bf16[128,6,16,128]{3,2,1,0:T(8,128)(2,1)S(1)} async-done(((bf16[128,6,16,128]{3,2,1,0:T(8,128)(2,1)}), bf16[128,6,16,128]{3,2,1,0:T(8,128)(2,1)S(1)}, u32[]{:S(2)}, u32[]{:S(2)}) %all-to-all-start) | async-done | bytes 3145760 | tf_op jit(solution)/shard_map/all_to_all | solution.py:350
  97.8 1.2 low_products.1
  99.0 1.2 copy-done.3
  100.2 4.4 %collective-permute-done.4.refs_6_ = bf16[2304,256]{1,0:T(8,128)(2,1)} collective-permute-done((bf16[2304,256]{1,0:T(8,128)(2,1)}, bf16[2304,256]{1,0:T(8,128)(2,1)}, u32[]{:S(2)}, u32[]{:S(2)}) %collective-permute-start.4) | collective-permute-done | bytes 1179680 | tf_op jit(solution)/shard_map/ppermute | solution.py:318
  104.6 3.3 %collective-permute-done.5.refs_7_ = bf16[2304,256]{1,0:T(8,128)(2,1)} collective-permute-done((bf16[2304,256]{1,0:T(8,128)(2,1)}, bf16[2304,256]{1,0:T(8,128)(2,1)}, u32[]{:S(2)}, u32[]{:S(2)}) %collective-permute-start.5) | collective-permute-done | bytes 1179680 | tf_op jit(solution)/shard_map/ppermute | solution.py:318
  108.0 14.1 %expert_slots.1 = (bf16[384,16,128]{2,1,0:T(8,128)(2,1)}, bf16[32,5632]{1,0:T(8,128)(2,1)S(1)}) custom-call(s32[1]{0:T(128)} %bitcast.2.rank, bf16[384,2048]{1,0:T(8,128)(2,1)S(1)} %get-tuple-element.18.rows_in, bf16[384,2048]{1,0:T(8,128)(2,1)} %copy-done.3, bf16[384,32]{1,0:T(8,128)(2,1)S(1)} %get-tuple-element.20.low_up, ...), custom_call_target="tpu_custom_call" | custom-call | flops 6039797760 | bytes 14155776 | tf_op jit(solution)/shard_map/expert_slots/pallas_call | solution.py:288
  122.1 14.3 %all-to-all-start.1 = ((bf16[128,3,16,128]{3,2,1,0:T(8,128)(2,1)}), bf16[128,3,16,128]{3,2,1,0:T(8,128)(2,1)S(1)}, u32[]{:S(2)}, u32[]{:S(2)}) async-start(bf16[128,3,16,128]{3,2,1,0:T(8,128)(2,1)} %bitcast.4), calls=%async_computation.1 | async-start | bytes 3145728 | tf_op jit(solution)/shard_map/all_to_all | solution.py:359
  136.4 2.2 %collective-permute-start.8 = (bf16[32,5632]{1,0:T(8,128)(2,1)S(1)}, bf16[32,5632]{1,0:T(8,128)(2,1)S(1)}, u32[]{:S(2)}, u32[]{:S(2)}) collective-permute-start(bf16[32,5632]{1,0:T(8,128)(2,1)S(1)} %get-tuple-element.26), channel_id=1, source_target_pairs={{0,384},{128,0},{256,128},{384,256},{1,385},{129,1},{257,129},{385... | collective-permute-start | bytes 1081352 | tf_op jit(solution)/shard_map/ppermute | solution.py:318
  138.6 3.3 %collective-permute-start.7 = (bf16[32,5632]{1,0:T(8,128)(2,1)S(1)}, bf16[32,5632]{1,0:T(8,128)(2,1)S(1)}, u32[]{:S(2)}, u32[]{:S(2)}) collective-permute-start(bf16[32,5632]{1,0:T(8,128)(2,1)S(1)} %get-tuple-element.26), channel_id=1, source_target_pairs={{0,256},{128,384},{256,0},{384,128},{1,257},{129,385},{257,1},{385... | collective-permute-start | bytes 1081352 | tf_op jit(solution)/shard_map/ppermute | solution.py:318
  141.9 4.0 %collective-permute-start.6 = (bf16[32,5632]{1,0:T(8,128)(2,1)S(1)}, bf16[32,5632]{1,0:T(8,128)(2,1)S(1)}, u32[]{:S(2)}, u32[]{:S(2)}) collective-permute-start(bf16[32,5632]{1,0:T(8,128)(2,1)S(1)} %get-tuple-element.26), channel_id=1, source_target_pairs={{0,128},{128,256},{256,384},{384,0},{1,129},{129,257},{257,385},{3... | collective-permute-start | bytes 1081352 | tf_op jit(solution)/shard_map/ppermute | solution.py:318
  145.9 11.2 %collective-permute-done.8 = bf16[32,5632]{1,0:T(8,128)(2,1)S(1)} collective-permute-done((bf16[32,5632]{1,0:T(8,128)(2,1)S(1)}, bf16[32,5632]{1,0:T(8,128)(2,1)S(1)}, u32[]{:S(2)}, u32[]{:S(2)}) %collective-permute-start.8) | collective-permute-done | bytes 360480 | tf_op jit(solution)/shard_map/ppermute | solution.py:318
  157.1 2.5 %collective-permute-done.6 = bf16[32,5632]{1,0:T(8,128)(2,1)S(1)} collective-permute-done((bf16[32,5632]{1,0:T(8,128)(2,1)S(1)}, bf16[32,5632]{1,0:T(8,128)(2,1)S(1)}, u32[]{:S(2)}, u32[]{:S(2)}) %collective-permute-start.6) | collective-permute-done | bytes 360480 | tf_op jit(solution)/shard_map/ppermute | solution.py:318
  160.5 0.8 slice_bitcast_fusion
  161.4 16.6 %all-to-all-done.1 = bf16[128,3,16,128]{3,2,1,0:T(8,128)(2,1)S(1)} async-done(((bf16[128,3,16,128]{3,2,1,0:T(8,128)(2,1)}), bf16[128,3,16,128]{3,2,1,0:T(8,128)(2,1)S(1)}, u32[]{:S(2)}, u32[]{:S(2)}) %all-to-all-start.1) | async-done | bytes 1572896 | tf_op jit(solution)/shard_map/all_to_all | solution.py:359
  178.0 2.1 %combine_rows.1 = bf16[32,2048]{1,0:T(8,128)(2,1)} custom-call(s32[8,32]{1,0:T(8,128)S(1)} %copy-done.2, bf16[384,16,128]{2,1,0:T(8,128)(2,1)S(1)} %bitcast.14), custom_call_target="tpu_custom_call" | custom-call | tf_op jit(solution)/shard_map/combine_rows/pallas_call | solution.py:149
  (21 shorter events, 0.9 us)
Async XLA Ops:
  6.4 91.4 %copy-start = (bf16[1,32,2048]{2,1,0:T(8,128)(2,1)S(1)}, bf16[1,32,2048]{2,1,0:T(8,128)(2,1)}, u32[]{:S(2)}) copy-start(bf16[1,32,2048]{2,1,0:T(8,128)(2,1)} %up_in.1) | copy-start | bytes 393220
  6.4 91.4 %copy-start.1 = (bf16[1,32,2048]{2,1,0:T(8,128)(2,1)S(1)}, bf16[1,32,2048]{2,1,0:T(8,128)(2,1)}, u32[]{:S(2)}) copy-start(bf16[1,32,2048]{2,1,0:T(8,128)(2,1)} %down_out.1) | copy-start | bytes 393220
  6.4 91.3 %all-to-all-start = ((bf16[128,6,16,128]{3,2,1,0:T(8,128)(2,1)}), bf16[128,6,16,128]{3,2,1,0:T(8,128)(2,1)S(1)}, u32[]{:S(2)}, u32[]{:S(2)}) async-start(bf16[128,6,16,128]{3,2,1,0:T(8,128)(2,1)} %bitcast.15), calls=%async_computation | async-start | bytes 6291456 | tf_op jit(solution)/shard_map/all_to_all | solution.py:350
  24.4 31.1 %collective-permute-start = (bf16[2304,256]{1,0:T(8,128)(2,1)}, bf16[2304,256]{1,0:T(8,128)(2,1)}, u32[]{:S(2)}, u32[]{:S(2)}) collective-permute-start(bf16[2304,256]{1,0:T(8,128)(2,1)} %get-tuple-element.23.refs_0_), channel_id=1, source_target_pairs={{0,128},{128,256},{256,384},{384,0},{1,129},{129,257},{257,385},{3... | collective-permute-start | bytes 3538952 | tf_op jit(solution)/shard_map/ppermute | solution.py:318
  26.8 32.3 %collective-permute-start.3 = (bf16[2304,256]{1,0:T(8,128)(2,1)}, bf16[2304,256]{1,0:T(8,128)(2,1)}, u32[]{:S(2)}, u32[]{:S(2)}) collective-permute-start(bf16[2304,256]{1,0:T(8,128)(2,1)} %get-tuple-element.24.refs_1_), channel_id=1, source_target_pairs={{0,384},{128,0},{256,128},{384,256},{1,385},{129,1},{257,129},{385... | collective-permute-start | bytes 3538952 | tf_op jit(solution)/shard_map/ppermute | solution.py:318
  30.2 70.0 %collective-permute-start.2 = (bf16[2304,256]{1,0:T(8,128)(2,1)}, bf16[2304,256]{1,0:T(8,128)(2,1)}, u32[]{:S(2)}, u32[]{:S(2)}) collective-permute-start(bf16[2304,256]{1,0:T(8,128)(2,1)} %get-tuple-element.23.refs_0_), channel_id=1, source_target_pairs={{0,384},{128,0},{256,128},{384,256},{1,385},{129,1},{257,129},{385... | collective-permute-start | bytes 3538952 | tf_op jit(solution)/shard_map/ppermute | solution.py:318
  33.0 67.2 %collective-permute-start.1 = (bf16[2304,256]{1,0:T(8,128)(2,1)}, bf16[2304,256]{1,0:T(8,128)(2,1)}, u32[]{:S(2)}, u32[]{:S(2)}) collective-permute-start(bf16[2304,256]{1,0:T(8,128)(2,1)} %get-tuple-element.24.refs_1_), channel_id=1, source_target_pairs={{0,128},{128,256},{256,384},{384,0},{1,129},{129,257},{257,385},{3... | collective-permute-start | bytes 3538952 | tf_op jit(solution)/shard_map/ppermute | solution.py:318
  55.5 49.2 %collective-permute-start.4 = (bf16[2304,256]{1,0:T(8,128)(2,1)}, bf16[2304,256]{1,0:T(8,128)(2,1)}, u32[]{:S(2)}, u32[]{:S(2)}) collective-permute-start(bf16[2304,256]{1,0:T(8,128)(2,1)} %collective-permute-done.refs_2_), channel_id=1, source_target_pairs={{0,128},{128,256},{256,384},{384,0},{1,129},{129,257},{257,385},{3... | collective-permute-start | bytes 3538952 | tf_op jit(solution)/shard_map/ppermute | solution.py:318
  59.1 48.9 %collective-permute-start.5 = (bf16[2304,256]{1,0:T(8,128)(2,1)}, bf16[2304,256]{1,0:T(8,128)(2,1)}, u32[]{:S(2)}, u32[]{:S(2)}) collective-permute-start(bf16[2304,256]{1,0:T(8,128)(2,1)} %collective-permute-done.3.refs_5_), channel_id=1, source_target_pairs={{0,384},{128,0},{256,128},{384,256},{1,385},{129,1},{257,129},{385... | collective-permute-start | bytes 3538952 | tf_op jit(solution)/shard_map/ppermute | solution.py:318
  61.5 46.4 %copy-start.6 = (bf16[1,32,768]{2,1,0:T(8,128)(2,1)S(1)}, bf16[1,32,768]{2,1,0:T(8,128)(2,1)}, u32[]{:S(2)}) copy-start(bf16[1,32,768]{2,1,0:T(8,128)(2,1)} %up_out.1) | copy-start | bytes 147460
  61.5 46.4 %copy-start.7 = (bf16[1,32,768]{2,1,0:T(8,128)(2,1)S(1)}, bf16[1,32,768]{2,1,0:T(8,128)(2,1)}, u32[]{:S(2)}) copy-start(bf16[1,32,768]{2,1,0:T(8,128)(2,1)} %down_in.1) | copy-start | bytes 147460
  97.8 10.2 %copy-start.4 = (bf16[2304,256]{1,0:T(8,128)(2,1)S(1)}, bf16[2304,256]{1,0:T(8,128)(2,1)}, u32[]{:S(2)}) copy-start(bf16[2304,256]{1,0:T(8,128)(2,1)} %get-tuple-element.23.refs_0_) | copy-start | bytes 3538948
  97.8 10.2 %copy-start.5 = (bf16[2304,256]{1,0:T(8,128)(2,1)S(1)}, bf16[2304,256]{1,0:T(8,128)(2,1)}, u32[]{:S(2)}) copy-start(bf16[2304,256]{1,0:T(8,128)(2,1)} %get-tuple-element.24.refs_1_) | copy-start | bytes 3538948
  99.0 1.2 copy-start.3
  122.1 55.9 %all-to-all-start.1 = ((bf16[128,3,16,128]{3,2,1,0:T(8,128)(2,1)}), bf16[128,3,16,128]{3,2,1,0:T(8,128)(2,1)S(1)}, u32[]{:S(2)}, u32[]{:S(2)}) async-start(bf16[128,3,16,128]{3,2,1,0:T(8,128)(2,1)} %bitcast.4), calls=%async_computation.1 | async-start | bytes 3145728 | tf_op jit(solution)/shard_map/all_to_all | solution.py:359
  136.4 20.8 %collective-permute-start.8 = (bf16[32,5632]{1,0:T(8,128)(2,1)S(1)}, bf16[32,5632]{1,0:T(8,128)(2,1)S(1)}, u32[]{:S(2)}, u32[]{:S(2)}) collective-permute-start(bf16[32,5632]{1,0:T(8,128)(2,1)S(1)} %get-tuple-element.26), channel_id=1, source_target_pairs={{0,384},{128,0},{256,128},{384,256},{1,385},{129,1},{257,129},{385... | collective-permute-start | bytes 1081352 | tf_op jit(solution)/shard_map/ppermute | solution.py:318
  138.6 18.5 %collective-permute-start.7 = (bf16[32,5632]{1,0:T(8,128)(2,1)S(1)}, bf16[32,5632]{1,0:T(8,128)(2,1)S(1)}, u32[]{:S(2)}, u32[]{:S(2)}) collective-permute-start(bf16[32,5632]{1,0:T(8,128)(2,1)S(1)} %get-tuple-element.26), channel_id=1, source_target_pairs={{0,256},{128,384},{256,0},{384,128},{1,257},{129,385},{257,1},{385... | collective-permute-start | bytes 1081352 | tf_op jit(solution)/shard_map/ppermute | solution.py:318
  141.9 17.7 %collective-permute-start.6 = (bf16[32,5632]{1,0:T(8,128)(2,1)S(1)}, bf16[32,5632]{1,0:T(8,128)(2,1)S(1)}, u32[]{:S(2)}, u32[]{:S(2)}) collective-permute-start(bf16[32,5632]{1,0:T(8,128)(2,1)S(1)} %get-tuple-element.26), channel_id=1, source_target_pairs={{0,128},{128,256},{256,384},{384,0},{1,129},{129,257},{257,385},{3... | collective-permute-start | bytes 1081352 | tf_op jit(solution)/shard_map/ppermute | solution.py:318
  159.8 18.1 %copy-start.2 = (s32[8,32]{1,0:T(8,128)S(1)}, s32[8,32]{1,0:T(8,128)}, u32[]{:S(2)}) copy-start(s32[8,32]{1,0:T(8,128)} %get-tuple-element.16.slots) | copy-start | bytes 3076

commit v9 on v8

--- a/solution.py
+++ b/solution.py
@@ -8,6 +8,7 @@
 CAP = 3
 LANES = 128
 COLS = 256
+ROW_STEPS = 4
 SCALE = 2.0
 F32 = jnp.float32
 BF16 = jnp.bfloat16
@@ -197,7 +198,7 @@
 
 def slot_kernel(rank, rows_in, rows_grad, low_up, back_low, up_in, up_out, down_in, *refs):
     owners = (refs[0:2], refs[2:4], refs[4:6], refs[6:8])
-    slot_grad, adapters, hidden, grad_up, up_low, gate_up, down, grads, slot_rows, sems = refs[8:]
+    slot_far, adapters, hidden, grad_up, up_low, gate_up, down, grads, slot_rows, slot_grad, sems, out_sems = refs[8:]
     width = gate_up.shape[0]
     inner = hidden.shape[1]
     shards = len(owners)
@@ -266,7 +267,13 @@
         slot_rows[:, cols] = (
             dot(grads[...], gate_up[cols, :], 1, 1) + SCALE * dot(up_low[...], up_in[:, cols], 1, 0)
         ).astype(BF16)
-    slot_grad[...] = slot_rows[...].reshape(slot_grad.shape)
+    step = slot_grad.shape[0] // ROW_STEPS
+    stores = []
+    for i in range(ROW_STEPS):
+        rows = pl.ds(i * step, step)
+        slot_grad[rows] = slot_rows[rows, :].reshape((step,) + slot_grad.shape[1:])
+        stores.append(pltpu.make_async_copy(slot_grad.at[rows], slot_far.at[rows], out_sems.at[i]))
+        stores[i].start()
     low_down = dot(hidden[...], down_in[0], 1, 1).astype(BF16)
     at = 0
     for left, right in (
@@ -279,6 +286,8 @@
             piece = dot(left, right[:, pl.ds(c * COLS, COLS)], 0, 0)
             adapters[:, pl.ds(at, COLS)] = (SCALE * piece).astype(BF16)
             at += COLS
+    for store in stores:
+        store.wait()
 
 
 def expert_slots(rows_in, rows_grad, weights, low_up, back_low, up_in, up_out, down_in):
@@ -292,7 +301,7 @@
             jax.ShapeDtypeStruct((rank, 2 * (width + inner)), BF16),
         ),
         in_specs=[SMEM] + [VMEM] * 7 + [HBM] * 8,
-        out_specs=(VMEM,) * 2,
+        out_specs=(HBM, VMEM),
         scratch_shapes=[
             pltpu.VMEM((rows, inner), BF16),
             pltpu.VMEM((rows, inner), BF16),
@@ -301,7 +310,9 @@
             pltpu.VMEM((inner, width), BF16),
             pltpu.VMEM((rows, 2 * inner), BF16),
             pltpu.VMEM((rows, width), BF16),
+            pltpu.VMEM((rows, width // LANES, LANES), BF16),
             pltpu.SemaphoreType.DMA((72,)),
+            pltpu.SemaphoreType.DMA((ROW_STEPS,)),
         ],
         compiler_params=params(40),
         cost_estimate=pl.CostEstimate(

time: 181 us -> 180 us (level)
  no operation moved by 1% of the time
where the time goes in v9:
time: 180 us
  waiting for transfers between devices  92.5 us (51%)
  starting transfers between devices  60.7 us (34%)
  Pallas kernels  22.7 us (13%)
  local copies, waits for them, and re-layouts  2.72 us (2%)
    ppermute x9, waiting for transfers between devices, shifted(): lax.ppermute(value, axis, [(i, (i + shift) % count) for i in range(count)])  39.7 us
    all_to_all x1, waiting for transfers between devices, on_device(): lax.all_to_all(send.reshape(experts, 2 * CAP, width // LANES, LANES), ('g...  36.2 us
    ppermute x9, starting transfers between devices, shifted(): lax.ppermute(value, axis, [(i, (i + shift) % count) for i in range(count)])  28.5 us
    all_to_all x1, starting transfers between devices, on_device(): lax.all_to_all(send.reshape(experts, 2 * CAP, width // LANES, LANES), ('g...  18 us
    all_to_all x1, waiting for transfers between devices, on_device(): lax.all_to_all(slot_grad.reshape(experts, CAP, width // LANES, LANES), ('...  16.6 us
    all_to_all x1, starting transfers between devices, on_device(): lax.all_to_all(slot_grad.reshape(experts, CAP, width // LANES, LANES), ('...  14.3 us
    pallas_call x1, Pallas kernels, expert_slots(): pl.pallas_call(slot_kernel, out_shape=(jax.ShapeDtypeStruct((rows, width...  13.6 us
    pallas_call x1, Pallas kernels, place_rows(): pl.pallas_call(place_kernel, out_shape=(jax.ShapeDtypeStruct((total, subs...  5.76 us
  transfers between devices with their start and end apart: 11, of which 7 were waited for; matrix products, arithmetic and copies ran while one was open for 1% of the time, Pallas kernels for 1%

profile of v9, /device:TPU:6, one launch (start us, length us, event | category | flops | bytes accessed | tf_op | source)
XLA Modules:
  0.0 179.6 jit_solution(13277113726446554058)
XLA Ops:
  0.6 5.8 %place_rows.1 = (bf16[768,16,128]{2,1,0:T(8,128)(2,1)}, s32[8,32]{1,0:T(8,128)}, bf16[2304,256]{1,0:T(8,128)(2,1)}, bf16[2304,256]{1,0:T(8,128)(2,1)}) custom-call(s32[8,32]{1,0:T(8,128)} %bitcast.16, f32[8,32]{1,0:T(8,128)} %bitcast.17, s32[128]{0:T(128)} %limits.1, bf16[32,2048]{1,0:T(8,128)(2,1)} %tokens.1, bf16[32,2048]{1,0:T(8,128)(2,1)} %grads.1, ...), custom_call_target="tpu_custom_call" | custom-call | tf_op jit(solution)/shard_map/place_rows/pallas_call | solution.py:110
  6.4 18.0 %all-to-all-start = ((bf16[128,6,16,128]{3,2,1,0:T(8,128)(2,1)}), bf16[128,6,16,128]{3,2,1,0:T(8,128)(2,1)S(1)}, u32[]{:S(2)}, u32[]{:S(2)}) async-start(bf16[128,6,16,128]{3,2,1,0:T(8,128)(2,1)} %bitcast.15), calls=%async_computation | async-start | bytes 6291456 | tf_op jit(solution)/shard_map/all_to_all | solution.py:361
  24.4 2.4 %collective-permute-start = (bf16[2304,256]{1,0:T(8,128)(2,1)}, bf16[2304,256]{1,0:T(8,128)(2,1)}, u32[]{:S(2)}, u32[]{:S(2)}) collective-permute-start(bf16[2304,256]{1,0:T(8,128)(2,1)} %get-tuple-element.23.refs_0_), channel_id=1, source_target_pairs={{0,128},{128,256},{256,384},{384,0},{1,129},{129,257},{257,385},{3... | collective-permute-start | bytes 3538952 | tf_op jit(solution)/shard_map/ppermute | solution.py:329
  26.8 3.5 %collective-permute-start.3 = (bf16[2304,256]{1,0:T(8,128)(2,1)}, bf16[2304,256]{1,0:T(8,128)(2,1)}, u32[]{:S(2)}, u32[]{:S(2)}) collective-permute-start(bf16[2304,256]{1,0:T(8,128)(2,1)} %get-tuple-element.24.refs_1_), channel_id=1, source_target_pairs={{0,384},{128,0},{256,128},{384,256},{1,385},{129,1},{257,129},{385... | collective-permute-start | bytes 3538952 | tf_op jit(solution)/shard_map/ppermute | solution.py:329
  30.2 2.7 %collective-permute-start.2 = (bf16[2304,256]{1,0:T(8,128)(2,1)}, bf16[2304,256]{1,0:T(8,128)(2,1)}, u32[]{:S(2)}, u32[]{:S(2)}) collective-permute-start(bf16[2304,256]{1,0:T(8,128)(2,1)} %get-tuple-element.23.refs_0_), channel_id=1, source_target_pairs={{0,384},{128,0},{256,128},{384,256},{1,385},{129,1},{257,129},{385... | collective-permute-start | bytes 3538952 | tf_op jit(solution)/shard_map/ppermute | solution.py:329
  33.0 4.3 %collective-permute-start.1 = (bf16[2304,256]{1,0:T(8,128)(2,1)}, bf16[2304,256]{1,0:T(8,128)(2,1)}, u32[]{:S(2)}, u32[]{:S(2)}) collective-permute-start(bf16[2304,256]{1,0:T(8,128)(2,1)} %get-tuple-element.24.refs_1_), channel_id=1, source_target_pairs={{0,128},{128,256},{256,384},{384,0},{1,129},{129,257},{257,385},{3... | collective-permute-start | bytes 3538952 | tf_op jit(solution)/shard_map/ppermute | solution.py:329
  37.3 18.2 %collective-permute-done.refs_2_ = bf16[2304,256]{1,0:T(8,128)(2,1)} collective-permute-done((bf16[2304,256]{1,0:T(8,128)(2,1)}, bf16[2304,256]{1,0:T(8,128)(2,1)}, u32[]{:S(2)}, u32[]{:S(2)}) %collective-permute-start) | collective-permute-done | bytes 1179680 | tf_op jit(solution)/shard_map/ppermute | solution.py:329
  55.5 3.6 %collective-permute-start.4 = (bf16[2304,256]{1,0:T(8,128)(2,1)}, bf16[2304,256]{1,0:T(8,128)(2,1)}, u32[]{:S(2)}, u32[]{:S(2)}) collective-permute-start(bf16[2304,256]{1,0:T(8,128)(2,1)} %collective-permute-done.refs_2_), channel_id=1, source_target_pairs={{0,128},{128,256},{256,384},{384,0},{1,129},{129,257},{257,385},{3... | collective-permute-start | bytes 3538952 | tf_op jit(solution)/shard_map/ppermute | solution.py:329
  59.1 2.4 %collective-permute-start.5 = (bf16[2304,256]{1,0:T(8,128)(2,1)}, bf16[2304,256]{1,0:T(8,128)(2,1)}, u32[]{:S(2)}, u32[]{:S(2)}) collective-permute-start(bf16[2304,256]{1,0:T(8,128)(2,1)} %collective-permute-done.3.refs_5_), channel_id=1, source_target_pairs={{0,384},{128,0},{256,128},{384,256},{1,385},{129,1},{257,129},{385... | collective-permute-start | bytes 3538952 | tf_op jit(solution)/shard_map/ppermute | solution.py:329
  61.6 36.2 %all-to-all-done.recv = bf16[128,6,16,128]{3,2,1,0:T(8,128)(2,1)S(1)} async-done(((bf16[128,6,16,128]{3,2,1,0:T(8,128)(2,1)}), bf16[128,6,16,128]{3,2,1,0:T(8,128)(2,1)S(1)}, u32[]{:S(2)}, u32[]{:S(2)}) %all-to-all-start) | async-done | bytes 3145760 | tf_op jit(solution)/shard_map/all_to_all | solution.py:361
  97.8 1.2 low_products.1
  99.0 1.2 copy-done.3
  100.2 4.4 %collective-permute-done.4.refs_6_ = bf16[2304,256]{1,0:T(8,128)(2,1)} collective-permute-done((bf16[2304,256]{1,0:T(8,128)(2,1)}, bf16[2304,256]{1,0:T(8,128)(2,1)}, u32[]{:S(2)}, u32[]{:S(2)}) %collective-permute-start.4) | collective-permute-done | bytes 1179680 | tf_op jit(solution)/shard_map/ppermute | solution.py:329
  104.6 3.3 %collective-permute-done.5.refs_7_ = bf16[2304,256]{1,0:T(8,128)(2,1)} collective-permute-done((bf16[2304,256]{1,0:T(8,128)(2,1)}, bf16[2304,256]{1,0:T(8,128)(2,1)}, u32[]{:S(2)}, u32[]{:S(2)}) %collective-permute-start.5) | collective-permute-done | bytes 1179680 | tf_op jit(solution)/shard_map/ppermute | solution.py:329
  108.0 13.6 %expert_slots.1 = (bf16[384,16,128]{2,1,0:T(8,128)(2,1)}, bf16[32,5632]{1,0:T(8,128)(2,1)S(1)}) custom-call(s32[1]{0:T(128)} %bitcast.2.rank, bf16[384,2048]{1,0:T(8,128)(2,1)S(1)} %get-tuple-element.18.rows_in, bf16[384,2048]{1,0:T(8,128)(2,1)} %copy-done.3, bf16[384,32]{1,0:T(8,128)(2,1)S(1)} %get-tuple-element.20.low_up, ...), custom_call_target="tpu_custom_call" | custom-call | flops 6039797760 | bytes 14155776 | tf_op jit(solution)/shard_map/expert_slots/pallas_call | solution.py:297
  121.5 14.3 %all-to-all-start.1 = ((bf16[128,3,16,128]{3,2,1,0:T(8,128)(2,1)}), bf16[128,3,16,128]{3,2,1,0:T(8,128)(2,1)S(1)}, u32[]{:S(2)}, u32[]{:S(2)}) async-start(bf16[128,3,16,128]{3,2,1,0:T(8,128)(2,1)} %bitcast.4), calls=%async_computation.1 | async-start | bytes 3145728 | tf_op jit(solution)/shard_map/all_to_all | solution.py:370
  135.8 2.2 %collective-permute-start.8 = (bf16[32,5632]{1,0:T(8,128)(2,1)S(1)}, bf16[32,5632]{1,0:T(8,128)(2,1)S(1)}, u32[]{:S(2)}, u32[]{:S(2)}) collective-permute-start(bf16[32,5632]{1,0:T(8,128)(2,1)S(1)} %get-tuple-element.26), channel_id=1, source_target_pairs={{0,384},{128,0},{256,128},{384,256},{1,385},{129,1},{257,129},{385... | collective-permute-start | bytes 1081352 | tf_op jit(solution)/shard_map/ppermute | solution.py:329
  138.1 3.3 %collective-permute-start.7 = (bf16[32,5632]{1,0:T(8,128)(2,1)S(1)}, bf16[32,5632]{1,0:T(8,128)(2,1)S(1)}, u32[]{:S(2)}, u32[]{:S(2)}) collective-permute-start(bf16[32,5632]{1,0:T(8,128)(2,1)S(1)} %get-tuple-element.26), channel_id=1, source_target_pairs={{0,256},{128,384},{256,0},{384,128},{1,257},{129,385},{257,1},{385... | collective-permute-start | bytes 1081352 | tf_op jit(solution)/shard_map/ppermute | solution.py:329
  141.4 4.0 %collective-permute-start.6 = (bf16[32,5632]{1,0:T(8,128)(2,1)S(1)}, bf16[32,5632]{1,0:T(8,128)(2,1)S(1)}, u32[]{:S(2)}, u32[]{:S(2)}) collective-permute-start(bf16[32,5632]{1,0:T(8,128)(2,1)S(1)} %get-tuple-element.26), channel_id=1, source_target_pairs={{0,128},{128,256},{256,384},{384,0},{1,129},{129,257},{257,385},{3... | collective-permute-start | bytes 1081352 | tf_op jit(solution)/shard_map/ppermute | solution.py:329
  145.4 11.2 %collective-permute-done.8 = bf16[32,5632]{1,0:T(8,128)(2,1)S(1)} collective-permute-done((bf16[32,5632]{1,0:T(8,128)(2,1)S(1)}, bf16[32,5632]{1,0:T(8,128)(2,1)S(1)}, u32[]{:S(2)}, u32[]{:S(2)}) %collective-permute-start.8) | collective-permute-done | bytes 360480 | tf_op jit(solution)/shard_map/ppermute | solution.py:329
  156.6 2.5 %collective-permute-done.6 = bf16[32,5632]{1,0:T(8,128)(2,1)S(1)} collective-permute-done((bf16[32,5632]{1,0:T(8,128)(2,1)S(1)}, bf16[32,5632]{1,0:T(8,128)(2,1)S(1)}, u32[]{:S(2)}, u32[]{:S(2)}) %collective-permute-start.6) | collective-permute-done | bytes 360480 | tf_op jit(solution)/shard_map/ppermute | solution.py:329
  160.0 0.8 slice_bitcast_fusion
  160.8 16.6 %all-to-all-done.1 = bf16[128,3,16,128]{3,2,1,0:T(8,128)(2,1)S(1)} async-done(((bf16[128,3,16,128]{3,2,1,0:T(8,128)(2,1)}), bf16[128,3,16,128]{3,2,1,0:T(8,128)(2,1)S(1)}, u32[]{:S(2)}, u32[]{:S(2)}) %all-to-all-start.1) | async-done | bytes 1572896 | tf_op jit(solution)/shard_map/all_to_all | solution.py:370
  177.4 2.1 %combine_rows.1 = bf16[32,2048]{1,0:T(8,128)(2,1)} custom-call(s32[8,32]{1,0:T(8,128)S(1)} %copy-done.2, bf16[384,16,128]{2,1,0:T(8,128)(2,1)S(1)} %bitcast.14), custom_call_target="tpu_custom_call" | custom-call | tf_op jit(solution)/shard_map/combine_rows/pallas_call | solution.py:150
  (21 shorter events, 0.9 us)
Async XLA Ops:
  6.4 91.4 %copy-start = (bf16[1,32,2048]{2,1,0:T(8,128)(2,1)S(1)}, bf16[1,32,2048]{2,1,0:T(8,128)(2,1)}, u32[]{:S(2)}) copy-start(bf16[1,32,2048]{2,1,0:T(8,128)(2,1)} %up_in.1) | copy-start | bytes 393220
  6.4 91.4 %copy-start.1 = (bf16[1,32,2048]{2,1,0:T(8,128)(2,1)S(1)}, bf16[1,32,2048]{2,1,0:T(8,128)(2,1)}, u32[]{:S(2)}) copy-start(bf16[1,32,2048]{2,1,0:T(8,128)(2,1)} %down_out.1) | copy-start | bytes 393220
  6.4 91.3 %all-to-all-start = ((bf16[128,6,16,128]{3,2,1,0:T(8,128)(2,1)}), bf16[128,6,16,128]{3,2,1,0:T(8,128)(2,1)S(1)}, u32[]{:S(2)}, u32[]{:S(2)}) async-start(bf16[128,6,16,128]{3,2,1,0:T(8,128)(2,1)} %bitcast.15), calls=%async_computation | async-start | bytes 6291456 | tf_op jit(solution)/shard_map/all_to_all | solution.py:361
  24.4 31.1 %collective-permute-start = (bf16[2304,256]{1,0:T(8,128)(2,1)}, bf16[2304,256]{1,0:T(8,128)(2,1)}, u32[]{:S(2)}, u32[]{:S(2)}) collective-permute-start(bf16[2304,256]{1,0:T(8,128)(2,1)} %get-tuple-element.23.refs_0_), channel_id=1, source_target_pairs={{0,128},{128,256},{256,384},{384,0},{1,129},{129,257},{257,385},{3... | collective-permute-start | bytes 3538952 | tf_op jit(solution)/shard_map/ppermute | solution.py:329
  26.8 32.3 %collective-permute-start.3 = (bf16[2304,256]{1,0:T(8,128)(2,1)}, bf16[2304,256]{1,0:T(8,128)(2,1)}, u32[]{:S(2)}, u32[]{:S(2)}) collective-permute-start(bf16[2304,256]{1,0:T(8,128)(2,1)} %get-tuple-element.24.refs_1_), channel_id=1, source_target_pairs={{0,384},{128,0},{256,128},{384,256},{1,385},{129,1},{257,129},{385... | collective-permute-start | bytes 3538952 | tf_op jit(solution)/shard_map/ppermute | solution.py:329
  30.2 70.0 %collective-permute-start.2 = (bf16[2304,256]{1,0:T(8,128)(2,1)}, bf16[2304,256]{1,0:T(8,128)(2,1)}, u32[]{:S(2)}, u32[]{:S(2)}) collective-permute-start(bf16[2304,256]{1,0:T(8,128)(2,1)} %get-tuple-element.23.refs_0_), channel_id=1, source_target_pairs={{0,384},{128,0},{256,128},{384,256},{1,385},{129,1},{257,129},{385... | collective-permute-start | bytes 3538952 | tf_op jit(solution)/shard_map/ppermute | solution.py:329
  33.0 67.2 %collective-permute-start.1 = (bf16[2304,256]{1,0:T(8,128)(2,1)}, bf16[2304,256]{1,0:T(8,128)(2,1)}, u32[]{:S(2)}, u32[]{:S(2)}) collective-permute-start(bf16[2304,256]{1,0:T(8,128)(2,1)} %get-tuple-element.24.refs_1_), channel_id=1, source_target_pairs={{0,128},{128,256},{256,384},{384,0},{1,129},{129,257},{257,385},{3... | collective-permute-start | bytes 3538952 | tf_op jit(solution)/shard_map/ppermute | solution.py:329
  55.5 49.2 %collective-permute-start.4 = (bf16[2304,256]{1,0:T(8,128)(2,1)}, bf16[2304,256]{1,0:T(8,128)(2,1)}, u32[]{:S(2)}, u32[]{:S(2)}) collective-permute-start(bf16[2304,256]{1,0:T(8,128)(2,1)} %collective-permute-done.refs_2_), channel_id=1, source_target_pairs={{0,128},{128,256},{256,384},{384,0},{1,129},{129,257},{257,385},{3... | collective-permute-start | bytes 3538952 | tf_op jit(solution)/shard_map/ppermute | solution.py:329
  59.1 48.9 %collective-permute-start.5 = (bf16[2304,256]{1,0:T(8,128)(2,1)}, bf16[2304,256]{1,0:T(8,128)(2,1)}, u32[]{:S(2)}, u32[]{:S(2)}) collective-permute-start(bf16[2304,256]{1,0:T(8,128)(2,1)} %collective-permute-done.3.refs_5_), channel_id=1, source_target_pairs={{0,384},{128,0},{256,128},{384,256},{1,385},{129,1},{257,129},{385... | collective-permute-start | bytes 3538952 | tf_op jit(solution)/shard_map/ppermute | solution.py:329
  61.5 46.4 %copy-start.6 = (bf16[1,32,768]{2,1,0:T(8,128)(2,1)S(1)}, bf16[1,32,768]{2,1,0:T(8,128)(2,1)}, u32[]{:S(2)}) copy-start(bf16[1,32,768]{2,1,0:T(8,128)(2,1)} %up_out.1) | copy-start | bytes 147460
  61.5 46.4 %copy-start.7 = (bf16[1,32,768]{2,1,0:T(8,128)(2,1)S(1)}, bf16[1,32,768]{2,1,0:T(8,128)(2,1)}, u32[]{:S(2)}) copy-start(bf16[1,32,768]{2,1,0:T(8,128)(2,1)} %down_in.1) | copy-start | bytes 147460
  97.8 10.2 %copy-start.4 = (bf16[2304,256]{1,0:T(8,128)(2,1)S(1)}, bf16[2304,256]{1,0:T(8,128)(2,1)}, u32[]{:S(2)}) copy-start(bf16[2304,256]{1,0:T(8,128)(2,1)} %get-tuple-element.23.refs_0_) | copy-start | bytes 3538948
  97.8 10.2 %copy-start.5 = (bf16[2304,256]{1,0:T(8,128)(2,1)S(1)}, bf16[2304,256]{1,0:T(8,128)(2,1)}, u32[]{:S(2)}) copy-start(bf16[2304,256]{1,0:T(8,128)(2,1)} %get-tuple-element.24.refs_1_) | copy-start | bytes 3538948
  99.0 1.2 copy-start.3
  121.5 55.9 %all-to-all-start.1 = ((bf16[128,3,16,128]{3,2,1,0:T(8,128)(2,1)}), bf16[128,3,16,128]{3,2,1,0:T(8,128)(2,1)S(1)}, u32[]{:S(2)}, u32[]{:S(2)}) async-start(bf16[128,3,16,128]{3,2,1,0:T(8,128)(2,1)} %bitcast.4), calls=%async_computation.1 | async-start | bytes 3145728 | tf_op jit(solution)/shard_map/all_to_all | solution.py:370
  135.8 20.8 %collective-permute-start.8 = (bf16[32,5632]{1,0:T(8,128)(2,1)S(1)}, bf16[32,5632]{1,0:T(8,128)(2,1)S(1)}, u32[]{:S(2)}, u32[]{:S(2)}) collective-permute-start(bf16[32,5632]{1,0:T(8,128)(2,1)S(1)} %get-tuple-element.26), channel_id=1, source_target_pairs={{0,384},{128,0},{256,128},{384,256},{1,385},{129,1},{257,129},{385... | collective-permute-start | bytes 1081352 | tf_op jit(solution)/shard_map/ppermute | solution.py:329
  138.1 18.5 %collective-permute-start.7 = (bf16[32,5632]{1,0:T(8,128)(2,1)S(1)}, bf16[32,5632]{1,0:T(8,128)(2,1)S(1)}, u32[]{:S(2)}, u32[]{:S(2)}) collective-permute-start(bf16[32,5632]{1,0:T(8,128)(2,1)S(1)} %get-tuple-element.26), channel_id=1, source_target_pairs={{0,256},{128,384},{256,0},{384,128},{1,257},{129,385},{257,1},{385... | collective-permute-start | bytes 1081352 | tf_op jit(solution)/shard_map/ppermute | solution.py:329
  141.4 17.7 %collective-permute-start.6 = (bf16[32,5632]{1,0:T(8,128)(2,1)S(1)}, bf16[32,5632]{1,0:T(8,128)(2,1)S(1)}, u32[]{:S(2)}, u32[]{:S(2)}) collective-permute-start(bf16[32,5632]{1,0:T(8,128)(2,1)S(1)} %get-tuple-element.26), channel_id=1, source_target_pairs={{0,128},{128,256},{256,384},{384,0},{1,129},{129,257},{257,385},{3... | collective-permute-start | bytes 1081352 | tf_op jit(solution)/shard_map/ppermute | solution.py:329
  159.3 18.1 %copy-start.2 = (s32[8,32]{1,0:T(8,128)S(1)}, s32[8,32]{1,0:T(8,128)}, u32[]{:S(2)}) copy-start(s32[8,32]{1,0:T(8,128)} %get-tuple-element.16.slots) | copy-start | bytes 3076
